TPU v7x, 256 devices: a whole 4x4x8 slice. The times are simulated.
256 devices in a mesh: leaf: 16 (over x, y_hi, core), wide: 16 (over z, y_lo).
Axes of the slice: x: 4, y: 4 (y_hi: 2, y_lo: 2; y = y_hi * 2 + y_lo), z: 8, core: 2. Of those that a mesh axis runs over, the one named last changes fastest.
Arguments:
- source: bfloat16 [4, 16, 16, 256, 1024], P(None, 'leaf', 'wide'), may hold values from -6 to 6
- row_factors: bfloat16 [4, 4, 16, 16, 256, 512], P(None, None, 'leaf', 'wide'), may hold values from -0.25 to 0.25
- column_factors: bfloat16 [4, 4, 16, 16, 256, 512], P(None, None, 'leaf', 'wide'), may hold values from -0.25 to 0.25
Outputs:
- result: bfloat16 [4, 16, 16, 256, 1024], P(None, 'leaf', 'wide')
All inputs are finite; a program needn't handle non-finite values.
Results may differ from a plain program's by a relative error of at most 0.015.
Values may be sent and summed in bfloat16 or wider, within the bound.
No kernel may reach another device: no remote copies, remote signals or barrier semaphores. Data moves between devices by JAX's collectives and lax.ppermute only.
A program may use at most 64 MiB of HBM per device.

v0:
```python
import jax
import jax.numpy as jnp
from jax import lax
from jax.sharding import PartitionSpec as P


def from_partner(value, axis, apart):
    mask = 2**apart
    pairs = [(source, source ^ mask) for source in range(lax.axis_size(axis))]
    return lax.ppermute(value, axis, pairs)


def combine(own_block, partner, is_lower, factors):
    rank_size = own_block.shape[1]
    leading = jnp.where(is_lower, own_block, partner)
    trailing = jnp.where(is_lower, partner, own_block)
    result = jnp.einsum(
        "brk,bkh->brh", factors[:, :, :rank_size], leading, preferred_element_type=jnp.float32
    )
    result = result + jnp.einsum(
        "brk,bkh->brh", factors[:, :, rank_size:], trailing, preferred_element_type=jnp.float32
    )
    return result.astype(jnp.bfloat16)


def row_cross(coeffs, factors, level_no):
    partner = from_partner(coeffs, "leaf", level_no)
    is_lower = lax.axis_index("leaf") >> level_no & 1 == 0
    return combine(coeffs, partner, is_lower, factors)


def column_cross(coeffs, factors, level_no):
    partner = from_partner(coeffs, "wide", level_no)
    is_lower = lax.axis_index("wide") >> level_no & 1 == 0
    return combine(coeffs, partner, is_lower, factors)


def run_pass(coeffs, factors, level_order, crosser):
    for level_no in level_order:
        half_count = coeffs.shape[0] // 2
        first_part = crosser(coeffs[:half_count], factors[level_no, :half_count], level_no)
        second_part = crosser(coeffs[half_count:], factors[level_no, half_count:], level_no)
        coeffs = jnp.concatenate([first_part, second_part], axis=0)
    return coeffs


def per_device(source, row_factors, column_factors):
    blocks = source.shape[0]
    rank_size = source.shape[3]
    rhs_count = source.shape[4]
    levels = row_factors.shape[0]
    coeffs = source.reshape(blocks, rank_size, rhs_count)
    forward = row_factors.reshape(levels, blocks, rank_size, 2 * rank_size)
    adjoint = column_factors.reshape(levels, blocks, rank_size, 2 * rank_size)
    coeffs = run_pass(coeffs, forward, list(range(levels)), row_cross)
    coeffs = run_pass(coeffs, adjoint, list(reversed(range(levels))), column_cross)
    return coeffs.reshape(source.shape)


def solution(mesh):
    return jax.shard_map(
        per_device,
        mesh=mesh,
        in_specs=(
            P(None, "leaf", "wide", None, None),
            P(None, None, "leaf", "wide", None, None),
            P(None, None, "leaf", "wide", None, None),
        ),
        out_specs=P(None, "leaf", "wide", None, None),
        check_vma=False,
    )
```

profile of v0, /device:TPU:1, one launch (start us, length us, event | category | flops | bytes accessed | tf_op | source)
XLA Modules:
  0.0 381.0 jit_solution(18031316450026539949)
XLA Ops:
  0.0 2.4 slice_bitcast_fusion.1
  2.4 3.2 collective-permute-start.8
  5.7 1.1 slice_bitcast_fusion
  6.7 3.8 %slice_bitcast_fusion.14 = (bf16[2,256,512]{2,1,0:T(8,128)(2,1)}, bf16[2,256,512]{2,1,0:T(8,128)(2,1)}, bf16[2,256,512]{2,1,0:T(8,128)(2,1)}, bf16[2,256,512]{2,...) fusion(bf16[4,4,256,512]{3,2,1,0:T(8,128)(2,1)} %bitcast.88), kind=kLoop, calls=%fused_computation.127 | loop fusion | bytes 8388608 | tf_op jit(solution)/shard_map/squeeze | solution.py:41
  10.6 1.0 copy-done.2
  11.5 0.6 fusion.37
  12.1 1.8 fusion.8
  14.0 1.3 collective-permute-start.9
  15.2 0.6 fusion.61
  15.8 2.8 fusion
  18.6 1.8 collective-permute-start.1
  20.4 20.4 %collective-permute-done.9 = bf16[2,256,1024]{1,2,0:T(8,128)(2,1)} collective-permute-done((bf16[2,256,1024]{1,2,0:T(8,128)(2,1)S(1)}, bf16[2,256,1024]{1,2,0:T(8,128)(2,1)}, u32[]{:S(2)}, u32[]{:S(2)}) %collective-permute-start.9) | collective-permute-done | bytes 1048608 | tf_op jit(solution)/shard_map/ppermute | solution.py:10
  40.8 1.8 fusion.34
  42.6 0.5 fusion.9
  43.3 19.5 %collective-permute-done.1 = bf16[2,256,1024]{1,2,0:T(8,128)(2,1)} collective-permute-done((bf16[2,256,1024]{1,2,0:T(8,128)(2,1)}, bf16[2,256,1024]{1,2,0:T(8,128)(2,1)}, u32[]{:S(2)}, u32[]{:S(2)}) %collective-permute-start.1) | collective-permute-done | bytes 1048608 | tf_op jit(solution)/shard_map/ppermute | solution.py:10
  62.8 1.7 fusion.58
  64.5 1.7 fusion.1
  66.3 1.8 collective-permute-done.10
  68.1 1.0 copy-done.4
  69.1 1.5 fusion.31
  70.6 0.5 fusion.10
  71.1 1.2 collective-permute-start.11
  72.3 18.5 %collective-permute-done.2 = bf16[2,256,1024]{1,2,0:T(8,128)(2,1)} collective-permute-done((bf16[2,256,1024]{1,2,0:T(8,128)(2,1)S(1)}, bf16[2,256,1024]{1,2,0:T(8,128)(2,1)}, u32[]{:S(2)}, u32[]{:S(2)}) %collective-permute-start.2) | collective-permute-done | bytes 1048608 | tf_op jit(solution)/shard_map/ppermute | solution.py:10
  90.8 1.7 fusion.55
  92.5 1.7 fusion.2
  94.2 1.1 collective-permute-start.3
  95.3 18.3 %collective-permute-done.11 = bf16[2,256,1024]{1,2,0:T(8,128)(2,1)S(1)} collective-permute-done((bf16[2,256,1024]{1,2,0:T(8,128)(2,1)S(1)}, bf16[2,256,1024]{1,2,0:T(8,128)(2,1)S(1)}, u32[]{:S(2)}, u32[]{:S(2)}) %collective-permute-start.11) | collective-permute-done | bytes 1048608 | tf_op jit(solution)/shard_map/ppermute | solution.py:10
  113.6 1.0 copy-done.3
  114.6 1.5 fusion.28
  116.1 0.5 fusion.11
  116.6 7.2 %collective-permute-start.12 = (bf16[2,256,1024]{1,2,0:T(8,128)(2,1)S(1)}, bf16[2,256,1024]{1,2,0:T(8,128)(2,1)}, u32[]{:S(2)}, u32[]{:S(2)}) collective-permute-start(bf16[2,256,1024]{1,2,0:T(8,128)(2,1)S(1)} %fusion.11), channel_id=1, source_target_pairs={{0,8},{1,9},{2,10},{3,11},{4,12},{5,13},{6,14},{7,15},{8,0},{9,1},... | collective-permute-start | bytes 3145736 | tf_op jit(solution)/shard_map/ppermute | solution.py:10
  123.8 12.4 %collective-permute-done.3 = bf16[2,256,1024]{1,2,0:T(8,128)(2,1)} collective-permute-done((bf16[2,256,1024]{1,2,0:T(8,128)(2,1)S(1)}, bf16[2,256,1024]{1,2,0:T(8,128)(2,1)}, u32[]{:S(2)}, u32[]{:S(2)}) %collective-permute-start.3) | collective-permute-done | bytes 1048608 | tf_op jit(solution)/shard_map/ppermute | solution.py:10
  136.2 1.7 fusion.52
  137.9 0.5 fusion.3
  138.4 7.0 %collective-permute-start.4 = (bf16[2,256,1024]{1,2,0:T(8,128)(2,1)S(1)}, bf16[2,256,1024]{1,2,0:T(8,128)(2,1)}, u32[]{:S(2)}, u32[]{:S(2)}) collective-permute-start(bf16[2,256,1024]{1,2,0:T(8,128)(2,1)S(1)} %fusion.3), channel_id=1, source_target_pairs={{0,8},{1,9},{2,10},{3,11},{4,12},{5,13},{6,14},{7,15},{8,0},{9,1},... | collective-permute-start | bytes 3145736 | tf_op jit(solution)/shard_map/ppermute | solution.py:10
  145.4 3.8 %slice_bitcast_fusion.10 = (bf16[2,256,512]{2,1,0:T(8,128)(2,1)}, bf16[2,256,512]{2,1,0:T(8,128)(2,1)}, bf16[2,256,512]{2,1,0:T(8,128)(2,1)}, bf16[2,256,512]{2,...) fusion(bf16[4,4,256,512]{3,2,1,0:T(8,128)(2,1)} %bitcast.89), kind=kLoop, calls=%fused_computation.123 | loop fusion | bytes 8388608 | tf_op jit(solution)/shard_map/squeeze | solution.py:41
  149.2 0.7 collective-permute-done.12
  149.9 1.7 fusion.25
  151.6 0.5 fusion.12
  152.2 50.2 %collective-permute-start.13 = (bf16[2,256,1024]{1,2,0:T(8,128)(2,1)S(1)}, bf16[2,256,1024]{1,2,0:T(8,128)(2,1)}, u32[]{:S(2)}, u32[]{:S(2)}) collective-permute-start(bf16[2,256,1024]{1,2,0:T(8,128)(2,1)S(1)} %fusion.12), channel_id=1, source_target_pairs={{0,4},{1,5},{2,6},{3,7},{4,0},{5,1},{6,2},{7,3},{8,12},{9,13},{10,... | collective-permute-start | bytes 3145736 | tf_op jit(solution)/shard_map/ppermute | solution.py:10
  202.3 1.7 fusion.49
  204.0 0.5 fusion.4
  204.5 24.2 %collective-permute-start.5 = (bf16[2,256,1024]{1,2,0:T(8,128)(2,1)S(1)}, bf16[2,256,1024]{1,2,0:T(8,128)(2,1)}, u32[]{:S(2)}, u32[]{:S(2)}) collective-permute-start(bf16[2,256,1024]{1,2,0:T(8,128)(2,1)S(1)} %fusion.4), channel_id=1, source_target_pairs={{0,4},{1,5},{2,6},{3,7},{4,0},{5,1},{6,2},{7,3},{8,12},{9,13},{10,... | collective-permute-start | bytes 3145736 | tf_op jit(solution)/shard_map/ppermute | solution.py:10
  228.7 54.6 %collective-permute-done.13 = bf16[2,256,1024]{1,2,0:T(8,128)(2,1)} collective-permute-done((bf16[2,256,1024]{1,2,0:T(8,128)(2,1)S(1)}, bf16[2,256,1024]{1,2,0:T(8,128)(2,1)}, u32[]{:S(2)}, u32[]{:S(2)}) %collective-permute-start.13) | collective-permute-done | bytes 1048608 | tf_op jit(solution)/shard_map/ppermute | solution.py:10
  283.3 1.8 fusion.22
  285.1 0.5 fusion.13
  285.7 20.1 %collective-permute-done.5 = bf16[2,256,1024]{1,2,0:T(8,128)(2,1)} collective-permute-done((bf16[2,256,1024]{1,2,0:T(8,128)(2,1)S(1)}, bf16[2,256,1024]{1,2,0:T(8,128)(2,1)}, u32[]{:S(2)}, u32[]{:S(2)}) %collective-permute-start.5) | collective-permute-done | bytes 1048608 | tf_op jit(solution)/shard_map/ppermute | solution.py:10
  305.8 1.7 fusion.46
  307.5 0.5 fusion.5
  308.1 20.1 %collective-permute-done.14 = bf16[2,256,1024]{1,2,0:T(8,128)(2,1)} collective-permute-done((bf16[2,256,1024]{1,2,0:T(8,128)(2,1)S(1)}, bf16[2,256,1024]{1,2,0:T(8,128)(2,1)}, u32[]{:S(2)}, u32[]{:S(2)}) %collective-permute-start.14) | collective-permute-done | bytes 1048608 | tf_op jit(solution)/shard_map/ppermute | solution.py:10
  328.2 1.8 fusion.19
  330.1 0.5 fusion.14
  330.6 1.3 collective-permute-start.15
  331.9 18.8 %collective-permute-done.6 = bf16[2,256,1024]{1,2,0:T(8,128)(2,1)} collective-permute-done((bf16[2,256,1024]{1,2,0:T(8,128)(2,1)S(1)}, bf16[2,256,1024]{1,2,0:T(8,128)(2,1)}, u32[]{:S(2)}, u32[]{:S(2)}) %collective-permute-start.6) | collective-permute-done | bytes 1048608 | tf_op jit(solution)/shard_map/ppermute | solution.py:10
  350.7 1.7 fusion.43
  352.4 0.5 fusion.6
  352.9 1.3 collective-permute-start.7
  354.2 0.7 collective-permute-done.15
  354.9 1.8 fusion.16
  356.7 0.5 fusion.15
  357.2 20.3 %collective-permute-done.7 = bf16[2,256,1024]{1,2,0:T(8,128)(2,1)S(1)} collective-permute-done((bf16[2,256,1024]{1,2,0:T(8,128)(2,1)S(1)}, bf16[2,256,1024]{1,2,0:T(8,128)(2,1)S(1)}, u32[]{:S(2)}, u32[]{:S(2)}) %collective-permute-start.7) | collective-permute-done | bytes 1048608 | tf_op jit(solution)/shard_map/ppermute | solution.py:10
  377.5 0.5 fusion.40
  378.0 0.5 fusion.7
  378.7 2.4 copy.9
  (40 shorter events, 0.6 us)
Async XLA Ops:
  0.0 5.7 %copy-start = (bf16[4,1,1,256,1024]{4,3,2,1,0:T(8,128)(2,1)S(1)}, bf16[4,1,1,256,1024]{4,3,2,1,0:T(8,128)(2,1)}, u32[]{:S(2)}) copy-start(bf16[4,1,1,256,1024]{4,3,2,1,0:T(8,128)(2,1)} %param.3) | copy-start | bytes 6291460
  2.4 8.1 %collective-permute-start.8 = (bf16[2,256,1024]{2,1,0:T(8,128)(2,1)}, bf16[2,256,1024]{2,1,0:T(8,128)(2,1)S(1)}, u32[]{:S(2)}, u32[]{:S(2)}) collective-permute-start(bf16[2,256,1024]{2,1,0:T(8,128)(2,1)} %slice_bitcast_fusion.1), channel_id=1, source_target_pairs={{0,16},{16,0},{32,48},{48,32},{64,80},{80,64},{96,112},{112,96},{1... | collective-permute-start | bytes 3145736 | tf_op jit(solution)/shard_map/ppermute | solution.py:10
  6.7 8.5 %collective-permute-start = (bf16[2,256,1024]{2,1,0:T(8,128)(2,1)}, bf16[2,256,1024]{2,1,0:T(8,128)(2,1)}, u32[]{:S(2)}, u32[]{:S(2)}) collective-permute-start(bf16[2,256,1024]{2,1,0:T(8,128)(2,1)} %slice_bitcast_fusion), channel_id=1, source_target_pairs={{0,16},{16,0},{32,48},{48,32},{64,80},{80,64},{96,112},{112,96},{1... | collective-permute-start | bytes 3145736 | tf_op jit(solution)/shard_map/ppermute | solution.py:10
  10.6 1.0 copy-start.2
  14.0 26.9 %collective-permute-start.9 = (bf16[2,256,1024]{1,2,0:T(8,128)(2,1)S(1)}, bf16[2,256,1024]{1,2,0:T(8,128)(2,1)}, u32[]{:S(2)}, u32[]{:S(2)}) collective-permute-start(bf16[2,256,1024]{1,2,0:T(8,128)(2,1)S(1)} %fusion.8), channel_id=1, source_target_pairs={{0,32},{16,48},{32,0},{48,16},{64,96},{80,112},{96,64},{112,80},{1... | collective-permute-start | bytes 3145736 | tf_op jit(solution)/shard_map/ppermute | solution.py:10
  18.6 44.2 %collective-permute-start.1 = (bf16[2,256,1024]{1,2,0:T(8,128)(2,1)}, bf16[2,256,1024]{1,2,0:T(8,128)(2,1)}, u32[]{:S(2)}, u32[]{:S(2)}) collective-permute-start(bf16[2,256,1024]{1,2,0:T(8,128)(2,1)} %fusion), channel_id=1, source_target_pairs={{0,32},{16,48},{32,0},{48,16},{64,96},{80,112},{96,64},{112,80},{1... | collective-permute-start | bytes 3145736 | tf_op jit(solution)/shard_map/ppermute | solution.py:10
  40.8 1.8 copy-start.16
  42.6 20.1 %copy-start.14 = (bf16[2,256,512]{2,1,0:T(8,128)(2,1)S(1)}, bf16[2,256,512]{2,1,0:T(8,128)(2,1)}, u32[]{:S(2)}) copy-start(bf16[2,256,512]{2,1,0:T(8,128)(2,1)} %get-tuple-element.19) | copy-start | bytes 1572868
  43.2 24.9 %collective-permute-start.10 = (bf16[2,256,1024]{1,2,0:T(8,128)(2,1)S(1)}, bf16[2,256,1024]{1,2,0:T(8,128)(2,1)S(1)}, u32[]{:S(2)}, u32[]{:S(2)}) collective-permute-start(bf16[2,256,1024]{1,2,0:T(8,128)(2,1)S(1)} %fusion.9), channel_id=1, source_target_pairs={{0,64},{16,80},{32,96},{48,112},{64,0},{80,16},{96,32},{112,48},{1... | collective-permute-start | bytes 3145736 | tf_op jit(solution)/shard_map/ppermute | solution.py:10
  66.2 24.6 %copy-start.1 = (bf16[2,256,1024]{1,2,0:T(8,128)(2,1)}, bf16[2,256,1024]{1,2,0:T(8,128)(2,1)S(1)}, u32[]{:S(2)}) copy-start(bf16[2,256,1024]{1,2,0:T(8,128)(2,1)S(1)} %fusion.1) | copy-start | bytes 3145732
  66.2 24.5 %collective-permute-start.2 = (bf16[2,256,1024]{1,2,0:T(8,128)(2,1)S(1)}, bf16[2,256,1024]{1,2,0:T(8,128)(2,1)}, u32[]{:S(2)}, u32[]{:S(2)}) collective-permute-start(bf16[2,256,1024]{1,2,0:T(8,128)(2,1)S(1)} %fusion.1), channel_id=1, source_target_pairs={{0,64},{16,80},{32,96},{48,112},{64,0},{80,16},{96,32},{112,48},{1... | collective-permute-start | bytes 3145736 | tf_op jit(solution)/shard_map/ppermute | solution.py:10
  68.1 1.0 copy-start.4
  69.1 1.5 copy-start.12
  70.6 20.2 %copy-start.10 = (bf16[2,256,512]{2,1,0:T(8,128)(2,1)S(1)}, bf16[2,256,512]{2,1,0:T(8,128)(2,1)}, u32[]{:S(2)}) copy-start(bf16[2,256,512]{2,1,0:T(8,128)(2,1)} %get-tuple-element.18) | copy-start | bytes 1572868
  71.1 42.5 %collective-permute-start.11 = (bf16[2,256,1024]{1,2,0:T(8,128)(2,1)S(1)}, bf16[2,256,1024]{1,2,0:T(8,128)(2,1)S(1)}, u32[]{:S(2)}, u32[]{:S(2)}) collective-permute-start(bf16[2,256,1024]{1,2,0:T(8,128)(2,1)S(1)} %fusion.10), channel_id=1, source_target_pairs={{0,128},{16,144},{32,160},{48,176},{64,192},{80,208},{96,224},{112... | collective-permute-start | bytes 3145736 | tf_op jit(solution)/shard_map/ppermute | solution.py:10
  94.2 42.0 %collective-permute-start.3 = (bf16[2,256,1024]{1,2,0:T(8,128)(2,1)S(1)}, bf16[2,256,1024]{1,2,0:T(8,128)(2,1)}, u32[]{:S(2)}, u32[]{:S(2)}) collective-permute-start(bf16[2,256,1024]{1,2,0:T(8,128)(2,1)S(1)} %fusion.2), channel_id=1, source_target_pairs={{0,128},{16,144},{32,160},{48,176},{64,192},{80,208},{96,224},{112... | collective-permute-start | bytes 3145736 | tf_op jit(solution)/shard_map/ppermute | solution.py:10
  113.6 1.0 copy-start.3
  114.6 1.5 copy-start.8
  116.1 20.1 %copy-start.5 = (bf16[2,256,512]{2,1,0:T(8,128)(2,1)S(1)}, bf16[2,256,512]{2,1,0:T(8,128)(2,1)}, u32[]{:S(2)}) copy-start(bf16[2,256,512]{2,1,0:T(8,128)(2,1)} %get-tuple-element.13) | copy-start | bytes 1572868
  116.6 33.3 %collective-permute-start.12 = (bf16[2,256,1024]{1,2,0:T(8,128)(2,1)S(1)}, bf16[2,256,1024]{1,2,0:T(8,128)(2,1)}, u32[]{:S(2)}, u32[]{:S(2)}) collective-permute-start(bf16[2,256,1024]{1,2,0:T(8,128)(2,1)S(1)} %fusion.11), channel_id=1, source_target_pairs={{0,8},{1,9},{2,10},{3,11},{4,12},{5,13},{6,14},{7,15},{8,0},{9,1},... | collective-permute-start | bytes 3145736 | tf_op jit(solution)/shard_map/ppermute | solution.py:10
  138.4 63.9 %collective-permute-start.4 = (bf16[2,256,1024]{1,2,0:T(8,128)(2,1)S(1)}, bf16[2,256,1024]{1,2,0:T(8,128)(2,1)}, u32[]{:S(2)}, u32[]{:S(2)}) collective-permute-start(bf16[2,256,1024]{1,2,0:T(8,128)(2,1)S(1)} %fusion.3), channel_id=1, source_target_pairs={{0,8},{1,9},{2,10},{3,11},{4,12},{5,13},{6,14},{7,15},{8,0},{9,1},... | collective-permute-start | bytes 3145736 | tf_op jit(solution)/shard_map/ppermute | solution.py:10
  152.2 131.1 %collective-permute-start.13 = (bf16[2,256,1024]{1,2,0:T(8,128)(2,1)S(1)}, bf16[2,256,1024]{1,2,0:T(8,128)(2,1)}, u32[]{:S(2)}, u32[]{:S(2)}) collective-permute-start(bf16[2,256,1024]{1,2,0:T(8,128)(2,1)S(1)} %fusion.12), channel_id=1, source_target_pairs={{0,4},{1,5},{2,6},{3,7},{4,0},{5,1},{6,2},{7,3},{8,12},{9,13},{10,... | collective-permute-start | bytes 3145736 | tf_op jit(solution)/shard_map/ppermute | solution.py:10
  204.5 101.3 %collective-permute-start.5 = (bf16[2,256,1024]{1,2,0:T(8,128)(2,1)S(1)}, bf16[2,256,1024]{1,2,0:T(8,128)(2,1)}, u32[]{:S(2)}, u32[]{:S(2)}) collective-permute-start(bf16[2,256,1024]{1,2,0:T(8,128)(2,1)S(1)} %fusion.4), channel_id=1, source_target_pairs={{0,4},{1,5},{2,6},{3,7},{4,0},{5,1},{6,2},{7,3},{8,12},{9,13},{10,... | collective-permute-start | bytes 3145736 | tf_op jit(solution)/shard_map/ppermute | solution.py:10
  283.3 1.8 copy-start.15
  285.1 20.7 %copy-start.13 = (bf16[2,256,512]{2,1,0:T(8,128)(2,1)S(1)}, bf16[2,256,512]{2,1,0:T(8,128)(2,1)}, u32[]{:S(2)}) copy-start(bf16[2,256,512]{2,1,0:T(8,128)(2,1)} %get-tuple-element.11) | copy-start | bytes 1572868
  285.6 42.6 %collective-permute-start.14 = (bf16[2,256,1024]{1,2,0:T(8,128)(2,1)S(1)}, bf16[2,256,1024]{1,2,0:T(8,128)(2,1)}, u32[]{:S(2)}, u32[]{:S(2)}) collective-permute-start(bf16[2,256,1024]{1,2,0:T(8,128)(2,1)S(1)} %fusion.13), channel_id=1, source_target_pairs={{0,2},{1,3},{2,0},{3,1},{4,6},{5,7},{6,4},{7,5},{8,10},{9,11},{10,... | collective-permute-start | bytes 3145736 | tf_op jit(solution)/shard_map/ppermute | solution.py:10
  308.0 42.7 %collective-permute-start.6 = (bf16[2,256,1024]{1,2,0:T(8,128)(2,1)S(1)}, bf16[2,256,1024]{1,2,0:T(8,128)(2,1)}, u32[]{:S(2)}, u32[]{:S(2)}) collective-permute-start(bf16[2,256,1024]{1,2,0:T(8,128)(2,1)S(1)} %fusion.5), channel_id=1, source_target_pairs={{0,2},{1,3},{2,0},{3,1},{4,6},{5,7},{6,4},{7,5},{8,10},{9,11},{10,... | collective-permute-start | bytes 3145736 | tf_op jit(solution)/shard_map/ppermute | solution.py:10
  328.2 1.8 copy-start.11
  330.0 20.7 %copy-start.9 = (bf16[2,256,512]{2,1,0:T(8,128)(2,1)S(1)}, bf16[2,256,512]{2,1,0:T(8,128)(2,1)}, u32[]{:S(2)}) copy-start(bf16[2,256,512]{2,1,0:T(8,128)(2,1)} %get-tuple-element.10) | copy-start | bytes 1572868
  330.6 24.3 %collective-permute-start.15 = (bf16[2,256,1024]{1,2,0:T(8,128)(2,1)S(1)}, bf16[2,256,1024]{1,2,0:T(8,128)(2,1)}, u32[]{:S(2)}, u32[]{:S(2)}) collective-permute-start(bf16[2,256,1024]{1,2,0:T(8,128)(2,1)S(1)} %fusion.14), channel_id=1, source_target_pairs={{0,1},{1,0},{2,3},{3,2},{4,5},{5,4},{6,7},{7,6},{8,9},{9,8},{10,11... | collective-permute-start | bytes 3145736 | tf_op jit(solution)/shard_map/ppermute | solution.py:10
  352.9 24.6 %collective-permute-start.7 = (bf16[2,256,1024]{1,2,0:T(8,128)(2,1)S(1)}, bf16[2,256,1024]{1,2,0:T(8,128)(2,1)S(1)}, u32[]{:S(2)}, u32[]{:S(2)}) collective-permute-start(bf16[2,256,1024]{1,2,0:T(8,128)(2,1)S(1)} %fusion.6), channel_id=1, source_target_pairs={{0,1},{1,0},{2,3},{3,2},{4,5},{5,4},{6,7},{7,6},{8,9},{9,8},{10,11... | collective-permute-start | bytes 3145736 | tf_op jit(solution)/shard_map/ppermute | solution.py:10
  354.9 1.8 copy-start.7
  356.7 20.8 %copy-start.6 = (bf16[2,256,512]{2,1,0:T(8,128)(2,1)S(1)}, bf16[2,256,512]{2,1,0:T(8,128)(2,1)}, u32[]{:S(2)}) copy-start(bf16[2,256,512]{2,1,0:T(8,128)(2,1)} %get-tuple-element.5) | copy-start | bytes 1572868
where the time goes:
time: 382 us; the launch traced here: 381 us
  waiting for transfers between devices  226 us (59%)
  starting transfers between devices  100 us (26%)
  matrix products  37.8 us (10%)
  local copies, waits for them, and re-layouts  16.5 us (4%)
    ppermute x16, waiting for transfers between devices, from_partner(): return lax.ppermute(value, axis, pairs)  226 us
    ppermute x16, starting transfers between devices, from_partner(): return lax.ppermute(value, axis, pairs)  100 us
    dot_general x16, matrix products, combine(): jnp.einsum('brk,bkh->brh', factors[:, :, rank_size:], trailing, preferred...  23.6 us
    dot_general x16, matrix products, combine(): jnp.einsum('brk,bkh->brh', factors[:, :, :rank_size], leading, preferred_...  14.2 us
    squeeze x2, local copies, waits for them, and re-layouts, run_pass(): factors[level_no, :half_count]  7.67 us
  transfers between devices with their start and end apart: 16, of which 13 were waited for; matrix products, arithmetic and copies ran while one was open for 12% of the time, Pallas kernels for 0%

commit v1 on v0

v1 whole, which is shorter than its diff:
```python
import functools

import jax
import jax.numpy as jnp
from jax import lax
from jax.experimental import pallas as pl
from jax.experimental.pallas import tpu as pltpu
from jax.sharding import PartitionSpec as P

WIDTHS = (512, 512)
RANK = 256
VMEM = 48 * 2**20


def swap_dest(step):
    pairs = []
    for device in range(256):
        leaf, wide = device >> 4, device & 15
        core, top, low = leaf & 1, wide >> 3, (wide >> 1) & 3
        dest_leaf = (leaf & ~1) | top
        dest_wide = (core << 3) | ((low ^ step) << 1) | (wide & 1)
        pairs.append((device, dest_leaf << 4 | dest_wide))
    return pairs


SWAPS = [swap_dest(step) for step in range(4)]


def swap(value, step):
    return lax.ppermute(value, ("leaf", "wide"), SWAPS[step])


def exchange(value, axis, mask):
    return lax.ppermute(value, axis, [(d, d ^ mask) for d in range(16)])


def dot(a, b):
    return jnp.dot(a, b, preferred_element_type=jnp.float32)


def cross(factor, own, other, high):
    first = pl.multiple_of(high * RANK, RANK)
    second = pl.multiple_of((1 - high) * RANK, RANK)
    total = dot(factor[:, pl.ds(first, RANK)], own) + dot(factor[:, pl.ds(second, RANK)], other)
    return total.astype(jnp.bfloat16)


def level_body(split, flags, factor, own, partner, *outs):
    high = flags[1]
    result = cross(factor.at[0, 0], own[0], partner[0], high)
    if split:
        for step in range(4):
            @pl.when(pl.program_id(0) == step)
            def _():
                outs[step][...] = result
    else:
        outs[-1][0] = result


def cost(n_dots, width, bytes_accessed):
    return pl.CostEstimate(flops=1, bytes_accessed=1, transcendentals=0)


def level_call(factors, level_no, own, partner, flags, width, natural=False, split=False, into=None, column=None, total_width=None, steps=(0, 1, 2, 3)):
    block = (1, RANK, width)
    stride, first = steps[1] - steps[0], steps[0]
    if natural:
        place = lambda t, s: (s[0] ^ t, 0, 0)
    else:
        place = lambda t, s: (t, 0, 0)
    in_specs = [
        pl.BlockSpec((1, 1, RANK, 2 * RANK), lambda t, s: (level_no, s[0] ^ (t * stride + first), 0, 0)),
        pl.BlockSpec(block, place),
        pl.BlockSpec(block, place),
    ]
    operands = [factors, own, partner]
    aliases = {}
    if split:
        out_shape = [jax.ShapeDtypeStruct((RANK, width), jnp.bfloat16)] * 4
        out_specs = [pl.BlockSpec((RANK, width), lambda t, s: (0, 0))] * 4
    elif column is not None:
        out_shape = jax.ShapeDtypeStruct((4, RANK, total_width), jnp.bfloat16)
        out_specs = pl.BlockSpec(block, lambda t, s: (s[0] ^ (t * stride + first), 0, column // width))
        if into is not None:
            in_specs.append(pl.BlockSpec(memory_space=pl.ANY))
            operands.append(into)
            aliases = {4: 0}
    else:
        out_shape = jax.ShapeDtypeStruct((4, RANK, width), jnp.bfloat16)
        out_specs = pl.BlockSpec(block, lambda t, s: (t, 0, 0))
    return pl.pallas_call(
        functools.partial(level_body, split),
        grid_spec=pltpu.PrefetchScalarGridSpec(num_scalar_prefetch=1, grid=(len(steps),), in_specs=in_specs, out_specs=out_specs),
        out_shape=out_shape,
        input_output_aliases=aliases,
        cost_estimate=cost(8, width, 4 * RANK * (3 * width + 2 * RANK) * 2),
        compiler_params=pltpu.CompilerParams(vmem_limit_bytes=VMEM),
    )(flags, *operands)


def take_body(flags, *refs):
    for t in range(4):
        for h in range(2):
            refs[4 + 2 * t + h][0] = refs[t][0, 0, h * (RANK // 2) : (h + 1) * (RANK // 2)]


def take_call(factors, flags):
    block = lambda step: pl.BlockSpec((1, 1, RANK, 2 * RANK), lambda g, s: (g + 1, s[0] ^ step, 0, 0))
    return pl.pallas_call(
        take_body,
        grid_spec=pltpu.PrefetchScalarGridSpec(
            num_scalar_prefetch=1,
            grid=(3,),
            in_specs=[block(t) for t in range(4)],
            out_specs=[pl.BlockSpec((1, RANK // 2, 2 * RANK), lambda g, s: (g, 0, 0))] * 8,
        ),
        out_shape=[jax.ShapeDtypeStruct((3, RANK // 2, 2 * RANK), jnp.bfloat16)] * 8,
        cost_estimate=cost(8, RANK, 1),
        compiler_params=pltpu.CompilerParams(vmem_limit_bytes=VMEM),
    )(flags, *[factors] * 4)


def three_body(flags, own, partner, *refs):
    low, high = flags[0], flags[1]
    factors, outs = refs[:8], refs[8:]

    def halves(t, row, mine, other, is_high):
        parts = [cross(factors[2 * t + h].at[row], mine, other, is_high) for h in range(2)]
        return jnp.concatenate(parts, axis=0)

    values = [halves(t, 2, own[t], partner[t], high) for t in range(4)]
    for bit, row in ((1, 1), (0, 0)):
        apart = 1 << bit
        values = [halves(t, row, values[t], values[t ^ apart], ((low ^ t) >> bit) & 1) for t in range(4)]
    for t in range(4):
        outs[t][...] = values[t]


def three_call(factors, own, partner, flags, width):
    whole = lambda shape: pl.BlockSpec(shape, lambda g, s: (0,) * len(shape))
    return pl.pallas_call(
        three_body,
        grid_spec=pltpu.PrefetchScalarGridSpec(
            num_scalar_prefetch=1,
            grid=(1,),
            in_specs=[whole((4, RANK, width))] * 2 + [whole((3, RANK // 2, 2 * RANK))] * 8,
            out_specs=[whole((RANK, width))] * 4,
        ),
        out_shape=[jax.ShapeDtypeStruct((RANK, width), jnp.bfloat16)] * 4,
        cost_estimate=cost(24, width, 4 * RANK * (3 * width + 6 * RANK) * 2),
        compiler_params=pltpu.CompilerParams(vmem_limit_bytes=VMEM),
    )(flags, own, partner, *factors)


GROUPS = ((1, 3), (0, 2))


def make_order():
    order = []
    work = lambda *name: order.append(("work", name))
    start = lambda *name: order.append(("start", name))
    done = lambda *name: order.append(("done", name))

    def level(number, chunk):
        done("send", number, chunk)
        work("level", number, chunk)

    def all_of(action, kind, chunk, steps=(1, 3, 0, 2)):
        for t in steps:
            action(kind, t, chunk)

    pieces = [(t, h) for h in range(2) for t in (1, 3, 0, 2)]
    batches = (pieces[:2], pieces[2:5], pieces[5:])

    def factor(batch, action):
        for piece in batches[batch]:
            action("fsend", *piece)

    work("cut", 0)
    start("send", 0, 0)
    work("fcut")
    factor(0, start)
    level(0, 0)
    start("send", 1, 0)
    work("cut", 1)
    start("send", 0, 1)
    level(0, 1)
    factor(0, done)
    factor(1, start)
    level(1, 0)
    start("send", 2, 0)
    start("send", 1, 1)
    factor(1, done)
    factor(2, start)
    level(2, 0)
    start("send", 3, 0)
    level(1, 1)
    factor(2, done)
    done("send", 3, 0)
    start("send", 2, 1)
    work("level", 3, 0)
    all_of(start, "go", 0)
    level(2, 1)
    start("send", 3, 1)
    all_of(done, "go", 0)
    start("acore", 0)
    done("acore", 0)
    work("three", 0)
    all_of(start, "back", 0)
    level(3, 1)
    all_of(done, "back", 0, GROUPS[0])
    all_of(start, "go", 1, GROUPS[0])
    start("dsend", 0, 0)
    all_of(done, "back", 0, GROUPS[1])
    all_of(start, "go", 1, GROUPS[1])
    done("dsend", 0, 0)
    start("dsend", 1, 0)
    work("last", 0, 0)
    all_of(done, "go", 1)
    start("acore", 1)
    done("dsend", 1, 0)
    work("last", 1, 0)
    done("acore", 1)
    work("three", 1)
    all_of(start, "back", 1)
    all_of(done, "back", 1, GROUPS[0])
    start("dsend", 0, 1)
    all_of(done, "back", 1, GROUPS[1])
    start("dsend", 1, 1)
    for h in range(2):
        done("dsend", h, 1)
        work("last", h, 1)
    return order


def per_device(source, row_factors, column_factors):
    columns = source.shape[-1]
    source = source.reshape(4, RANK, columns)
    forward = row_factors.reshape(4, 4, RANK, 2 * RANK)
    adjoint = column_factors.reshape(4, 4, RANK, 2 * RANK)
    leaf, wide = lax.axis_index("leaf"), lax.axis_index("wide")
    low = (wide >> 1) & 3
    row_flags = [jnp.stack([low, (leaf >> level) & 1]).astype(jnp.int32) for level in range(4)]
    last_flags = jnp.stack([low, wide & 1]).astype(jnp.int32)
    starts = [sum(WIDTHS[:c]) for c in range(len(WIDTHS))]

    order = make_order()
    values = {}
    token = last_flags
    output = None

    def tie(value):
        nonlocal token
        value, token = lax.optimization_barrier((value, token))
        return value

    for action, name in order:
        kind = name[0]
        if action == "done":
            values[name] = tie(values[name])
        elif action == "work":
            c = name[-1]
            if kind == "fcut":
                values[name] = tie(take_call(adjoint, tie(last_flags)))
            elif kind == "cut":
                block = lax.slice_in_dim(tie(source), starts[c], starts[c] + WIDTHS[c], axis=2)
                values[name] = tie(block)
            elif kind == "level":
                level = name[1]
                own = values["cut", c] if level == 0 else values["level", level - 1, c]
                result = level_call(
                    forward, level, tie(own), values["send", level, c], row_flags[level], WIDTHS[c],
                    natural=level == 0, split=level == 3,
                )
                values[name] = tie(result)
            elif kind == "three":
                result = three_call(
                    [values["fsend", t, h] for t in range(4) for h in range(2)], tie(values["stack", c]), values["acore", c], row_flags[0], WIDTHS[c],
                )
                values[name] = tie(result)
            elif kind == "last":
                half = name[1]
                output = level_call(
                    adjoint, 0, tie(values["dstack", half, c]), values["dsend", half, c], last_flags, WIDTHS[c],
                    into=output, column=starts[c], total_width=columns, steps=GROUPS[half],
                )
                output = tie(output)
        else:
            c = name[-1]
            if kind == "fsend":
                values[name] = swap(tie(values["fcut",][2 * name[1] + c]), name[1])
            elif kind == "send":
                level = name[1]
                own = values["cut", c] if level == 0 else values["level", level - 1, c]
                values[name] = exchange(tie(own), "leaf", 1 << level)
            elif kind == "go":
                values[name] = swap(tie(values["level", 3, c][name[1]]), name[1])
            elif kind == "acore":
                values["stack", c] = tie(jnp.stack([values["go", t, c] for t in range(4)]))
                values[name] = exchange(values["stack", c], "leaf", 1)
            elif kind == "back":
                values[name] = swap(tie(values["three", c][name[1]]), name[1])
            elif kind == "dsend":
                half = name[1]
                stack = tie(jnp.stack([values["back", t, c] for t in GROUPS[half]]))
                values["dstack", half, c] = stack
                values[name] = exchange(stack, "wide", 1)
    return output.reshape(4, 1, 1, RANK, columns)


def solution(mesh):
    return jax.shard_map(
        per_device,
        mesh=mesh,
        in_specs=(
            P(None, "leaf", "wide", None, None),
            P(None, None, "leaf", "wide", None, None),
            P(None, None, "leaf", "wide", None, None),
        ),
        out_specs=P(None, "leaf", "wide", None, None),
        check_vma=False,
    )
```

time: 382 us -> 270 us (0.71)
  waiting for transfers between devices: 226 us -> 113 us
  Pallas kernels: 0 us -> 48.2 us
  matrix products: 37.8 us -> 0 us
  local copies, waits for them, and re-layouts: 16.5 us -> 5.56 us
    ppermute x16 -> x38, waiting for transfers between devices: 226 us -> 113 us  [the longest x24 82.5 us: swap(): return lax.ppermute(value, ('leaf', 'wide'), SWAPS[step])]
    pallas_call x0 -> x15, Pallas kernels: none -> 48.2 us  [the longest x12 35.9 us: level_call(): pl.pallas_call(functools.partial(level_body, split), grid_spec=pltpu.Pref...]
    dot_general x32 -> x0, matrix products: 37.8 us -> none  [the longest x16 23.6 us: combine(): jnp.einsum('brk,bkh->brh', factors[:, :, rank_size:], trailing, preferred...]
    squeeze x2 -> x0, local copies, waits for them, and re-layouts: 7.67 us -> none  [run_pass(): factors[level_no, :half_count]]
    ppermute x16 -> x38, starting transfers between devices: 100 us -> 100 us  [the longest x24 83.4 us: swap(): return lax.ppermute(value, ('leaf', 'wide'), SWAPS[step])]
  transfers between devices with their start and end apart: 16 -> 38, of which waited for: 13 -> 19; matrix products, arithmetic and copies ran while one was open for 12% -> 0% of each run, Pallas kernels for 0% -> 13%
where the time goes in v1:
time: 270 us; the launch traced here: 268 us
  waiting for transfers between devices  113 us (42%)
  starting transfers between devices  100 us (37%)
  Pallas kernels  48.2 us (18%)
  local copies, waits for them, and re-layouts  5.56 us (2%)
    ppermute x24, starting transfers between devices, swap(): return lax.ppermute(value, ('leaf', 'wide'), SWAPS[step])  83.4 us
    ppermute x24, waiting for transfers between devices, swap(): return lax.ppermute(value, ('leaf', 'wide'), SWAPS[step])  82.5 us
    pallas_call x12, Pallas kernels, level_call(): pl.pallas_call(functools.partial(level_body, split), grid_spec=pltpu.Pref...  35.9 us
    ppermute x14, waiting for transfers between devices, exchange(): return lax.ppermute(value, axis, [(d, d ^ mask) for d in range(16)])  30.3 us
    ppermute x14, starting transfers between devices, exchange(): return lax.ppermute(value, axis, [(d, d ^ mask) for d in range(16)])  17 us
    pallas_call x2, Pallas kernels, three_call(): pl.pallas_call(three_body, grid_spec=pltpu.PrefetchScalarGridSpec(num_sca...  7.89 us
  transfers between devices with their start and end apart: 38, of which 19 were waited for; matrix products, arithmetic and copies ran while one was open for 0% of the time, Pallas kernels for 13%

profile of v1, /device:TPU:1, one launch (start us, length us, event | category | flops | bytes accessed | tf_op | source)
XLA Modules:
  0.0 268.1 jit_solution(14098009029671826608)
XLA Ops:
  0.1 1.3 slice.6.own
  1.4 3.3 %collective-permute-start = (bf16[4,256,512]{2,1,0:T(8,128)(2,1)S(1)}, bf16[4,256,512]{2,1,0:T(8,128)(2,1)S(1)}, u32[]{:S(2)}, u32[]{:S(2)}) collective-permute-start(bf16[4,256,512]{2,1,0:T(8,128)(2,1)S(1)} %slice.6.own), channel_id=1, source_target_pairs={{0,16},{16,0},{32,48},{48,32},{64,80},{80,64},{96,112},{112,96},{1... | collective-permute-start | bytes 3145736 | tf_op jit(solution)/shard_map/ppermute | solution.py:34
  4.7 4.5 %shard_map.37 = (bf16[3,128,512]{2,1,0:T(8,128)(2,1)}, bf16[3,128,512]{2,1,0:T(8,128)(2,1)S(1)}, bf16[3,128,512]{2,1,0:T(8,128)(2,1)}, bf16[3,128,512]{2,1,0:T(8...) custom-call(s32[2]{0:T(128)S(1)} %get-tuple-element.410.flags, ...), custom_call_target="tpu_custom_call" | custom-call | flops 1 | bytes 1 | tf_op jit(solution)/shard_map/pallas_call | solution.py:109
  9.2 3.9 %shard_map.38.own = bf16[4,256,512]{2,1,0:T(8,128)(2,1)S(1)} custom-call(s32[2]{0:T(128)S(1)} %get-tuple-element.462.flags, bf16[4,4,256,512]{3,2,1,0:T(8,128)(2,1)} %bitcast.36, bf16[4,256,512]{2,1,0:T(8,128)(2,1)S(1)} %slice.6.own, bf16[4,256,512]{2,1,0:T(8,128)(2,1)S(1)} %collective-permute-done.partner), custom_call_target="tpu_custom_call" | custom-call | flops 1 | bytes 1 | tf_op jit(solution)/shard_map/pallas_call | solution.py:91
  13.4 1.3 collective-permute-start.2
  14.6 7.0 %collective-permute-start.4 = (bf16[3,128,512]{2,1,0:T(8,128)(2,1)}, bf16[3,128,512]{2,1,0:T(8,128)(2,1)S(1)}, u32[]{:S(2)}, u32[]{:S(2)}) collective-permute-start(bf16[3,128,512]{2,1,0:T(8,128)(2,1)} %get-tuple-element.274), channel_id=1, source_target_pairs={{0,2},{1,3},{2,0},{3,1},{4,6},{5,7},{6,4},{7,5},{8,18},{9,19},{10,... | collective-permute-start | bytes 1179656 | tf_op jit(solution)/shard_map/ppermute | solution.py:30
  21.8 1.0 copy-done.1
  22.7 1.2 copy-done.2
  23.9 3.4 %shard_map.39.own = bf16[4,256,512]{2,1,0:T(8,128)(2,1)S(1)} custom-call(s32[2]{0:T(128)S(1)} %get-tuple-element.462.flags, bf16[4,4,256,512]{3,2,1,0:T(8,128)(2,1)} %bitcast.37, bf16[4,256,512]{2,1,0:T(8,128)(2,1)S(1)} %slice.7.own, bf16[4,256,512]{2,1,0:T(8,128)(2,1)S(1)} %copy-done.2), custom_call_target="tpu_custom_call" | custom-call | flops 1 | bytes 1 | tf_op jit(solution)/shard_map/pallas_call | solution.py:91
  27.4 7.8 %collective-permute-done.4.refs_2_ = bf16[3,128,512]{2,1,0:T(8,128)(2,1)S(1)} collective-permute-done((bf16[3,128,512]{2,1,0:T(8,128)(2,1)}, bf16[3,128,512]{2,1,0:T(8,128)(2,1)S(1)}, u32[]{:S(2)}, u32[]{:S(2)}) %collective-permute-start.4) | collective-permute-done | bytes 393248 | tf_op jit(solution)/shard_map/ppermute | solution.py:30
  35.2 4.3 %collective-permute-done.3.refs_6_ = bf16[3,128,512]{2,1,0:T(8,128)(2,1)} collective-permute-done((bf16[3,128,512]{2,1,0:T(8,128)(2,1)}, bf16[3,128,512]{2,1,0:T(8,128)(2,1)}, u32[]{:S(2)}, u32[]{:S(2)}) %collective-permute-start.3) | collective-permute-done | bytes 393248 | tf_op jit(solution)/shard_map/ppermute | solution.py:30
  39.5 3.6 %shard_map.40.own = bf16[4,256,512]{2,1,0:T(8,128)(2,1)S(1)} custom-call(s32[2]{0:T(128)S(1)} %pad_add_fusion.4.flags, bf16[4,4,256,512]{3,2,1,0:T(8,128)(2,1)} %bitcast.38, bf16[4,256,512]{2,1,0:T(8,128)(2,1)S(1)} %shard_map.38.own, bf16[4,256,512]{2,1,0:T(8,128)(2,1)} %collective-permute-done.2.partner), custom_call_target="tpu_custom_call" | custom-call | flops 1 | bytes 1 | tf_op jit(solution)/shard_map/pallas_call | solution.py:91
  43.1 1.2 collective-permute-start.6
  44.3 8.5 %collective-permute-start.9 = (bf16[3,128,512]{2,1,0:T(8,128)(2,1)}, bf16[3,128,512]{2,1,0:T(8,128)(2,1)S(1)}, u32[]{:S(2)}, u32[]{:S(2)}) collective-permute-start(bf16[3,128,512]{2,1,0:T(8,128)(2,1)} %get-tuple-element.294), channel_id=1, source_target_pairs={{0,0},{1,1},{2,2},{3,3},{4,4},{5,5},{6,6},{7,7},{8,16},{9,17},{10,... | collective-permute-start | bytes 1179656 | tf_op jit(solution)/shard_map/ppermute | solution.py:30
  52.9 4.3 %collective-permute-start.7 = (bf16[3,128,512]{2,1,0:T(8,128)(2,1)}, bf16[3,128,512]{2,1,0:T(8,128)(2,1)}, u32[]{:S(2)}, u32[]{:S(2)}) collective-permute-start(bf16[3,128,512]{2,1,0:T(8,128)(2,1)} %get-tuple-element.292), channel_id=1, source_target_pairs={{0,2},{1,3},{2,0},{3,1},{4,6},{5,7},{6,4},{7,5},{8,18},{9,19},{10,... | collective-permute-start | bytes 1179656 | tf_op jit(solution)/shard_map/ppermute | solution.py:30
  57.3 2.9 %collective-permute-start.5 = (bf16[4,256,512]{2,1,0:T(8,128)(2,1)S(1)}, bf16[4,256,512]{2,1,0:T(8,128)(2,1)S(1)}, u32[]{:S(2)}, u32[]{:S(2)}) collective-permute-start(bf16[4,256,512]{2,1,0:T(8,128)(2,1)S(1)} %shard_map.39.own), channel_id=1, source_target_pairs={{0,32},{16,48},{32,0},{48,16},{64,96},{80,112},{96,64},{112,80},{1... | collective-permute-start | bytes 3145736 | tf_op jit(solution)/shard_map/ppermute | solution.py:34
  60.2 11.8 %collective-permute-done.9.refs_0_ = bf16[3,128,512]{2,1,0:T(8,128)(2,1)S(1)} collective-permute-done((bf16[3,128,512]{2,1,0:T(8,128)(2,1)}, bf16[3,128,512]{2,1,0:T(8,128)(2,1)S(1)}, u32[]{:S(2)}, u32[]{:S(2)}) %collective-permute-start.9) | collective-permute-done | bytes 393248 | tf_op jit(solution)/shard_map/ppermute | solution.py:30
  72.0 6.3 %collective-permute-done.8.refs_4_ = bf16[3,128,512]{2,1,0:T(8,128)(2,1)S(1)} collective-permute-done((bf16[3,128,512]{2,1,0:T(8,128)(2,1)}, bf16[3,128,512]{2,1,0:T(8,128)(2,1)S(1)}, u32[]{:S(2)}, u32[]{:S(2)}) %collective-permute-start.8) | collective-permute-done | bytes 393248 | tf_op jit(solution)/shard_map/ppermute | solution.py:30
  79.0 3.6 %shard_map.41.own = bf16[4,256,512]{2,1,0:T(8,128)(2,1)S(1)} custom-call(s32[2]{0:T(128)S(1)} %get-tuple-element.464.flags, bf16[4,4,256,512]{3,2,1,0:T(8,128)(2,1)} %bitcast.39, bf16[4,256,512]{2,1,0:T(8,128)(2,1)S(1)} %shard_map.40.own, bf16[4,256,512]{2,1,0:T(8,128)(2,1)} %collective-permute-done.6.partner), custom_call_target="tpu_custom_call" | custom-call | flops 1 | bytes 1 | tf_op jit(solution)/shard_map/pallas_call | solution.py:91
  82.6 2.5 collective-permute-start.10
  85.1 1.3 collective-permute-start.13
  86.5 4.9 %collective-permute-start.12 = (bf16[3,128,512]{2,1,0:T(8,128)(2,1)S(1)}, bf16[3,128,512]{2,1,0:T(8,128)(2,1)S(1)}, u32[]{:S(2)}, u32[]{:S(2)}) collective-permute-start(bf16[3,128,512]{2,1,0:T(8,128)(2,1)S(1)} %copy-done.6), channel_id=1, source_target_pairs={{0,0},{1,1},{2,2},{3,3},{4,4},{5,5},{6,6},{7,7},{8,16},{9,17},{10,... | collective-permute-start | bytes 1179656 | tf_op jit(solution)/shard_map/ppermute | solution.py:30
  91.4 6.4 %collective-permute-start.11 = (bf16[3,128,512]{2,1,0:T(8,128)(2,1)S(1)}, bf16[3,128,512]{2,1,0:T(8,128)(2,1)S(1)}, u32[]{:S(2)}, u32[]{:S(2)}) collective-permute-start(bf16[3,128,512]{2,1,0:T(8,128)(2,1)S(1)} %copy-done.4), channel_id=1, source_target_pairs={{0,4},{1,5},{2,6},{3,7},{4,0},{5,1},{6,2},{7,3},{8,20},{9,21},{10,... | collective-permute-start | bytes 1179656 | tf_op jit(solution)/shard_map/ppermute | solution.py:30
  97.8 3.4 %shard_map.42.own = bf16[4,256,512]{2,1,0:T(8,128)(2,1)S(1)} custom-call(s32[2]{0:T(128)S(1)} %pad_add_fusion.4.flags, bf16[4,4,256,512]{3,2,1,0:T(8,128)(2,1)} %bitcast.40, bf16[4,256,512]{2,1,0:T(8,128)(2,1)S(1)} %shard_map.39.own, bf16[4,256,512]{2,1,0:T(8,128)(2,1)S(1)} %collective-permute-done.5.partner), custom_call_target="tpu_custom_call" | custom-call | flops 1 | bytes 1 | tf_op jit(solution)/shard_map/pallas_call | solution.py:91
  101.2 2.5 collective-permute-done.12.refs_1_
  103.7 17.5 %collective-permute-done.11.refs_5_ = bf16[3,128,512]{2,1,0:T(8,128)(2,1)S(1)} collective-permute-done((bf16[3,128,512]{2,1,0:T(8,128)(2,1)S(1)}, bf16[3,128,512]{2,1,0:T(8,128)(2,1)S(1)}, u32[]{:S(2)}, u32[]{:S(2)}) %collective-permute-start.11) | collective-permute-done | bytes 393248 | tf_op jit(solution)/shard_map/ppermute | solution.py:30
  121.2 3.5 %shard_map.43 = (bf16[256,512]{1,0:T(8,128)(2,1)S(1)}, bf16[256,512]{1,0:T(8,128)(2,1)S(1)}, bf16[256,512]{1,0:T(8,128)(2,1)S(1)}, bf16[256,512]{1,0:T(8,128)(2,1)S(1)}) custom-call(s32[2]{0:T(128)S(1)} %get-tuple-element.463.flags, bf16[4,4,256,512]{3,2,1,0:T(8,128)(2,1)} %bitcast.41, bf16[4,256,512]{2,1,0:T(8,128)(2,1)S(1)} %shard_map.41.own, ...), custom_call_target="tpu_custom_call" | custom-call | flops 1 | bytes 1 | tf_op jit(solution)/shard_map/pallas_call | solution.py:91
  124.9 6.2 %collective-permute-start.16 = (bf16[256,512]{1,0:T(8,128)(2,1)S(1)}, bf16[256,512]{1,0:T(8,128)(2,1)S(1)}, u32[]{:S(2)}, u32[]{:S(2)}) collective-permute-start(bf16[256,512]{1,0:T(8,128)(2,1)S(1)} %get-tuple-element.346), channel_id=1, source_target_pairs={{0,0},{1,1},{2,2},{3,3},{4,4},{5,5},{6,6},{7,7},{8,16},{9,17},{10,... | collective-permute-start | bytes 786440 | tf_op jit(solution)/shard_map/ppermute | solution.py:30
  131.2 5.1 %collective-permute-start.19 = (bf16[256,512]{1,0:T(8,128)(2,1)S(1)}, bf16[256,512]{1,0:T(8,128)(2,1)S(1)}, u32[]{:S(2)}, u32[]{:S(2)}) collective-permute-start(bf16[256,512]{1,0:T(8,128)(2,1)S(1)} %get-tuple-element.354), channel_id=1, source_target_pairs={{0,4},{1,5},{2,6},{3,7},{4,0},{5,1},{6,2},{7,3},{8,20},{9,21},{10,... | collective-permute-start | bytes 786440 | tf_op jit(solution)/shard_map/ppermute | solution.py:30
  136.3 3.4 %shard_map.44.own = bf16[4,256,512]{2,1,0:T(8,128)(2,1)S(1)} custom-call(s32[2]{0:T(128)S(1)} %get-tuple-element.464.flags, bf16[4,4,256,512]{3,2,1,0:T(8,128)(2,1)} %bitcast.42, bf16[4,256,512]{2,1,0:T(8,128)(2,1)S(1)} %shard_map.42.own, bf16[4,256,512]{2,1,0:T(8,128)(2,1)S(1)} %collective-permute-done.14.partner), custom_call_target="tpu_custom_call" | custom-call | flops 1 | bytes 1 | tf_op jit(solution)/shard_map/pallas_call | solution.py:91
  139.7 5.1 %collective-permute-done.17 = bf16[256,512]{1,0:T(8,128)(2,1)S(1)} collective-permute-done((bf16[256,512]{1,0:T(8,128)(2,1)S(1)}, bf16[256,512]{1,0:T(8,128)(2,1)S(1)}, u32[]{:S(2)}, u32[]{:S(2)}) %collective-permute-start.17) | collective-permute-done | bytes 262176 | tf_op jit(solution)/shard_map/ppermute | solution.py:30
  144.8 1.8 collective-permute-done.19
  146.8 1.0 collective-permute-start.15
  147.8 1.7 collective-permute-done.20.partner
  149.4 1.0 copy-done.11
  150.4 3.8 %shard_map.45 = (bf16[256,512]{1,0:T(8,128)(2,1)S(1)}, bf16[256,512]{1,0:T(8,128)(2,1)S(1)}, bf16[256,512]{1,0:T(8,128)(2,1)S(1)}, bf16[256,512]{1,0:T(8,128)(2,1)S(1)}) custom-call(s32[2]{0:T(128)S(1)} %get-tuple-element.462.flags, bf16[4,256,512]{2,1,0:T(8,128)(2,1)S(1)} %pad_maximum_fusion.own, bf16[4,256,512]{2,1,0:T(8,128)(2,1)} %copy-done.11, ...), custom_call_target="tpu_custom_call" | custom-call | flops 1 | bytes 1 | tf_op jit(solution)/shard_map/pallas_call | solution.py:141
  154.2 5.9 %collective-permute-start.23 = (bf16[256,512]{1,0:T(8,128)(2,1)S(1)}, bf16[256,512]{1,0:T(8,128)(2,1)S(1)}, u32[]{:S(2)}, u32[]{:S(2)}) collective-permute-start(bf16[256,512]{1,0:T(8,128)(2,1)S(1)} %get-tuple-element.397), channel_id=1, source_target_pairs={{0,2},{1,3},{2,0},{3,1},{4,6},{5,7},{6,4},{7,5},{8,18},{9,19},{10,... | collective-permute-start | bytes 786440 | tf_op jit(solution)/shard_map/ppermute | solution.py:30
  160.1 5.4 %collective-permute-start.22 = (bf16[256,512]{1,0:T(8,128)(2,1)S(1)}, bf16[256,512]{1,0:T(8,128)(2,1)S(1)}, u32[]{:S(2)}, u32[]{:S(2)}) collective-permute-start(bf16[256,512]{1,0:T(8,128)(2,1)S(1)} %get-tuple-element.396), channel_id=1, source_target_pairs={{0,0},{1,1},{2,2},{3,3},{4,4},{5,5},{6,6},{7,7},{8,16},{9,17},{10,... | collective-permute-start | bytes 786440 | tf_op jit(solution)/shard_map/ppermute | solution.py:30
  165.5 1.4 collective-permute-start.21
  167.0 6.1 %collective-permute-done.15.partner = bf16[4,256,512]{2,1,0:T(8,128)(2,1)S(1)} collective-permute-done((bf16[4,256,512]{2,1,0:T(8,128)(2,1)S(1)}, bf16[4,256,512]{2,1,0:T(8,128)(2,1)S(1)}, u32[]{:S(2)}, u32[]{:S(2)}) %collective-permute-start.15) | collective-permute-done | bytes 1048608 | tf_op jit(solution)/shard_map/ppermute | solution.py:34
  173.1 3.5 %shard_map.46 = (bf16[256,512]{1,0:T(8,128)(2,1)S(1)}, bf16[256,512]{1,0:T(8,128)(2,1)S(1)}, bf16[256,512]{1,0:T(8,128)(2,1)S(1)}, bf16[256,512]{1,0:T(8,128)(2,1)S(1)}) custom-call(s32[2]{0:T(128)S(1)} %get-tuple-element.463.flags, bf16[4,4,256,512]{3,2,1,0:T(8,128)(2,1)} %bitcast.43, bf16[4,256,512]{2,1,0:T(8,128)(2,1)S(1)} %shard_map.44.own, ...), custom_call_target="tpu_custom_call" | custom-call | flops 1 | bytes 1 | tf_op jit(solution)/shard_map/pallas_call | solution.py:91
  176.6 5.4 %collective-permute-start.29 = (bf16[256,512]{1,0:T(8,128)(2,1)S(1)}, bf16[256,512]{1,0:T(8,128)(2,1)S(1)}, u32[]{:S(2)}, u32[]{:S(2)}) collective-permute-start(bf16[256,512]{1,0:T(8,128)(2,1)S(1)} %get-tuple-element.430), channel_id=1, source_target_pairs={{0,4},{1,5},{2,6},{3,7},{4,0},{5,1},{6,2},{7,3},{8,20},{9,21},{10,... | collective-permute-start | bytes 786440 | tf_op jit(solution)/shard_map/ppermute | solution.py:30
  182.0 2.3 collective-permute-start.27
  184.4 5.4 %collective-permute-start.25 = (bf16[256,512]{1,0:T(8,128)(2,1)S(1)}, bf16[256,512]{1,0:T(8,128)(2,1)S(1)}, u32[]{:S(2)}, u32[]{:S(2)}) collective-permute-start(bf16[256,512]{1,0:T(8,128)(2,1)S(1)} %get-tuple-element.411), channel_id=1, source_target_pairs={{0,0},{1,1},{2,2},{3,3},{4,4},{5,5},{6,6},{7,7},{8,16},{9,17},{10,... | collective-permute-start | bytes 786440 | tf_op jit(solution)/shard_map/ppermute | solution.py:30
  189.8 7.4 %collective-permute-done.29 = bf16[256,512]{1,0:T(8,128)(2,1)S(1)} collective-permute-done((bf16[256,512]{1,0:T(8,128)(2,1)S(1)}, bf16[256,512]{1,0:T(8,128)(2,1)S(1)}, u32[]{:S(2)}, u32[]{:S(2)}) %collective-permute-start.29) | collective-permute-done | bytes 262176 | tf_op jit(solution)/shard_map/ppermute | solution.py:30
  197.1 7.0 %collective-permute-done.27 = bf16[256,512]{1,0:T(8,128)(2,1)S(1)} collective-permute-done((bf16[256,512]{1,0:T(8,128)(2,1)S(1)}, bf16[256,512]{1,0:T(8,128)(2,1)S(1)}, u32[]{:S(2)}, u32[]{:S(2)}) %collective-permute-start.27) | collective-permute-done | bytes 262176 | tf_op jit(solution)/shard_map/ppermute | solution.py:30
  204.4 2.6 collective-permute-done.30.partner
  207.0 1.0 copy-done.10
  208.0 4.1 %shard_map.49 = (bf16[256,512]{1,0:T(8,128)(2,1)S(1)}, bf16[256,512]{1,0:T(8,128)(2,1)S(1)}, bf16[256,512]{1,0:T(8,128)(2,1)S(1)}, bf16[256,512]{1,0:T(8,128)(2,1)S(1)}) custom-call(s32[2]{0:T(128)S(1)} %get-tuple-element.462.flags, bf16[4,256,512]{2,1,0:T(8,128)(2,1)S(1)} %pad_maximum_fusion.1.own, bf16[4,256,512]{2,1,0:T(8,128)(2,1)} %copy-done.10, ...), custom_call_target="tpu_custom_call" | custom-call | flops 1 | bytes 1 | tf_op jit(solution)/shard_map/pallas_call | solution.py:141
  212.1 1.7 collective-permute-start.36
  213.8 5.7 %collective-permute-start.35 = (bf16[256,512]{1,0:T(8,128)(2,1)S(1)}, bf16[256,512]{1,0:T(8,128)(2,1)S(1)}, u32[]{:S(2)}, u32[]{:S(2)}) collective-permute-start(bf16[256,512]{1,0:T(8,128)(2,1)S(1)} %get-tuple-element.456), channel_id=1, source_target_pairs={{0,2},{1,3},{2,0},{3,1},{4,6},{5,7},{6,4},{7,5},{8,18},{9,19},{10,... | collective-permute-start | bytes 786440 | tf_op jit(solution)/shard_map/ppermute | solution.py:30
  219.6 5.9 %collective-permute-start.32 = (bf16[256,512]{1,0:T(8,128)(2,1)S(1)}, bf16[256,512]{1,0:T(8,128)(2,1)S(1)}, u32[]{:S(2)}, u32[]{:S(2)}) collective-permute-start(bf16[256,512]{1,0:T(8,128)(2,1)S(1)} %get-tuple-element.452), channel_id=1, source_target_pairs={{0,0},{1,1},{2,2},{3,3},{4,4},{5,5},{6,6},{7,7},{8,16},{9,17},{10,... | collective-permute-start | bytes 786440 | tf_op jit(solution)/shard_map/ppermute | solution.py:30
  225.6 1.5 collective-permute-start.31
  227.2 5.7 %collective-permute-done.35 = bf16[256,512]{1,0:T(8,128)(2,1)S(1)} collective-permute-done((bf16[256,512]{1,0:T(8,128)(2,1)S(1)}, bf16[256,512]{1,0:T(8,128)(2,1)S(1)}, u32[]{:S(2)}, u32[]{:S(2)}) %collective-permute-start.35) | collective-permute-done | bytes 262176 | tf_op jit(solution)/shard_map/ppermute | solution.py:30
  232.9 1.5 collective-permute-start.37
  234.4 4.7 %collective-permute-done.33 = bf16[256,512]{1,0:T(8,128)(2,1)S(1)} collective-permute-done((bf16[256,512]{1,0:T(8,128)(2,1)S(1)}, bf16[256,512]{1,0:T(8,128)(2,1)S(1)}, u32[]{:S(2)}, u32[]{:S(2)}) %collective-permute-start.33) | collective-permute-done | bytes 262176 | tf_op jit(solution)/shard_map/ppermute | solution.py:30
  239.1 1.5 collective-permute-start.34
  240.6 10.3 %collective-permute-done.28.partner = bf16[2,256,512]{2,1,0:T(8,128)(2,1)S(1)} collective-permute-done((bf16[2,256,512]{2,1,0:T(8,128)(2,1)S(1)}, bf16[2,256,512]{2,1,0:T(8,128)(2,1)S(1)}, u32[]{:S(2)}, u32[]{:S(2)}) %collective-permute-start.28) | collective-permute-done | bytes 524320 | tf_op jit(solution)/shard_map/ppermute | solution.py:34
  250.9 1.9 shard_map.47.outs_0_
  252.8 1.9 shard_map.48.outs_0_
  254.7 5.9 %collective-permute-done.37.partner = bf16[2,256,512]{2,1,0:T(8,128)(2,1)S(1)} collective-permute-done((bf16[2,256,512]{2,1,0:T(8,128)(2,1)S(1)}, bf16[2,256,512]{2,1,0:T(8,128)(2,1)S(1)}, u32[]{:S(2)}, u32[]{:S(2)}) %collective-permute-start.37) | collective-permute-done | bytes 524320 | tf_op jit(solution)/shard_map/ppermute | solution.py:34
  260.6 1.9 shard_map.50.outs_0_
  262.5 3.7 %collective-permute-done.34.partner = bf16[2,256,512]{2,1,0:T(8,128)(2,1)S(1)} collective-permute-done((bf16[2,256,512]{2,1,0:T(8,128)(2,1)S(1)}, bf16[2,256,512]{2,1,0:T(8,128)(2,1)S(1)}, u32[]{:S(2)}, u32[]{:S(2)}) %collective-permute-start.34) | collective-permute-done | bytes 524320 | tf_op jit(solution)/shard_map/ppermute | solution.py:34
  266.2 1.9 shard_map.51
  (62 shorter events, 2.3 us)
Async XLA Ops:
  1.4 7.8 %collective-permute-start = (bf16[4,256,512]{2,1,0:T(8,128)(2,1)S(1)}, bf16[4,256,512]{2,1,0:T(8,128)(2,1)S(1)}, u32[]{:S(2)}, u32[]{:S(2)}) collective-permute-start(bf16[4,256,512]{2,1,0:T(8,128)(2,1)S(1)} %slice.6.own), channel_id=1, source_target_pairs={{0,16},{16,0},{32,48},{48,32},{64,80},{80,64},{96,112},{112,96},{1... | collective-permute-start | bytes 3145736 | tf_op jit(solution)/shard_map/ppermute | solution.py:34
  9.2 4.0 %copy-start.3 = (bf16[3,128,512]{2,1,0:T(8,128)(2,1)}, bf16[3,128,512]{2,1,0:T(8,128)(2,1)S(1)}, u32[]{:S(2)}) copy-start(bf16[3,128,512]{2,1,0:T(8,128)(2,1)S(1)} %get-tuple-element.313) | copy-start | bytes 1179652
  9.2 4.0 %copy-start.5 = (bf16[3,128,512]{2,1,0:T(8,128)(2,1)}, bf16[3,128,512]{2,1,0:T(8,128)(2,1)S(1)}, u32[]{:S(2)}) copy-start(bf16[3,128,512]{2,1,0:T(8,128)(2,1)S(1)} %get-tuple-element.314) | copy-start | bytes 1179652
  9.2 4.0 %copy-start.7 = (bf16[3,128,512]{2,1,0:T(8,128)(2,1)}, bf16[3,128,512]{2,1,0:T(8,128)(2,1)S(1)}, u32[]{:S(2)}) copy-start(bf16[3,128,512]{2,1,0:T(8,128)(2,1)S(1)} %get-tuple-element.315) | copy-start | bytes 1179652
  9.2 4.0 %copy-start.9 = (bf16[4,1,1,256,1024]{4,3,2,1,0:T(8,128)(2,1)S(1)}, bf16[4,1,1,256,1024]{4,3,2,1,0:T(8,128)(2,1)}, u32[]{:S(2)}) copy-start(bf16[4,1,1,256,1024]{4,3,2,1,0:T(8,128)(2,1)} %param.3) | copy-start | bytes 6291460
  13.3 8.5 %collective-permute-start.1 = (bf16[4,256,512]{2,1,0:T(8,128)(2,1)S(1)}, bf16[4,256,512]{2,1,0:T(8,128)(2,1)S(1)}, u32[]{:S(2)}, u32[]{:S(2)}) collective-permute-start(bf16[4,256,512]{2,1,0:T(8,128)(2,1)S(1)} %slice.7.own), channel_id=1, source_target_pairs={{0,16},{16,0},{32,48},{48,32},{64,80},{80,64},{96,112},{112,96},{1... | collective-permute-start | bytes 3145736 | tf_op jit(solution)/shard_map/ppermute | solution.py:34
  13.4 26.1 %collective-permute-start.2 = (bf16[4,256,512]{2,1,0:T(8,128)(2,1)S(1)}, bf16[4,256,512]{2,1,0:T(8,128)(2,1)}, u32[]{:S(2)}, u32[]{:S(2)}) collective-permute-start(bf16[4,256,512]{2,1,0:T(8,128)(2,1)S(1)} %shard_map.38.own), channel_id=1, source_target_pairs={{0,32},{16,48},{32,0},{48,16},{64,96},{80,112},{96,64},{112,80},{1... | collective-permute-start | bytes 3145736 | tf_op jit(solution)/shard_map/ppermute | solution.py:34
  14.6 20.6 %collective-permute-start.4 = (bf16[3,128,512]{2,1,0:T(8,128)(2,1)}, bf16[3,128,512]{2,1,0:T(8,128)(2,1)S(1)}, u32[]{:S(2)}, u32[]{:S(2)}) collective-permute-start(bf16[3,128,512]{2,1,0:T(8,128)(2,1)} %get-tuple-element.274), channel_id=1, source_target_pairs={{0,2},{1,3},{2,0},{3,1},{4,6},{5,7},{6,4},{7,5},{8,18},{9,19},{10,... | collective-permute-start | bytes 1179656 | tf_op jit(solution)/shard_map/ppermute | solution.py:30
  21.7 17.8 %collective-permute-start.3 = (bf16[3,128,512]{2,1,0:T(8,128)(2,1)}, bf16[3,128,512]{2,1,0:T(8,128)(2,1)}, u32[]{:S(2)}, u32[]{:S(2)}) collective-permute-start(bf16[3,128,512]{2,1,0:T(8,128)(2,1)} %get-tuple-element.273), channel_id=1, source_target_pairs={{0,6},{1,7},{2,4},{3,5},{4,2},{5,3},{6,0},{7,1},{8,22},{9,23},{10,... | collective-permute-start | bytes 1179656 | tf_op jit(solution)/shard_map/ppermute | solution.py:30
  21.7 1.0 copy-start.1
  22.7 1.2 copy-start.2
  43.1 35.9 %collective-permute-start.6 = (bf16[4,256,512]{2,1,0:T(8,128)(2,1)S(1)}, bf16[4,256,512]{2,1,0:T(8,128)(2,1)}, u32[]{:S(2)}, u32[]{:S(2)}) collective-permute-start(bf16[4,256,512]{2,1,0:T(8,128)(2,1)S(1)} %shard_map.40.own), channel_id=1, source_target_pairs={{0,64},{16,80},{32,96},{48,112},{64,0},{80,16},{96,32},{112,48},{1... | collective-permute-start | bytes 3145736 | tf_op jit(solution)/shard_map/ppermute | solution.py:34
  44.3 27.7 %collective-permute-start.9 = (bf16[3,128,512]{2,1,0:T(8,128)(2,1)}, bf16[3,128,512]{2,1,0:T(8,128)(2,1)S(1)}, u32[]{:S(2)}, u32[]{:S(2)}) collective-permute-start(bf16[3,128,512]{2,1,0:T(8,128)(2,1)} %get-tuple-element.294), channel_id=1, source_target_pairs={{0,0},{1,1},{2,2},{3,3},{4,4},{5,5},{6,6},{7,7},{8,16},{9,17},{10,... | collective-permute-start | bytes 1179656 | tf_op jit(solution)/shard_map/ppermute | solution.py:30
  52.8 25.5 %collective-permute-start.8 = (bf16[3,128,512]{2,1,0:T(8,128)(2,1)}, bf16[3,128,512]{2,1,0:T(8,128)(2,1)S(1)}, u32[]{:S(2)}, u32[]{:S(2)}) collective-permute-start(bf16[3,128,512]{2,1,0:T(8,128)(2,1)} %get-tuple-element.293), channel_id=1, source_target_pairs={{0,4},{1,5},{2,6},{3,7},{4,0},{5,1},{6,2},{7,3},{8,20},{9,21},{10,... | collective-permute-start | bytes 1179656 | tf_op jit(solution)/shard_map/ppermute | solution.py:30
  52.9 26.1 %collective-permute-start.7 = (bf16[3,128,512]{2,1,0:T(8,128)(2,1)}, bf16[3,128,512]{2,1,0:T(8,128)(2,1)}, u32[]{:S(2)}, u32[]{:S(2)}) collective-permute-start(bf16[3,128,512]{2,1,0:T(8,128)(2,1)} %get-tuple-element.292), channel_id=1, source_target_pairs={{0,2},{1,3},{2,0},{3,1},{4,6},{5,7},{6,4},{7,5},{8,18},{9,19},{10,... | collective-permute-start | bytes 1179656 | tf_op jit(solution)/shard_map/ppermute | solution.py:30
  57.3 40.5 %collective-permute-start.5 = (bf16[4,256,512]{2,1,0:T(8,128)(2,1)S(1)}, bf16[4,256,512]{2,1,0:T(8,128)(2,1)S(1)}, u32[]{:S(2)}, u32[]{:S(2)}) collective-permute-start(bf16[4,256,512]{2,1,0:T(8,128)(2,1)S(1)} %shard_map.39.own), channel_id=1, source_target_pairs={{0,32},{16,48},{32,0},{48,16},{64,96},{80,112},{96,64},{112,80},{1... | collective-permute-start | bytes 3145736 | tf_op jit(solution)/shard_map/ppermute | solution.py:34
  79.0 6.2 %copy-start.8 = (bf16[3,128,512]{2,1,0:T(8,128)(2,1)S(1)}, bf16[3,128,512]{2,1,0:T(8,128)(2,1)}, u32[]{:S(2)}) copy-start(bf16[3,128,512]{2,1,0:T(8,128)(2,1)} %copy-done.7) | copy-start | bytes 1179652
  79.0 7.5 %copy-start.6 = (bf16[3,128,512]{2,1,0:T(8,128)(2,1)S(1)}, bf16[3,128,512]{2,1,0:T(8,128)(2,1)}, u32[]{:S(2)}) copy-start(bf16[3,128,512]{2,1,0:T(8,128)(2,1)} %copy-done.5) | copy-start | bytes 1179652
  79.0 12.4 %copy-start.4 = (bf16[3,128,512]{2,1,0:T(8,128)(2,1)S(1)}, bf16[3,128,512]{2,1,0:T(8,128)(2,1)}, u32[]{:S(2)}) copy-start(bf16[3,128,512]{2,1,0:T(8,128)(2,1)} %copy-done.3) | copy-start | bytes 1179652
  82.6 38.6 %collective-permute-start.10 = (bf16[4,256,512]{2,1,0:T(8,128)(2,1)S(1)}, bf16[4,256,512]{2,1,0:T(8,128)(2,1)S(1)}, u32[]{:S(2)}, u32[]{:S(2)}) collective-permute-start(bf16[4,256,512]{2,1,0:T(8,128)(2,1)S(1)} %shard_map.41.own), channel_id=1, source_target_pairs={{0,128},{16,144},{32,160},{48,176},{64,192},{80,208},{96,224},{112... | collective-permute-start | bytes 3145736 | tf_op jit(solution)/shard_map/ppermute | solution.py:34
  85.1 16.1 %collective-permute-start.13 = (bf16[3,128,512]{2,1,0:T(8,128)(2,1)S(1)}, bf16[3,128,512]{2,1,0:T(8,128)(2,1)S(1)}, u32[]{:S(2)}, u32[]{:S(2)}) collective-permute-start(bf16[3,128,512]{2,1,0:T(8,128)(2,1)S(1)} %copy-done.8), channel_id=1, source_target_pairs={{0,6},{1,7},{2,4},{3,5},{4,2},{5,3},{6,0},{7,1},{8,22},{9,23},{10,... | collective-permute-start | bytes 1179656 | tf_op jit(solution)/shard_map/ppermute | solution.py:30
  86.5 17.3 %collective-permute-start.12 = (bf16[3,128,512]{2,1,0:T(8,128)(2,1)S(1)}, bf16[3,128,512]{2,1,0:T(8,128)(2,1)S(1)}, u32[]{:S(2)}, u32[]{:S(2)}) collective-permute-start(bf16[3,128,512]{2,1,0:T(8,128)(2,1)S(1)} %copy-done.6), channel_id=1, source_target_pairs={{0,0},{1,1},{2,2},{3,3},{4,4},{5,5},{6,6},{7,7},{8,16},{9,17},{10,... | collective-permute-start | bytes 1179656 | tf_op jit(solution)/shard_map/ppermute | solution.py:30
  91.4 29.8 %collective-permute-start.11 = (bf16[3,128,512]{2,1,0:T(8,128)(2,1)S(1)}, bf16[3,128,512]{2,1,0:T(8,128)(2,1)S(1)}, u32[]{:S(2)}, u32[]{:S(2)}) collective-permute-start(bf16[3,128,512]{2,1,0:T(8,128)(2,1)S(1)} %copy-done.4), channel_id=1, source_target_pairs={{0,4},{1,5},{2,6},{3,7},{4,0},{5,1},{6,2},{7,3},{8,20},{9,21},{10,... | collective-permute-start | bytes 1179656 | tf_op jit(solution)/shard_map/ppermute | solution.py:30
  121.2 15.1 %collective-permute-start.14 = (bf16[4,256,512]{2,1,0:T(8,128)(2,1)S(1)}, bf16[4,256,512]{2,1,0:T(8,128)(2,1)S(1)}, u32[]{:S(2)}, u32[]{:S(2)}) collective-permute-start(bf16[4,256,512]{2,1,0:T(8,128)(2,1)S(1)} %shard_map.42.own), channel_id=1, source_target_pairs={{0,64},{16,80},{32,96},{48,112},{64,0},{80,16},{96,32},{112,48},{1... | collective-permute-start | bytes 3145736 | tf_op jit(solution)/shard_map/ppermute | solution.py:34
  124.7 15.0 %collective-permute-start.18 = (bf16[256,512]{1,0:T(8,128)(2,1)S(1)}, bf16[256,512]{1,0:T(8,128)(2,1)S(1)}, u32[]{:S(2)}, u32[]{:S(2)}) collective-permute-start(bf16[256,512]{1,0:T(8,128)(2,1)S(1)} %get-tuple-element.348), channel_id=1, source_target_pairs={{0,2},{1,3},{2,0},{3,1},{4,6},{5,7},{6,4},{7,5},{8,18},{9,19},{10,... | collective-permute-start | bytes 786440 | tf_op jit(solution)/shard_map/ppermute | solution.py:30
  124.8 20.0 %collective-permute-start.17 = (bf16[256,512]{1,0:T(8,128)(2,1)S(1)}, bf16[256,512]{1,0:T(8,128)(2,1)S(1)}, u32[]{:S(2)}, u32[]{:S(2)}) collective-permute-start(bf16[256,512]{1,0:T(8,128)(2,1)S(1)} %get-tuple-element.347), channel_id=1, source_target_pairs={{0,6},{1,7},{2,4},{3,5},{4,2},{5,3},{6,0},{7,1},{8,22},{9,23},{10,... | collective-permute-start | bytes 786440 | tf_op jit(solution)/shard_map/ppermute | solution.py:30
  124.9 19.9 %collective-permute-start.16 = (bf16[256,512]{1,0:T(8,128)(2,1)S(1)}, bf16[256,512]{1,0:T(8,128)(2,1)S(1)}, u32[]{:S(2)}, u32[]{:S(2)}) collective-permute-start(bf16[256,512]{1,0:T(8,128)(2,1)S(1)} %get-tuple-element.346), channel_id=1, source_target_pairs={{0,0},{1,1},{2,2},{3,3},{4,4},{5,5},{6,6},{7,7},{8,16},{9,17},{10,... | collective-permute-start | bytes 786440 | tf_op jit(solution)/shard_map/ppermute | solution.py:30
  131.2 15.4 %collective-permute-start.19 = (bf16[256,512]{1,0:T(8,128)(2,1)S(1)}, bf16[256,512]{1,0:T(8,128)(2,1)S(1)}, u32[]{:S(2)}, u32[]{:S(2)}) collective-permute-start(bf16[256,512]{1,0:T(8,128)(2,1)S(1)} %get-tuple-element.354), channel_id=1, source_target_pairs={{0,4},{1,5},{2,6},{3,7},{4,0},{5,1},{6,2},{7,3},{8,20},{9,21},{10,... | collective-permute-start | bytes 786440 | tf_op jit(solution)/shard_map/ppermute | solution.py:30
  146.7 2.7 %collective-permute-start.20 = (bf16[4,256,512]{2,1,0:T(8,128)(2,1)S(1)}, bf16[4,256,512]{2,1,0:T(8,128)(2,1)S(1)}, u32[]{:S(2)}, u32[]{:S(2)}) collective-permute-start(bf16[4,256,512]{2,1,0:T(8,128)(2,1)S(1)} %pad_maximum_fusion.own), channel_id=1, source_target_pairs={{0,16},{16,0},{32,48},{48,32},{64,80},{80,64},{96,112},{112,96},{1... | collective-permute-start | bytes 3145736 | tf_op jit(solution)/shard_map/ppermute | solution.py:34
  146.8 26.3 %collective-permute-start.15 = (bf16[4,256,512]{2,1,0:T(8,128)(2,1)S(1)}, bf16[4,256,512]{2,1,0:T(8,128)(2,1)S(1)}, u32[]{:S(2)}, u32[]{:S(2)}) collective-permute-start(bf16[4,256,512]{2,1,0:T(8,128)(2,1)S(1)} %shard_map.44.own), channel_id=1, source_target_pairs={{0,128},{16,144},{32,160},{48,176},{64,192},{80,208},{96,224},{112... | collective-permute-start | bytes 3145736 | tf_op jit(solution)/shard_map/ppermute | solution.py:34
  149.4 1.0 copy-start.11
  154.2 27.8 %collective-permute-start.23 = (bf16[256,512]{1,0:T(8,128)(2,1)S(1)}, bf16[256,512]{1,0:T(8,128)(2,1)S(1)}, u32[]{:S(2)}, u32[]{:S(2)}) collective-permute-start(bf16[256,512]{1,0:T(8,128)(2,1)S(1)} %get-tuple-element.397), channel_id=1, source_target_pairs={{0,2},{1,3},{2,0},{3,1},{4,6},{5,7},{6,4},{7,5},{8,18},{9,19},{10,... | collective-permute-start | bytes 786440 | tf_op jit(solution)/shard_map/ppermute | solution.py:30
  160.1 21.9 %collective-permute-start.24 = (bf16[256,512]{1,0:T(8,128)(2,1)S(1)}, bf16[256,512]{1,0:T(8,128)(2,1)S(1)}, u32[]{:S(2)}, u32[]{:S(2)}) collective-permute-start(bf16[256,512]{1,0:T(8,128)(2,1)S(1)} %get-tuple-element.400), channel_id=1, source_target_pairs={{0,6},{1,7},{2,4},{3,5},{4,2},{5,3},{6,0},{7,1},{8,22},{9,23},{10,... | collective-permute-start | bytes 786440 | tf_op jit(solution)/shard_map/ppermute | solution.py:30
  160.1 24.3 %collective-permute-start.22 = (bf16[256,512]{1,0:T(8,128)(2,1)S(1)}, bf16[256,512]{1,0:T(8,128)(2,1)S(1)}, u32[]{:S(2)}, u32[]{:S(2)}) collective-permute-start(bf16[256,512]{1,0:T(8,128)(2,1)S(1)} %get-tuple-element.396), channel_id=1, source_target_pairs={{0,0},{1,1},{2,2},{3,3},{4,4},{5,5},{6,6},{7,7},{8,16},{9,17},{10,... | collective-permute-start | bytes 786440 | tf_op jit(solution)/shard_map/ppermute | solution.py:30
  165.5 18.9 %collective-permute-start.21 = (bf16[256,512]{1,0:T(8,128)(2,1)S(1)}, bf16[256,512]{1,0:T(8,128)(2,1)S(1)}, u32[]{:S(2)}, u32[]{:S(2)}) collective-permute-start(bf16[256,512]{1,0:T(8,128)(2,1)S(1)} %get-tuple-element.395), channel_id=1, source_target_pairs={{0,4},{1,5},{2,6},{3,7},{4,0},{5,1},{6,2},{7,3},{8,20},{9,21},{10,... | collective-permute-start | bytes 786440 | tf_op jit(solution)/shard_map/ppermute | solution.py:30
  176.6 20.6 %collective-permute-start.29 = (bf16[256,512]{1,0:T(8,128)(2,1)S(1)}, bf16[256,512]{1,0:T(8,128)(2,1)S(1)}, u32[]{:S(2)}, u32[]{:S(2)}) collective-permute-start(bf16[256,512]{1,0:T(8,128)(2,1)S(1)} %get-tuple-element.430), channel_id=1, source_target_pairs={{0,4},{1,5},{2,6},{3,7},{4,0},{5,1},{6,2},{7,3},{8,20},{9,21},{10,... | collective-permute-start | bytes 786440 | tf_op jit(solution)/shard_map/ppermute | solution.py:30
  182.0 15.1 %collective-permute-start.26 = (bf16[256,512]{1,0:T(8,128)(2,1)S(1)}, bf16[256,512]{1,0:T(8,128)(2,1)S(1)}, u32[]{:S(2)}, u32[]{:S(2)}) collective-permute-start(bf16[256,512]{1,0:T(8,128)(2,1)S(1)} %get-tuple-element.412), channel_id=1, source_target_pairs={{0,6},{1,7},{2,4},{3,5},{4,2},{5,3},{6,0},{7,1},{8,22},{9,23},{10,... | collective-permute-start | bytes 786440 | tf_op jit(solution)/shard_map/ppermute | solution.py:30
  182.0 22.1 %collective-permute-start.27 = (bf16[256,512]{1,0:T(8,128)(2,1)S(1)}, bf16[256,512]{1,0:T(8,128)(2,1)S(1)}, u32[]{:S(2)}, u32[]{:S(2)}) collective-permute-start(bf16[256,512]{1,0:T(8,128)(2,1)S(1)} %get-tuple-element.413), channel_id=1, source_target_pairs={{0,2},{1,3},{2,0},{3,1},{4,6},{5,7},{6,4},{7,5},{8,18},{9,19},{10,... | collective-permute-start | bytes 786440 | tf_op jit(solution)/shard_map/ppermute | solution.py:30
  184.4 19.7 %collective-permute-start.25 = (bf16[256,512]{1,0:T(8,128)(2,1)S(1)}, bf16[256,512]{1,0:T(8,128)(2,1)S(1)}, u32[]{:S(2)}, u32[]{:S(2)}) collective-permute-start(bf16[256,512]{1,0:T(8,128)(2,1)S(1)} %get-tuple-element.411), channel_id=1, source_target_pairs={{0,0},{1,1},{2,2},{3,3},{4,4},{5,5},{6,6},{7,7},{8,16},{9,17},{10,... | collective-permute-start | bytes 786440 | tf_op jit(solution)/shard_map/ppermute | solution.py:30
  204.3 2.7 %collective-permute-start.30 = (bf16[4,256,512]{2,1,0:T(8,128)(2,1)S(1)}, bf16[4,256,512]{2,1,0:T(8,128)(2,1)S(1)}, u32[]{:S(2)}, u32[]{:S(2)}) collective-permute-start(bf16[4,256,512]{2,1,0:T(8,128)(2,1)S(1)} %pad_maximum_fusion.1.own), channel_id=1, source_target_pairs={{0,16},{16,0},{32,48},{48,32},{64,80},{80,64},{96,112},{112,96},{1... | collective-permute-start | bytes 3145736 | tf_op jit(solution)/shard_map/ppermute | solution.py:34
  207.0 1.0 copy-start.10
  208.0 42.9 %copy-start = (bf16[4,4,1,1,256,512]{5,4,3,2,1,0:T(8,128)(2,1)S(1)}, bf16[4,4,1,1,256,512]{5,4,3,2,1,0:T(8,128)(2,1)}, u32[]{:S(2)}) copy-start(bf16[4,4,1,1,256,512]{5,4,3,2,1,0:T(8,128)(2,1)} %param.5) | copy-start | bytes 12582916
  212.1 15.0 %collective-permute-start.36 = (bf16[256,512]{1,0:T(8,128)(2,1)S(1)}, bf16[256,512]{1,0:T(8,128)(2,1)S(1)}, u32[]{:S(2)}, u32[]{:S(2)}) collective-permute-start(bf16[256,512]{1,0:T(8,128)(2,1)S(1)} %get-tuple-element.459), channel_id=1, source_target_pairs={{0,6},{1,7},{2,4},{3,5},{4,2},{5,3},{6,0},{7,1},{8,22},{9,23},{10,... | collective-permute-start | bytes 786440 | tf_op jit(solution)/shard_map/ppermute | solution.py:30
  213.8 19.0 %collective-permute-start.35 = (bf16[256,512]{1,0:T(8,128)(2,1)S(1)}, bf16[256,512]{1,0:T(8,128)(2,1)S(1)}, u32[]{:S(2)}, u32[]{:S(2)}) collective-permute-start(bf16[256,512]{1,0:T(8,128)(2,1)S(1)} %get-tuple-element.456), channel_id=1, source_target_pairs={{0,2},{1,3},{2,0},{3,1},{4,6},{5,7},{6,4},{7,5},{8,18},{9,19},{10,... | collective-permute-start | bytes 786440 | tf_op jit(solution)/shard_map/ppermute | solution.py:30
  219.6 19.5 %collective-permute-start.33 = (bf16[256,512]{1,0:T(8,128)(2,1)S(1)}, bf16[256,512]{1,0:T(8,128)(2,1)S(1)}, u32[]{:S(2)}, u32[]{:S(2)}) collective-permute-start(bf16[256,512]{1,0:T(8,128)(2,1)S(1)} %get-tuple-element.453), channel_id=1, source_target_pairs={{0,4},{1,5},{2,6},{3,7},{4,0},{5,1},{6,2},{7,3},{8,20},{9,21},{10,... | collective-permute-start | bytes 786440 | tf_op jit(solution)/shard_map/ppermute | solution.py:30
  219.6 19.5 %collective-permute-start.32 = (bf16[256,512]{1,0:T(8,128)(2,1)S(1)}, bf16[256,512]{1,0:T(8,128)(2,1)S(1)}, u32[]{:S(2)}, u32[]{:S(2)}) collective-permute-start(bf16[256,512]{1,0:T(8,128)(2,1)S(1)} %get-tuple-element.452), channel_id=1, source_target_pairs={{0,0},{1,1},{2,2},{3,3},{4,4},{5,5},{6,6},{7,7},{8,16},{9,17},{10,... | collective-permute-start | bytes 786440 | tf_op jit(solution)/shard_map/ppermute | solution.py:30
  225.6 27.2 %collective-permute-start.31 = (bf16[2,256,512]{2,1,0:T(8,128)(2,1)S(1)}, bf16[2,256,512]{2,1,0:T(8,128)(2,1)S(1)}, u32[]{:S(2)}, u32[]{:S(2)}) collective-permute-start(bf16[2,256,512]{2,1,0:T(8,128)(2,1)S(1)} %pad_maximum_fusion.5.own), channel_id=1, source_target_pairs={{0,1},{1,0},{2,3},{3,2},{4,5},{5,4},{6,7},{7,6},{8,9},{9,8},{10,11... | collective-permute-start | bytes 1572872 | tf_op jit(solution)/shard_map/ppermute | solution.py:34
  227.1 23.8 %collective-permute-start.28 = (bf16[2,256,512]{2,1,0:T(8,128)(2,1)S(1)}, bf16[2,256,512]{2,1,0:T(8,128)(2,1)S(1)}, u32[]{:S(2)}, u32[]{:S(2)}) collective-permute-start(bf16[2,256,512]{2,1,0:T(8,128)(2,1)S(1)} %pad_maximum_fusion.2.own), channel_id=1, source_target_pairs={{0,1},{1,0},{2,3},{3,2},{4,5},{5,4},{6,7},{7,6},{8,9},{9,8},{10,11... | collective-permute-start | bytes 1572872 | tf_op jit(solution)/shard_map/ppermute | solution.py:34
  232.9 27.7 %collective-permute-start.37 = (bf16[2,256,512]{2,1,0:T(8,128)(2,1)S(1)}, bf16[2,256,512]{2,1,0:T(8,128)(2,1)S(1)}, u32[]{:S(2)}, u32[]{:S(2)}) collective-permute-start(bf16[2,256,512]{2,1,0:T(8,128)(2,1)S(1)} %pad_maximum_fusion.4.own), channel_id=1, source_target_pairs={{0,1},{1,0},{2,3},{3,2},{4,5},{5,4},{6,7},{7,6},{8,9},{9,8},{10,11... | collective-permute-start | bytes 1572872 | tf_op jit(solution)/shard_map/ppermute | solution.py:34
  239.1 27.1 %collective-permute-start.34 = (bf16[2,256,512]{2,1,0:T(8,128)(2,1)S(1)}, bf16[2,256,512]{2,1,0:T(8,128)(2,1)S(1)}, u32[]{:S(2)}, u32[]{:S(2)}) collective-permute-start(bf16[2,256,512]{2,1,0:T(8,128)(2,1)S(1)} %pad_maximum_fusion.3.own), channel_id=1, source_target_pairs={{0,1},{1,0},{2,3},{3,2},{4,5},{5,4},{6,7},{7,6},{8,9},{9,8},{10,11... | collective-permute-start | bytes 1572872 | tf_op jit(solution)/shard_map/ppermute | solution.py:34

commit v2 on v1

v2 whole, which is shorter than its diff:
```python
import functools

import jax
import jax.numpy as jnp
from jax import lax
from jax.experimental import pallas as pl
from jax.experimental.pallas import tpu as pltpu
from jax.sharding import PartitionSpec as P

WIDTHS = (512, 512)
RANK = 256
VMEM = 48 * 2**20


def swap_dest(step):
    pairs = []
    for device in range(256):
        leaf, wide = device >> 4, device & 15
        core, top, low = leaf & 1, wide >> 3, (wide >> 1) & 3
        dest_leaf = (leaf & ~1) | top
        dest_wide = (core << 3) | ((low ^ step) << 1) | (wide & 1)
        pairs.append((device, dest_leaf << 4 | dest_wide))
    return pairs


SWAPS = [swap_dest(step) for step in range(4)]


def swap(value, step):
    return lax.ppermute(value, ("leaf", "wide"), SWAPS[step])


def exchange(value, axis, mask):
    return lax.ppermute(value, axis, [(d, d ^ mask) for d in range(16)])


def dot(a, b):
    return jnp.dot(a, b, preferred_element_type=jnp.float32)


def cross(factor, own, other, high):
    first = pl.multiple_of(high * RANK, RANK)
    second = pl.multiple_of((1 - high) * RANK, RANK)
    total = dot(factor[:, pl.ds(first, RANK)], own) + dot(factor[:, pl.ds(second, RANK)], other)
    return total.astype(jnp.bfloat16)


def level_body(split, flags, factor, own, partner, *outs):
    high = flags[1]
    result = cross(factor.at[0, 0], own[0], partner[0], high)
    if split:
        for place in range(2):
            @pl.when(pl.program_id(0) == place)
            def _():
                outs[place][...] = result
    else:
        outs[-1][0] = result


def cost(n_dots, width, bytes_accessed):
    return pl.CostEstimate(flops=1, bytes_accessed=1, transcendentals=0)


def level_call(factors, level_no, own, partner, flags, width, natural=False, split=False, into=None, column=None, total_width=None, steps=(0, 1, 2, 3)):
    block = (1, RANK, width)
    stride, first = steps[1] - steps[0], steps[0]
    if natural:
        place = lambda t, s: (s[0] ^ (t * stride + first), 0, 0)
    else:
        place = lambda t, s: (t, 0, 0)
    in_specs = [
        pl.BlockSpec((1, 1, RANK, 2 * RANK), lambda t, s: (level_no, s[0] ^ (t * stride + first), 0, 0)),
        pl.BlockSpec(block, place),
        pl.BlockSpec(block, place),
    ]
    operands = [factors, own, partner]
    aliases = {}
    if split:
        out_shape = [jax.ShapeDtypeStruct((RANK, width), jnp.bfloat16)] * 2
        out_specs = [pl.BlockSpec((RANK, width), lambda t, s: (0, 0))] * 2
    elif column is not None:
        out_shape = jax.ShapeDtypeStruct((4, RANK, total_width), jnp.bfloat16)
        out_specs = pl.BlockSpec(block, lambda t, s: (s[0] ^ (t * stride + first), 0, column // width))
        if into is not None:
            in_specs.append(pl.BlockSpec(memory_space=pl.ANY))
            operands.append(into)
            aliases = {4: 0}
    else:
        out_shape = jax.ShapeDtypeStruct((len(steps), RANK, width), jnp.bfloat16)
        out_specs = pl.BlockSpec(block, lambda t, s: (t, 0, 0))
    return pl.pallas_call(
        functools.partial(level_body, split),
        grid_spec=pltpu.PrefetchScalarGridSpec(num_scalar_prefetch=1, grid=(len(steps),), in_specs=in_specs, out_specs=out_specs),
        out_shape=out_shape,
        input_output_aliases=aliases,
        cost_estimate=cost(8, width, 4 * RANK * (3 * width + 2 * RANK) * 2),
        compiler_params=pltpu.CompilerParams(vmem_limit_bytes=VMEM),
    )(flags, *operands)


def take_body(flags, *refs):
    for t in range(4):
        refs[4 + t][0] = refs[t][0, 0]


def take_call(factors, flags):
    block = lambda step: pl.BlockSpec((1, 1, RANK, 2 * RANK), lambda g, s: (g + 1, s[0] ^ step, 0, 0))
    return pl.pallas_call(
        take_body,
        grid_spec=pltpu.PrefetchScalarGridSpec(
            num_scalar_prefetch=1,
            grid=(3,),
            in_specs=[block(t) for t in range(4)],
            out_specs=[pl.BlockSpec((1, RANK, 2 * RANK), lambda g, s: (g, 0, 0))] * 4,
        ),
        out_shape=[jax.ShapeDtypeStruct((3, RANK, 2 * RANK), jnp.bfloat16)] * 4,
        cost_estimate=cost(8, RANK, 1),
        compiler_params=pltpu.CompilerParams(vmem_limit_bytes=VMEM),
    )(flags, *[factors] * 4)


def three_body(flags, own, partner, *refs):
    low, high = flags[0], flags[1]
    factors, outs = refs[:4], refs[4:]
    values = [cross(factors[t].at[2], own[t], partner[t], high) for t in range(4)]
    for bit, row in ((1, 1), (0, 0)):
        apart = 1 << bit
        values = [
            cross(factors[t].at[row], values[t], values[t ^ apart], ((low ^ t) >> bit) & 1) for t in range(4)
        ]
    for t in range(4):
        outs[t][...] = values[t]


def three_call(factors, own, partner, flags, width):
    whole = lambda shape: pl.BlockSpec(shape, lambda g, s: (0,) * len(shape))
    return pl.pallas_call(
        three_body,
        grid_spec=pltpu.PrefetchScalarGridSpec(
            num_scalar_prefetch=1,
            grid=(1,),
            in_specs=[whole((4, RANK, width))] * 2 + [whole((3, RANK, 2 * RANK))] * 4,
            out_specs=[whole((RANK, width))] * 4,
        ),
        out_shape=[jax.ShapeDtypeStruct((RANK, width), jnp.bfloat16)] * 4,
        cost_estimate=cost(24, width, 4 * RANK * (3 * width + 6 * RANK) * 2),
        compiler_params=pltpu.CompilerParams(vmem_limit_bytes=VMEM),
    )(flags, own, partner, *factors)


GROUPS = ((0, 2), (1, 3))


class Order(list):
    def work(self, *name):
        self.append(("work", name))

    def start(self, *name):
        self.append(("start", name))

    def done(self, *name):
        self.append(("done", name))

    def level(self, number, u):
        if number:
            self.done("send", number, u % 2, u // 2)
        self.work("level", number, u % 2, u // 2)

    def send(self, number, u):
        self.start("send", number, u % 2, u // 2)


def order_before():
    o = Order()
    o.work("cut", 0)
    o.start("core", 0)
    o.work("fcut")
    o.work("cut", 1)
    o.start("core", 1)
    o.done("core", 0)
    o.done("core", 1)
    o.start("fsend", 0)
    o.start("fsend", 1)
    o.start("fsend", 2)
    return o


def order_region():
    o = Order()
    o.level(0, 0)
    o.send(1, 0)
    o.level(0, 1)
    o.send(1, 1)
    o.level(0, 2)
    o.level(0, 3)
    o.level(1, 0)
    o.send(2, 0)
    o.level(1, 1)
    o.send(2, 1)
    o.level(2, 0)
    o.send(3, 0)
    o.level(2, 1)
    o.send(1, 2)
    o.done("send", 3, 0, 0)
    o.send(3, 1)
    o.work("level", 3, 0, 0)
    o.level(1, 2)
    o.send(1, 3)
    o.level(3, 1)
    o.level(1, 3)
    return o


def order_after():
    o = Order()
    o.send(2, 2)
    o.send(2, 3)
    o.start("fsend", 3)
    o.start("go", 0, 0)
    o.start("go", 2, 0)
    o.done("fsend", 0)
    o.done("fsend", 1)
    o.done("fsend", 2)
    o.level(2, 2)
    o.send(3, 2)
    o.done("fsend", 3)
    o.start("go", 1, 0)
    o.done("go", 2, 0)
    o.start("go", 3, 0)
    o.level(2, 3)
    o.send(3, 3)
    o.done("go", 0, 0)
    o.level(3, 2)
    o.start("go", 0, 1)
    o.done("go", 1, 0)
    o.start("go", 2, 1)
    o.level(3, 3)
    o.start("go", 1, 1)
    o.done("go", 3, 0)
    o.start("go", 3, 1)
    o.start("acore", 0)
    o.done("acore", 0)
    o.work("three", 0)
    o.done("go", 2, 1)
    o.start("back", 0, 0)
    o.done("go", 0, 1)
    o.start("back", 2, 0)
    o.done("go", 1, 1)
    o.start("back", 1, 0)
    o.done("go", 3, 1)
    o.start("back", 3, 0)
    o.start("acore", 1)
    o.done("back", 2, 0)
    o.done("back", 0, 0)
    o.start("dsend", 0, 0)
    o.done("acore", 1)
    o.work("three", 1)
    o.start("back", 0, 1)
    o.start("back", 2, 1)
    o.done("back", 1, 0)
    o.done("back", 3, 0)
    o.start("dsend", 1, 0)
    o.start("back", 1, 1)
    o.start("back", 3, 1)
    o.done("dsend", 0, 0)
    o.work("last", 0, 0)
    o.done("back", 2, 1)
    o.done("back", 0, 1)
    o.start("dsend", 0, 1)
    o.done("dsend", 1, 0)
    o.work("last", 1, 0)
    o.done("back", 1, 1)
    o.done("back", 3, 1)
    o.start("dsend", 1, 1)
    for h in range(2):
        o.done("dsend", h, 1)
        o.work("last", h, 1)
    return o


def region(function, *operands):
    shapes = jax.eval_shape(function, *operands)
    empty = lambda *_: jax.tree.map(lambda s: jnp.zeros(s.shape, s.dtype), shapes)
    return lax.cond(lax.axis_index("leaf") < 16, function, empty, *operands)


def per_device(source, row_factors, column_factors):
    columns = source.shape[-1]
    source = source.reshape(4, RANK, columns)
    forward = row_factors.reshape(4, 4, RANK, 2 * RANK)
    adjoint = column_factors.reshape(4, 4, RANK, 2 * RANK)
    leaf, wide = lax.axis_index("leaf"), lax.axis_index("wide")
    low = (wide >> 1) & 3
    row_flags = [jnp.stack([low, (leaf >> level) & 1]).astype(jnp.int32) for level in range(4)]
    last_flags = jnp.stack([low, wide & 1]).astype(jnp.int32)
    starts = [sum(WIDTHS[:c]) for c in range(len(WIDTHS))]

    values = {}
    token = last_flags
    output = None

    def tie(value):
        nonlocal token
        value, token = lax.optimization_barrier((value, token))
        return value

    def run(order):
        for action, name in order:
            step(action, name)

    def step(action, name):
        nonlocal output
        kind = name[0]
        if action == "done":
            values[name] = tie(values[name])
        elif action == "work":
            c = name[-1]
            if kind == "fcut":
                values[name] = tie(take_call(adjoint, tie(last_flags)))
            elif kind == "cut":
                block = lax.slice_in_dim(tie(source), starts[c], starts[c] + WIDTHS[c], axis=2)
                values[name] = tie(block)
            elif kind == "level":
                level, g = name[1:3]
                own = values["cut", c] if level == 0 else values["level", level - 1, g, c]
                partner = values["core", c] if level == 0 else values["send", level, g, c]
                result = level_call(
                    forward, level, tie(own), partner, row_flags[level], WIDTHS[c],
                    natural=level == 0, split=level == 3, steps=GROUPS[g],
                )
                values[name] = tie(result)
            elif kind == "three":
                result = three_call(
                    [values["fsend", t] for t in range(4)], tie(values["stack", c]), values["acore", c], row_flags[0], WIDTHS[c],
                )
                values[name] = tie(result)
            elif kind == "last":
                half = name[1]
                output = level_call(
                    adjoint, 0, tie(values["dstack", half, c]), values["dsend", half, c], last_flags, WIDTHS[c],
                    into=output, column=starts[c], total_width=columns, steps=GROUPS[half],
                )
                output = tie(output)
        else:
            c = name[-1]
            if kind == "fsend":
                values[name] = swap(tie(values["fcut",][c]), c)
            elif kind == "core":
                values[name] = exchange(tie(values["cut", c]), "leaf", 1)
            elif kind == "send":
                level, g = name[1:3]
                values[name] = exchange(tie(values["level", level - 1, g, c]), "leaf", 1 << level)
            elif kind == "go":
                g = name[1] % 2
                values[name] = swap(tie(values["level", 3, g, c][GROUPS[g].index(name[1])]), name[1])
            elif kind == "acore":
                values["stack", c] = tie(jnp.stack([values["go", t, c] for t in range(4)]))
                values[name] = exchange(values["stack", c], "leaf", 1)
            elif kind == "back":
                values[name] = swap(tie(values["three", c][name[1]]), name[1])
            elif kind == "dsend":
                half = name[1]
                stack = tie(jnp.stack([values["back", t, c] for t in GROUPS[half]]))
                values["dstack", half, c] = stack
                values[name] = exchange(stack, "wide", 1)
    run(order_before())
    keep = [("level", 3, g, 0) for g in range(2)] + [("level", 1, g, 1) for g in range(2)]

    def body(first):
        nonlocal token
        token = first
        run(order_region())
        return [values[name] for name in keep], token

    kept, token = region(body, token)
    values.update(zip(keep, kept))
    run(order_after())
    return output.reshape(4, 1, 1, RANK, columns)


def solution(mesh):
    return jax.shard_map(
        per_device,
        mesh=mesh,
        in_specs=(
            P(None, "leaf", "wide", None, None),
            P(None, None, "leaf", "wide", None, None),
            P(None, None, "leaf", "wide", None, None),
        ),
        out_specs=P(None, "leaf", "wide", None, None),
        check_vma=False,
    )
```

time: 270 us -> 261 us (0.967)
  Pallas kernels: 48.2 us -> 40.6 us
  waiting for transfers between devices: 113 us -> 119 us
  starting transfers between devices: 100 us -> 96.5 us
    ppermute x14 -> x20, waiting for transfers between devices: 30.3 us -> 70.8 us  [exchange(): return lax.ppermute(value, axis, [(d, d ^ mask) for d in range(16)])]
    ppermute x24 -> x20, waiting for transfers between devices: 82.5 us -> 48.6 us  [swap(): return lax.ppermute(value, ('leaf', 'wide'), SWAPS[step])]
    ppermute x24 -> x20, starting transfers between devices: 83.4 us -> 65.2 us  [swap(): return lax.ppermute(value, ('leaf', 'wide'), SWAPS[step])]
    ppermute x14 -> x20, starting transfers between devices: 17 us -> 31.4 us  [exchange(): return lax.ppermute(value, axis, [(d, d ^ mask) for d in range(16)])]
    pallas_call x12 -> x20, Pallas kernels: 35.9 us -> 29 us  [level_call(): pl.pallas_call(functools.partial(level_body, split), grid_spec=pltpu.Pref...]
  transfers between devices with their start and end apart: 38 -> 40, of which waited for: 19 -> 25; matrix products, arithmetic and copies ran while one was open for 0% -> 0% of each run, Pallas kernels for 13% -> 15%
where the time goes in v2:
time: 261 us
  waiting for transfers between devices  119 us (46%)
  starting transfers between devices  96.5 us (37%)
  Pallas kernels  40.6 us (16%)
  local copies, waits for them, and re-layouts  3.38 us (1%)
    ppermute x20, waiting for transfers between devices, exchange(): return lax.ppermute(value, axis, [(d, d ^ mask) for d in range(16)])  70.8 us
    ppermute x20, starting transfers between devices, swap(): return lax.ppermute(value, ('leaf', 'wide'), SWAPS[step])  65.2 us
    ppermute x20, waiting for transfers between devices, swap(): return lax.ppermute(value, ('leaf', 'wide'), SWAPS[step])  48.6 us
    ppermute x20, starting transfers between devices, exchange(): return lax.ppermute(value, axis, [(d, d ^ mask) for d in range(16)])  31.4 us
    pallas_call x20, Pallas kernels, level_call(): pl.pallas_call(functools.partial(level_body, split), grid_spec=pltpu.Pref...  29 us
    pallas_call x2, Pallas kernels, three_call(): pl.pallas_call(three_body, grid_spec=pltpu.PrefetchScalarGridSpec(num_sca...  7.15 us
  transfers between devices with their start and end apart: 40, of which 25 were waited for; matrix products, arithmetic and copies ran while one was open for 0% of the time, Pallas kernels for 15%

profile of v2, /device:TPU:1, one launch (start us, length us, event | category | flops | bytes accessed | tf_op | source)
XLA Modules:
  0.0 261.1 jit_solution(17512803286023468452)
XLA Ops:
  0.1 1.3 slice.6
  1.4 3.3 %collective-permute-start.9 = (bf16[4,256,512]{2,1,0:T(8,128)(2,1)S(1)}, bf16[4,256,512]{2,1,0:T(8,128)(2,1)S(1)}, u32[]{:S(2)}, u32[]{:S(2)}) collective-permute-start(bf16[4,256,512]{2,1,0:T(8,128)(2,1)S(1)} %slice.6), channel_id=1, source_target_pairs={{0,16},{16,0},{32,48},{48,32},{64,80},{80,64},{96,112},{112,96},{1... | collective-permute-start | bytes 3145736 | tf_op jit(solution)/shard_map/ppermute | solution.py:34
  4.7 4.4 %shard_map.37 = (bf16[3,256,512]{2,1,0:T(8,128)(2,1)}, bf16[3,256,512]{2,1,0:T(8,128)(2,1)}, bf16[3,256,512]{2,1,0:T(8,128)(2,1)S(1)}, bf16[3,256,512]{2,1,0:T(8,128)(2,1)S(1)}) custom-call(s32[2]{0:T(128)S(1)} %get-tuple-element.320.flags, bf16[4,4,256,512]{3,2,1,0:T(8,128)(2,1)} %bitcast.28, bf16[4,4,256,512]{3,2,1,0:T(8,128)(2,1)} %bitcast.29, ...), custom_call_target="tpu_custom_call" | custom-call | flops 1 | bytes 1 | tf_op jit(solution)/shard_map/pallas_call | solution.py:108
  9.7 2.4 collective-permute-done.8
  12.0 4.9 %collective-permute-start.12 = (bf16[3,256,512]{2,1,0:T(8,128)(2,1)}, bf16[3,256,512]{2,1,0:T(8,128)(2,1)S(1)}, u32[]{:S(2)}, u32[]{:S(2)}) collective-permute-start(bf16[3,256,512]{2,1,0:T(8,128)(2,1)} %get-tuple-element.328), channel_id=1, source_target_pairs={{0,2},{1,3},{2,0},{3,1},{4,6},{5,7},{6,4},{7,5},{8,18},{9,19},{10,... | collective-permute-start | bytes 2359304 | tf_op jit(solution)/shard_map/ppermute | solution.py:30
  17.0 3.3 %collective-permute-start.13 = (bf16[3,256,512]{2,1,0:T(8,128)(2,1)}, bf16[3,256,512]{2,1,0:T(8,128)(2,1)S(1)}, u32[]{:S(2)}, u32[]{:S(2)}) collective-permute-start(bf16[3,256,512]{2,1,0:T(8,128)(2,1)} %get-tuple-element.329), channel_id=1, source_target_pairs={{0,0},{1,1},{2,2},{3,3},{4,4},{5,5},{6,6},{7,7},{8,16},{9,17},{10,... | collective-permute-start | bytes 2359304 | tf_op jit(solution)/shard_map/ppermute | solution.py:30
  20.4 3.4 %collective-permute-start.11 = (bf16[3,256,512]{2,1,0:T(8,128)(2,1)}, bf16[3,256,512]{2,1,0:T(8,128)(2,1)S(1)}, u32[]{:S(2)}, u32[]{:S(2)}) collective-permute-start(bf16[3,256,512]{2,1,0:T(8,128)(2,1)} %copy-done.1), channel_id=1, source_target_pairs={{0,4},{1,5},{2,6},{3,7},{4,0},{5,1},{6,2},{7,3},{8,20},{9,21},{10,... | collective-permute-start | bytes 2359304 | tf_op jit(solution)/shard_map/ppermute | solution.py:30
  23.8 69.8 %conditional.1 = (bf16[256,512]{1,0:T(8,128)(2,1)S(1)}, bf16[256,512]{1,0:T(8,128)(2,1)S(1)}, bf16[256,512]{1,0:T(8,128)(2,1)S(1)}, bf16[256,512]{1,0:T(8,128)(2...) conditional(s32[]{:T(128)} %convert_element_type.3, () %tuple.134, ...), branch_computations={%region_0.0_spmd, %region_1.0_spmd} | conditional | flops 12 | bytes 50332180 | solution.py:284
  23.8 2.6 branch_1_fun.12.own
  26.4 3.0 %collective-permute-start = (bf16[2,256,512]{2,1,0:T(8,128)(2,1)S(1)}, bf16[2,256,512]{2,1,0:T(8,128)(2,1)S(1)}, u32[]{:S(2)}, u32[]{:S(2)}) collective-permute-start(bf16[2,256,512]{2,1,0:T(8,128)(2,1)S(1)} %branch_1_fun.12.own), channel_id=1, source_target_pairs={{0,32},{16,48},{32,0},{48,16},{64,96},{80,112},{96,64},{112,80},{1... | collective-permute-start | bytes 1572872 | tf_op jit(solution)/shard_map/cond/branch_1_fun/ppermute | solution.py:34
  33.7 8.3 %collective-permute-done.partner = bf16[2,256,512]{2,1,0:T(8,128)(2,1)S(1)} collective-permute-done((bf16[2,256,512]{2,1,0:T(8,128)(2,1)S(1)}, bf16[2,256,512]{2,1,0:T(8,128)(2,1)S(1)}, u32[]{:S(2)}, u32[]{:S(2)}) %collective-permute-start) | collective-permute-done | bytes 524320 | tf_op jit(solution)/shard_map/cond/branch_1_fun/ppermute | solution.py:34
  43.1 1.3 collective-permute-start.1
  44.4 2.9 %collective-permute-done.2.partner = bf16[2,256,512]{2,1,0:T(8,128)(2,1)S(1)} collective-permute-done((bf16[2,256,512]{2,1,0:T(8,128)(2,1)S(1)}, bf16[2,256,512]{2,1,0:T(8,128)(2,1)S(1)}, u32[]{:S(2)}, u32[]{:S(2)}) %collective-permute-start.2) | collective-permute-done | bytes 524320 | tf_op jit(solution)/shard_map/cond/branch_1_fun/ppermute | solution.py:34
  48.5 1.3 collective-permute-start.3
  49.8 6.5 %collective-permute-done.1.partner = bf16[2,256,512]{2,1,0:T(8,128)(2,1)S(1)} collective-permute-done((bf16[2,256,512]{2,1,0:T(8,128)(2,1)S(1)}, bf16[2,256,512]{2,1,0:T(8,128)(2,1)S(1)}, u32[]{:S(2)}, u32[]{:S(2)}) %collective-permute-start.1) | collective-permute-done | bytes 524320 | tf_op jit(solution)/shard_map/cond/branch_1_fun/ppermute | solution.py:34
  57.5 2.8 %collective-permute-start.4 = (bf16[2,256,512]{2,1,0:T(8,128)(2,1)S(1)}, bf16[2,256,512]{2,1,0:T(8,128)(2,1)S(1)}, u32[]{:S(2)}, u32[]{:S(2)}) collective-permute-start(bf16[2,256,512]{2,1,0:T(8,128)(2,1)S(1)} %branch_1_fun.18.own), channel_id=1, source_target_pairs={{0,128},{16,144},{32,160},{48,176},{64,192},{80,208},{96,224},{112... | collective-permute-start | bytes 1572872 | tf_op jit(solution)/shard_map/cond/branch_1_fun/ppermute | solution.py:34
  60.3 7.2 %collective-permute-done.3.partner = bf16[2,256,512]{2,1,0:T(8,128)(2,1)S(1)} collective-permute-done((bf16[2,256,512]{2,1,0:T(8,128)(2,1)S(1)}, bf16[2,256,512]{2,1,0:T(8,128)(2,1)S(1)}, u32[]{:S(2)}, u32[]{:S(2)}) %collective-permute-start.3) | collective-permute-done | bytes 524320 | tf_op jit(solution)/shard_map/cond/branch_1_fun/ppermute | solution.py:34
  68.7 3.1 %collective-permute-start.6 = (bf16[2,256,512]{2,1,0:T(8,128)(2,1)S(1)}, bf16[2,256,512]{2,1,0:T(8,128)(2,1)S(1)}, u32[]{:S(2)}, u32[]{:S(2)}) collective-permute-start(bf16[2,256,512]{2,1,0:T(8,128)(2,1)S(1)} %branch_1_fun.14.own), channel_id=1, source_target_pairs={{0,32},{16,48},{32,0},{48,16},{64,96},{80,112},{96,64},{112,80},{1... | collective-permute-start | bytes 1572872 | tf_op jit(solution)/shard_map/cond/branch_1_fun/ppermute | solution.py:34
  71.9 4.1 %collective-permute-done.4.partner = bf16[2,256,512]{2,1,0:T(8,128)(2,1)S(1)} collective-permute-done((bf16[2,256,512]{2,1,0:T(8,128)(2,1)S(1)}, bf16[2,256,512]{2,1,0:T(8,128)(2,1)S(1)}, u32[]{:S(2)}, u32[]{:S(2)}) %collective-permute-start.4) | collective-permute-done | bytes 524320 | tf_op jit(solution)/shard_map/cond/branch_1_fun/ppermute | solution.py:34
  75.9 1.2 branch_1_fun.20
  77.1 1.6 collective-permute-done.6.partner
  78.7 2.4 collective-permute-start.5
  82.4 3.3 %collective-permute-start.7 = (bf16[2,256,512]{2,1,0:T(8,128)(2,1)S(1)}, bf16[2,256,512]{2,1,0:T(8,128)(2,1)S(1)}, u32[]{:S(2)}, u32[]{:S(2)}) collective-permute-start(bf16[2,256,512]{2,1,0:T(8,128)(2,1)S(1)} %branch_1_fun.15.own), channel_id=1, source_target_pairs={{0,32},{16,48},{32,0},{48,16},{64,96},{80,112},{96,64},{112,80},{1... | collective-permute-start | bytes 1572872 | tf_op jit(solution)/shard_map/cond/branch_1_fun/ppermute | solution.py:34
  85.7 3.1 %collective-permute-done.5.partner = bf16[2,256,512]{2,1,0:T(8,128)(2,1)S(1)} collective-permute-done((bf16[2,256,512]{2,1,0:T(8,128)(2,1)S(1)}, bf16[2,256,512]{2,1,0:T(8,128)(2,1)S(1)}, u32[]{:S(2)}, u32[]{:S(2)}) %collective-permute-start.5) | collective-permute-done | bytes 524320 | tf_op jit(solution)/shard_map/cond/branch_1_fun/ppermute | solution.py:34
  88.8 1.2 branch_1_fun.22
  90.0 2.4 collective-permute-done.7.partner
  93.6 3.5 %collective-permute-start.18 = (bf16[3,256,512]{2,1,0:T(8,128)(2,1)S(1)}, bf16[3,256,512]{2,1,0:T(8,128)(2,1)S(1)}, u32[]{:S(2)}, u32[]{:S(2)}) collective-permute-start(bf16[3,256,512]{2,1,0:T(8,128)(2,1)S(1)} %get-tuple-element.353), channel_id=1, source_target_pairs={{0,6},{1,7},{2,4},{3,5},{4,2},{5,3},{6,0},{7,1},{8,22},{9,23},{10,... | collective-permute-start | bytes 2359304 | tf_op jit(solution)/shard_map/ppermute | solution.py:30
  99.7 9.7 %collective-permute-done.10.partner = bf16[2,256,512]{2,1,0:T(8,128)(2,1)S(1)} collective-permute-done((bf16[2,256,512]{2,1,0:T(8,128)(2,1)S(1)}, bf16[2,256,512]{2,1,0:T(8,128)(2,1)S(1)}, u32[]{:S(2)}, u32[]{:S(2)}) %collective-permute-start.10) | collective-permute-done | bytes 524320 | tf_op jit(solution)/shard_map/ppermute | solution.py:34
  109.4 2.1 shard_map.38.own
  111.5 6.5 %collective-permute-done.18.refs_3_ = bf16[3,256,512]{2,1,0:T(8,128)(2,1)S(1)} collective-permute-done((bf16[3,256,512]{2,1,0:T(8,128)(2,1)S(1)}, bf16[3,256,512]{2,1,0:T(8,128)(2,1)S(1)}, u32[]{:S(2)}, u32[]{:S(2)}) %collective-permute-start.18) | collective-permute-done | bytes 786464 | tf_op jit(solution)/shard_map/ppermute | solution.py:30
  118.6 1.6 collective-permute-done.17
  121.3 2.7 %collective-permute-start.22 = (bf16[2,256,512]{2,1,0:T(8,128)(2,1)S(1)}, bf16[2,256,512]{2,1,0:T(8,128)(2,1)S(1)}, u32[]{:S(2)}, u32[]{:S(2)}) collective-permute-start(bf16[2,256,512]{2,1,0:T(8,128)(2,1)S(1)} %shard_map.39.own), channel_id=1, source_target_pairs={{0,128},{16,144},{32,160},{48,176},{64,192},{80,208},{96,224},{112... | collective-permute-start | bytes 1572872 | tf_op jit(solution)/shard_map/ppermute | solution.py:34
  124.1 5.0 %collective-permute-start.15 = (bf16[256,512]{1,0:T(8,128)(2,1)S(1)}, bf16[256,512]{1,0:T(8,128)(2,1)S(1)}, u32[]{:S(2)}, u32[]{:S(2)}) collective-permute-start(bf16[256,512]{1,0:T(8,128)(2,1)S(1)} %get-tuple-element.348), channel_id=1, source_target_pairs={{0,0},{1,1},{2,2},{3,3},{4,4},{5,5},{6,6},{7,7},{8,16},{9,17},{10,... | collective-permute-start | bytes 786440 | tf_op jit(solution)/shard_map/ppermute | solution.py:30
  130.3 3.1 %collective-permute-start.21 = (bf16[256,512]{1,0:T(8,128)(2,1)S(1)}, bf16[256,512]{1,0:T(8,128)(2,1)S(1)}, u32[]{:S(2)}, u32[]{:S(2)}) collective-permute-start(bf16[256,512]{1,0:T(8,128)(2,1)S(1)} %get-tuple-element.379), channel_id=1, source_target_pairs={{0,6},{1,7},{2,4},{3,5},{4,2},{5,3},{6,0},{7,1},{8,22},{9,23},{10,... | collective-permute-start | bytes 786440 | tf_op jit(solution)/shard_map/ppermute | solution.py:30
  133.3 5.4 %collective-permute-done.15 = bf16[256,512]{1,0:T(8,128)(2,1)S(1)} collective-permute-done((bf16[256,512]{1,0:T(8,128)(2,1)S(1)}, bf16[256,512]{1,0:T(8,128)(2,1)S(1)}, u32[]{:S(2)}, u32[]{:S(2)}) %collective-permute-start.15) | collective-permute-done | bytes 262176 | tf_op jit(solution)/shard_map/ppermute | solution.py:30
  138.7 1.2 shard_map.40
  139.9 4.5 %collective-permute-done.20 = bf16[256,512]{1,0:T(8,128)(2,1)S(1)} collective-permute-done((bf16[256,512]{1,0:T(8,128)(2,1)S(1)}, bf16[256,512]{1,0:T(8,128)(2,1)S(1)}, u32[]{:S(2)}, u32[]{:S(2)}) %collective-permute-start.20) | collective-permute-done | bytes 262176 | tf_op jit(solution)/shard_map/ppermute | solution.py:30
  144.4 1.2 shard_map.41
  145.6 2.2 collective-permute-done.21
  148.0 3.0 %collective-permute-start.24 = (bf16[256,512]{1,0:T(8,128)(2,1)S(1)}, bf16[256,512]{1,0:T(8,128)(2,1)S(1)}, u32[]{:S(2)}, u32[]{:S(2)}) collective-permute-start(bf16[256,512]{1,0:T(8,128)(2,1)S(1)} %get-tuple-element.413), channel_id=1, source_target_pairs={{0,4},{1,5},{2,6},{3,7},{4,0},{5,1},{6,2},{7,3},{8,20},{9,21},{10,... | collective-permute-start | bytes 786440 | tf_op jit(solution)/shard_map/ppermute | solution.py:30
  151.0 3.5 %collective-permute-start.19 = (bf16[256,512]{1,0:T(8,128)(2,1)S(1)}, bf16[256,512]{1,0:T(8,128)(2,1)S(1)}, u32[]{:S(2)}, u32[]{:S(2)}) collective-permute-start(bf16[256,512]{1,0:T(8,128)(2,1)S(1)} %get-tuple-element.373), channel_id=1, source_target_pairs={{0,0},{1,1},{2,2},{3,3},{4,4},{5,5},{6,6},{7,7},{8,16},{9,17},{10,... | collective-permute-start | bytes 786440 | tf_op jit(solution)/shard_map/ppermute | solution.py:30
  154.5 4.4 %collective-permute-start.25 = (bf16[256,512]{1,0:T(8,128)(2,1)S(1)}, bf16[256,512]{1,0:T(8,128)(2,1)S(1)}, u32[]{:S(2)}, u32[]{:S(2)}) collective-permute-start(bf16[256,512]{1,0:T(8,128)(2,1)S(1)} %get-tuple-element.418), channel_id=1, source_target_pairs={{0,2},{1,3},{2,0},{3,1},{4,6},{5,7},{6,4},{7,5},{8,18},{9,19},{10,... | collective-permute-start | bytes 786440 | tf_op jit(solution)/shard_map/ppermute | solution.py:30
  159.8 3.6 %shard_map.42 = (bf16[256,512]{1,0:T(8,128)(2,1)S(1)}, bf16[256,512]{1,0:T(8,128)(2,1)S(1)}, bf16[256,512]{1,0:T(8,128)(2,1)S(1)}, bf16[256,512]{1,0:T(8,128)(2,1)S(1)}) custom-call(s32[2]{0:T(128)S(1)} %get-tuple-element.479.flags, bf16[4,256,512]{2,1,0:T(8,128)(2,1)S(1)} %pad_maximum_fusion.own, bf16[4,256,512]{2,1,0:T(8,128)(2,1)} %copy-done.14, ...), custom_call_target="tpu_custom_call" | custom-call | flops 1 | bytes 1 | tf_op jit(solution)/shard_map/pallas_call | solution.py:137
  163.4 2.5 collective-permute-done.19
  165.9 10.7 %collective-permute-done.25 = bf16[256,512]{1,0:T(8,128)(2,1)S(1)} collective-permute-done((bf16[256,512]{1,0:T(8,128)(2,1)S(1)}, bf16[256,512]{1,0:T(8,128)(2,1)S(1)}, u32[]{:S(2)}, u32[]{:S(2)}) %collective-permute-start.25) | collective-permute-done | bytes 262176 | tf_op jit(solution)/shard_map/ppermute | solution.py:30
  177.2 3.4 %collective-permute-start.31 = (bf16[256,512]{1,0:T(8,128)(2,1)S(1)}, bf16[256,512]{1,0:T(8,128)(2,1)S(1)}, u32[]{:S(2)}, u32[]{:S(2)}) collective-permute-start(bf16[256,512]{1,0:T(8,128)(2,1)S(1)} %get-tuple-element.457), channel_id=1, source_target_pairs={{0,6},{1,7},{2,4},{3,5},{4,2},{5,3},{6,0},{7,1},{8,22},{9,23},{10,... | collective-permute-start | bytes 786440 | tf_op jit(solution)/shard_map/ppermute | solution.py:30
  180.6 4.3 %collective-permute-start.29 = (bf16[256,512]{1,0:T(8,128)(2,1)S(1)}, bf16[256,512]{1,0:T(8,128)(2,1)S(1)}, u32[]{:S(2)}, u32[]{:S(2)}) collective-permute-start(bf16[256,512]{1,0:T(8,128)(2,1)S(1)} %get-tuple-element.434), channel_id=1, source_target_pairs={{0,4},{1,5},{2,6},{3,7},{4,0},{5,1},{6,2},{7,3},{8,20},{9,21},{10,... | collective-permute-start | bytes 786440 | tf_op jit(solution)/shard_map/ppermute | solution.py:30
  184.9 3.3 %collective-permute-start.28 = (bf16[256,512]{1,0:T(8,128)(2,1)S(1)}, bf16[256,512]{1,0:T(8,128)(2,1)S(1)}, u32[]{:S(2)}, u32[]{:S(2)}) collective-permute-start(bf16[256,512]{1,0:T(8,128)(2,1)S(1)} %get-tuple-element.433), channel_id=1, source_target_pairs={{0,0},{1,1},{2,2},{3,3},{4,4},{5,5},{6,6},{7,7},{8,16},{9,17},{10,... | collective-permute-start | bytes 786440 | tf_op jit(solution)/shard_map/ppermute | solution.py:30
  189.3 3.6 %shard_map.43 = (bf16[256,512]{1,0:T(8,128)(2,1)S(1)}, bf16[256,512]{1,0:T(8,128)(2,1)S(1)}, bf16[256,512]{1,0:T(8,128)(2,1)S(1)}, bf16[256,512]{1,0:T(8,128)(2,1)S(1)}) custom-call(s32[2]{0:T(128)S(1)} %get-tuple-element.479.flags, bf16[4,256,512]{2,1,0:T(8,128)(2,1)S(1)} %pad_maximum_fusion.1.own, bf16[4,256,512]{2,1,0:T(8,128)(2,1)} %copy-done.13, ...), custom_call_target="tpu_custom_call" | custom-call | flops 1 | bytes 1 | tf_op jit(solution)/shard_map/pallas_call | solution.py:137
  192.8 2.8 %collective-permute-start.36 = (bf16[256,512]{1,0:T(8,128)(2,1)S(1)}, bf16[256,512]{1,0:T(8,128)(2,1)S(1)}, u32[]{:S(2)}, u32[]{:S(2)}) collective-permute-start(bf16[256,512]{1,0:T(8,128)(2,1)S(1)} %get-tuple-element.467), channel_id=1, source_target_pairs={{0,4},{1,5},{2,6},{3,7},{4,0},{5,1},{6,2},{7,3},{8,20},{9,21},{10,... | collective-permute-start | bytes 786440 | tf_op jit(solution)/shard_map/ppermute | solution.py:30
  195.7 3.4 %collective-permute-start.35 = (bf16[256,512]{1,0:T(8,128)(2,1)S(1)}, bf16[256,512]{1,0:T(8,128)(2,1)S(1)}, u32[]{:S(2)}, u32[]{:S(2)}) collective-permute-start(bf16[256,512]{1,0:T(8,128)(2,1)S(1)} %get-tuple-element.466), channel_id=1, source_target_pairs={{0,0},{1,1},{2,2},{3,3},{4,4},{5,5},{6,6},{7,7},{8,16},{9,17},{10,... | collective-permute-start | bytes 786440 | tf_op jit(solution)/shard_map/ppermute | solution.py:30
  199.1 2.9 %collective-permute-start.33 = (bf16[256,512]{1,0:T(8,128)(2,1)S(1)}, bf16[256,512]{1,0:T(8,128)(2,1)S(1)}, u32[]{:S(2)}, u32[]{:S(2)}) collective-permute-start(bf16[256,512]{1,0:T(8,128)(2,1)S(1)} %get-tuple-element.465), channel_id=1, source_target_pairs={{0,6},{1,7},{2,4},{3,5},{4,2},{5,3},{6,0},{7,1},{8,22},{9,23},{10,... | collective-permute-start | bytes 786440 | tf_op jit(solution)/shard_map/ppermute | solution.py:30
  202.0 1.5 collective-permute-done.29
  203.5 8.6 %collective-permute-start.32 = (bf16[256,512]{1,0:T(8,128)(2,1)S(1)}, bf16[256,512]{1,0:T(8,128)(2,1)S(1)}, u32[]{:S(2)}, u32[]{:S(2)}) collective-permute-start(bf16[256,512]{1,0:T(8,128)(2,1)S(1)} %get-tuple-element.462), channel_id=1, source_target_pairs={{0,2},{1,3},{2,0},{3,1},{4,6},{5,7},{6,4},{7,5},{8,18},{9,19},{10,... | collective-permute-start | bytes 786440 | tf_op jit(solution)/shard_map/ppermute | solution.py:30
  213.7 2.0 collective-permute-start.39
  216.4 12.7 %collective-permute-done.32 = bf16[256,512]{1,0:T(8,128)(2,1)S(1)} collective-permute-done((bf16[256,512]{1,0:T(8,128)(2,1)S(1)}, bf16[256,512]{1,0:T(8,128)(2,1)S(1)}, u32[]{:S(2)}, u32[]{:S(2)}) %collective-permute-start.32) | collective-permute-done | bytes 262176 | tf_op jit(solution)/shard_map/ppermute | solution.py:30
  229.1 1.6 collective-permute-start.34
  230.7 1.9 shard_map.44.outs_0_
  232.6 5.1 %collective-permute-done.39.partner = bf16[2,256,512]{2,1,0:T(8,128)(2,1)S(1)} collective-permute-done((bf16[2,256,512]{2,1,0:T(8,128)(2,1)S(1)}, bf16[2,256,512]{2,1,0:T(8,128)(2,1)S(1)}, u32[]{:S(2)}, u32[]{:S(2)}) %collective-permute-start.39) | collective-permute-done | bytes 524320 | tf_op jit(solution)/shard_map/ppermute | solution.py:34
  237.7 1.9 shard_map.45.outs_0_
  239.6 9.3 %collective-permute-done.38.partner = bf16[2,256,512]{2,1,0:T(8,128)(2,1)S(1)} collective-permute-done((bf16[2,256,512]{2,1,0:T(8,128)(2,1)S(1)}, bf16[2,256,512]{2,1,0:T(8,128)(2,1)S(1)}, u32[]{:S(2)}, u32[]{:S(2)}) %collective-permute-start.38) | collective-permute-done | bytes 524320 | tf_op jit(solution)/shard_map/ppermute | solution.py:34
  248.9 1.9 shard_map.46.outs_0_
  250.8 8.3 %collective-permute-done.34.partner = bf16[2,256,512]{2,1,0:T(8,128)(2,1)S(1)} collective-permute-done((bf16[2,256,512]{2,1,0:T(8,128)(2,1)S(1)}, bf16[2,256,512]{2,1,0:T(8,128)(2,1)S(1)}, u32[]{:S(2)}, u32[]{:S(2)}) %collective-permute-start.34) | collective-permute-done | bytes 524320 | tf_op jit(solution)/shard_map/ppermute | solution.py:34
  259.2 1.9 shard_map.47
  (82 shorter events, 22.5 us)
Async XLA Ops:
  1.4 7.8 %copy-start.4 = (bf16[4,256,512]{2,1,0:T(8,128)(2,1)}, bf16[4,256,512]{2,1,0:T(8,128)(2,1)S(1)}, u32[]{:S(2)}) copy-start(bf16[4,256,512]{2,1,0:T(8,128)(2,1)S(1)} %slice.6) | copy-start | bytes 3145732
  1.4 8.3 %collective-permute-start.9 = (bf16[4,256,512]{2,1,0:T(8,128)(2,1)S(1)}, bf16[4,256,512]{2,1,0:T(8,128)(2,1)S(1)}, u32[]{:S(2)}, u32[]{:S(2)}) collective-permute-start(bf16[4,256,512]{2,1,0:T(8,128)(2,1)S(1)} %slice.6), channel_id=1, source_target_pairs={{0,16},{16,0},{32,48},{48,32},{64,80},{80,64},{96,112},{112,96},{1... | collective-permute-start | bytes 3145736 | tf_op jit(solution)/shard_map/ppermute | solution.py:34
  4.7 4.4 %copy-start.12 = (bf16[4,1,1,256,1024]{4,3,2,1,0:T(8,128)(2,1)S(1)}, bf16[4,1,1,256,1024]{4,3,2,1,0:T(8,128)(2,1)}, u32[]{:S(2)}) copy-start(bf16[4,1,1,256,1024]{4,3,2,1,0:T(8,128)(2,1)} %param.5) | copy-start | bytes 6291460
  9.2 11.2 %copy-start.1 = (bf16[3,256,512]{2,1,0:T(8,128)(2,1)}, bf16[3,256,512]{2,1,0:T(8,128)(2,1)S(1)}, u32[]{:S(2)}) copy-start(bf16[3,256,512]{2,1,0:T(8,128)(2,1)S(1)} %get-tuple-element.327) | copy-start | bytes 2359300
  9.3 2.8 %copy-start.6 = (bf16[4,256,512]{2,1,0:T(8,128)(2,1)}, bf16[4,256,512]{2,1,0:T(8,128)(2,1)S(1)}, u32[]{:S(2)}) copy-start(bf16[4,256,512]{2,1,0:T(8,128)(2,1)S(1)} %slice.7) | copy-start | bytes 3145732
  9.3 2.7 %collective-permute-start.8 = (bf16[4,256,512]{2,1,0:T(8,128)(2,1)S(1)}, bf16[4,256,512]{2,1,0:T(8,128)(2,1)S(1)}, u32[]{:S(2)}, u32[]{:S(2)}) collective-permute-start(bf16[4,256,512]{2,1,0:T(8,128)(2,1)S(1)} %slice.7), channel_id=1, source_target_pairs={{0,16},{16,0},{32,48},{48,32},{64,80},{80,64},{96,112},{112,96},{1... | collective-permute-start | bytes 3145736 | tf_op jit(solution)/shard_map/ppermute | solution.py:34
  9.7 7.3 %copy-start.8 = (bf16[4,256,512]{2,1,0:T(8,128)(2,1)}, bf16[4,256,512]{2,1,0:T(8,128)(2,1)S(1)}, u32[]{:S(2)}) copy-start(bf16[4,256,512]{2,1,0:T(8,128)(2,1)S(1)} %collective-permute-done.9) | copy-start | bytes 3145732
  12.0 4.9 %copy-start.10 = (bf16[4,256,512]{2,1,0:T(8,128)(2,1)}, bf16[4,256,512]{2,1,0:T(8,128)(2,1)S(1)}, u32[]{:S(2)}) copy-start(bf16[4,256,512]{2,1,0:T(8,128)(2,1)S(1)} %collective-permute-done.8) | copy-start | bytes 3145732
  12.0 85.7 %collective-permute-start.12 = (bf16[3,256,512]{2,1,0:T(8,128)(2,1)}, bf16[3,256,512]{2,1,0:T(8,128)(2,1)S(1)}, u32[]{:S(2)}, u32[]{:S(2)}) collective-permute-start(bf16[3,256,512]{2,1,0:T(8,128)(2,1)} %get-tuple-element.328), channel_id=1, source_target_pairs={{0,2},{1,3},{2,0},{3,1},{4,6},{5,7},{6,4},{7,5},{8,18},{9,19},{10,... | collective-permute-start | bytes 2359304 | tf_op jit(solution)/shard_map/ppermute | solution.py:30
  17.0 81.6 %collective-permute-start.13 = (bf16[3,256,512]{2,1,0:T(8,128)(2,1)}, bf16[3,256,512]{2,1,0:T(8,128)(2,1)S(1)}, u32[]{:S(2)}, u32[]{:S(2)}) collective-permute-start(bf16[3,256,512]{2,1,0:T(8,128)(2,1)} %get-tuple-element.329), channel_id=1, source_target_pairs={{0,0},{1,1},{2,2},{3,3},{4,4},{5,5},{6,6},{7,7},{8,16},{9,17},{10,... | collective-permute-start | bytes 2359304 | tf_op jit(solution)/shard_map/ppermute | solution.py:30
  20.4 79.3 %collective-permute-start.11 = (bf16[3,256,512]{2,1,0:T(8,128)(2,1)}, bf16[3,256,512]{2,1,0:T(8,128)(2,1)S(1)}, u32[]{:S(2)}, u32[]{:S(2)}) collective-permute-start(bf16[3,256,512]{2,1,0:T(8,128)(2,1)} %copy-done.1), channel_id=1, source_target_pairs={{0,4},{1,5},{2,6},{3,7},{4,0},{5,1},{6,2},{7,3},{8,20},{9,21},{10,... | collective-permute-start | bytes 2359304 | tf_op jit(solution)/shard_map/ppermute | solution.py:30
  23.8 5.6 %copy-start.3 = (bf16[4,4,256,512]{3,2,1,0:T(8,128)(2,1)S(1)}, bf16[4,4,256,512]{3,2,1,0:T(8,128)(2,1)}, u32[]{:S(2)}) copy-start(bf16[4,4,256,512]{3,2,1,0:T(8,128)(2,1)} %get-tuple-element.26.factor) | copy-start | bytes 12582916 | tf_op jit(solution)/shard_map/cond
  23.8 5.6 %copy-start.5 = (bf16[4,256,512]{2,1,0:T(8,128)(2,1)S(1)}, bf16[4,256,512]{2,1,0:T(8,128)(2,1)}, u32[]{:S(2)}) copy-start(bf16[4,256,512]{2,1,0:T(8,128)(2,1)} %get-tuple-element.39.own) | copy-start | bytes 3145732 | tf_op jit(solution)/shard_map/cond
  23.8 5.6 %copy-start.9 = (bf16[4,256,512]{2,1,0:T(8,128)(2,1)S(1)}, bf16[4,256,512]{2,1,0:T(8,128)(2,1)}, u32[]{:S(2)}) copy-start(bf16[4,256,512]{2,1,0:T(8,128)(2,1)} %get-tuple-element.33.partner) | copy-start | bytes 3145732 | tf_op jit(solution)/shard_map/cond
  26.4 4.9 %copy-start.7 = (bf16[4,256,512]{2,1,0:T(8,128)(2,1)S(1)}, bf16[4,256,512]{2,1,0:T(8,128)(2,1)}, u32[]{:S(2)}) copy-start(bf16[4,256,512]{2,1,0:T(8,128)(2,1)} %get-tuple-element.46.own) | copy-start | bytes 3145732 | tf_op jit(solution)/shard_map/cond
  26.4 4.9 %copy-start.11 = (bf16[4,256,512]{2,1,0:T(8,128)(2,1)S(1)}, bf16[4,256,512]{2,1,0:T(8,128)(2,1)}, u32[]{:S(2)}) copy-start(bf16[4,256,512]{2,1,0:T(8,128)(2,1)} %get-tuple-element.43.partner) | copy-start | bytes 3145732 | tf_op jit(solution)/shard_map/cond
  26.4 15.5 %collective-permute-start = (bf16[2,256,512]{2,1,0:T(8,128)(2,1)S(1)}, bf16[2,256,512]{2,1,0:T(8,128)(2,1)S(1)}, u32[]{:S(2)}, u32[]{:S(2)}) collective-permute-start(bf16[2,256,512]{2,1,0:T(8,128)(2,1)S(1)} %branch_1_fun.12.own), channel_id=1, source_target_pairs={{0,32},{16,48},{32,0},{48,16},{64,96},{80,112},{96,64},{112,80},{1... | collective-permute-start | bytes 1572872 | tf_op jit(solution)/shard_map/cond/branch_1_fun/ppermute | solution.py:34
  30.6 16.7 %collective-permute-start.2 = (bf16[2,256,512]{2,1,0:T(8,128)(2,1)S(1)}, bf16[2,256,512]{2,1,0:T(8,128)(2,1)S(1)}, u32[]{:S(2)}, u32[]{:S(2)}) collective-permute-start(bf16[2,256,512]{2,1,0:T(8,128)(2,1)S(1)} %branch_1_fun.13.own), channel_id=1, source_target_pairs={{0,32},{16,48},{32,0},{48,16},{64,96},{80,112},{96,64},{112,80},{1... | collective-permute-start | bytes 1572872 | tf_op jit(solution)/shard_map/cond/branch_1_fun/ppermute | solution.py:34
  43.1 13.2 %collective-permute-start.1 = (bf16[2,256,512]{2,1,0:T(8,128)(2,1)S(1)}, bf16[2,256,512]{2,1,0:T(8,128)(2,1)S(1)}, u32[]{:S(2)}, u32[]{:S(2)}) collective-permute-start(bf16[2,256,512]{2,1,0:T(8,128)(2,1)S(1)} %branch_1_fun.16.own), channel_id=1, source_target_pairs={{0,64},{16,80},{32,96},{48,112},{64,0},{80,16},{96,32},{112,48},{1... | collective-permute-start | bytes 1572872 | tf_op jit(solution)/shard_map/cond/branch_1_fun/ppermute | solution.py:34
  48.5 19.1 %collective-permute-start.3 = (bf16[2,256,512]{2,1,0:T(8,128)(2,1)S(1)}, bf16[2,256,512]{2,1,0:T(8,128)(2,1)S(1)}, u32[]{:S(2)}, u32[]{:S(2)}) collective-permute-start(bf16[2,256,512]{2,1,0:T(8,128)(2,1)S(1)} %branch_1_fun.17.own), channel_id=1, source_target_pairs={{0,64},{16,80},{32,96},{48,112},{64,0},{80,16},{96,32},{112,48},{1... | collective-permute-start | bytes 1572872 | tf_op jit(solution)/shard_map/cond/branch_1_fun/ppermute | solution.py:34
  57.5 18.4 %collective-permute-start.4 = (bf16[2,256,512]{2,1,0:T(8,128)(2,1)S(1)}, bf16[2,256,512]{2,1,0:T(8,128)(2,1)S(1)}, u32[]{:S(2)}, u32[]{:S(2)}) collective-permute-start(bf16[2,256,512]{2,1,0:T(8,128)(2,1)S(1)} %branch_1_fun.18.own), channel_id=1, source_target_pairs={{0,128},{16,144},{32,160},{48,176},{64,192},{80,208},{96,224},{112... | collective-permute-start | bytes 1572872 | tf_op jit(solution)/shard_map/cond/branch_1_fun/ppermute | solution.py:34
  68.7 10.0 %collective-permute-start.6 = (bf16[2,256,512]{2,1,0:T(8,128)(2,1)S(1)}, bf16[2,256,512]{2,1,0:T(8,128)(2,1)S(1)}, u32[]{:S(2)}, u32[]{:S(2)}) collective-permute-start(bf16[2,256,512]{2,1,0:T(8,128)(2,1)S(1)} %branch_1_fun.14.own), channel_id=1, source_target_pairs={{0,32},{16,48},{32,0},{48,16},{64,96},{80,112},{96,64},{112,80},{1... | collective-permute-start | bytes 1572872 | tf_op jit(solution)/shard_map/cond/branch_1_fun/ppermute | solution.py:34
  78.7 10.0 %collective-permute-start.5 = (bf16[2,256,512]{2,1,0:T(8,128)(2,1)S(1)}, bf16[2,256,512]{2,1,0:T(8,128)(2,1)S(1)}, u32[]{:S(2)}, u32[]{:S(2)}) collective-permute-start(bf16[2,256,512]{2,1,0:T(8,128)(2,1)S(1)} %branch_1_fun.19.own), channel_id=1, source_target_pairs={{0,128},{16,144},{32,160},{48,176},{64,192},{80,208},{96,224},{112... | collective-permute-start | bytes 1572872 | tf_op jit(solution)/shard_map/cond/branch_1_fun/ppermute | solution.py:34
  82.4 10.1 %collective-permute-start.7 = (bf16[2,256,512]{2,1,0:T(8,128)(2,1)S(1)}, bf16[2,256,512]{2,1,0:T(8,128)(2,1)S(1)}, u32[]{:S(2)}, u32[]{:S(2)}) collective-permute-start(bf16[2,256,512]{2,1,0:T(8,128)(2,1)S(1)} %branch_1_fun.15.own), channel_id=1, source_target_pairs={{0,32},{16,48},{32,0},{48,16},{64,96},{80,112},{96,64},{112,80},{1... | collective-permute-start | bytes 1572872 | tf_op jit(solution)/shard_map/cond/branch_1_fun/ppermute | solution.py:34
  93.6 24.4 %collective-permute-start.18 = (bf16[3,256,512]{2,1,0:T(8,128)(2,1)S(1)}, bf16[3,256,512]{2,1,0:T(8,128)(2,1)S(1)}, u32[]{:S(2)}, u32[]{:S(2)}) collective-permute-start(bf16[3,256,512]{2,1,0:T(8,128)(2,1)S(1)} %get-tuple-element.353), channel_id=1, source_target_pairs={{0,6},{1,7},{2,4},{3,5},{4,2},{5,3},{6,0},{7,1},{8,22},{9,23},{10,... | collective-permute-start | bytes 2359304 | tf_op jit(solution)/shard_map/ppermute | solution.py:30
  97.1 12.3 %collective-permute-start.10 = (bf16[2,256,512]{2,1,0:T(8,128)(2,1)S(1)}, bf16[2,256,512]{2,1,0:T(8,128)(2,1)S(1)}, u32[]{:S(2)}, u32[]{:S(2)}) collective-permute-start(bf16[2,256,512]{2,1,0:T(8,128)(2,1)S(1)} %get-tuple-element.343.own), channel_id=1, source_target_pairs={{0,64},{16,80},{32,96},{48,112},{64,0},{80,16},{96,32},{112,48},{1... | collective-permute-start | bytes 1572872 | tf_op jit(solution)/shard_map/ppermute | solution.py:34
  97.7 22.4 %collective-permute-start.16 = (bf16[2,256,512]{2,1,0:T(8,128)(2,1)S(1)}, bf16[2,256,512]{2,1,0:T(8,128)(2,1)S(1)}, u32[]{:S(2)}, u32[]{:S(2)}) collective-permute-start(bf16[2,256,512]{2,1,0:T(8,128)(2,1)S(1)} %get-tuple-element.360.own), channel_id=1, source_target_pairs={{0,64},{16,80},{32,96},{48,112},{64,0},{80,16},{96,32},{112,48},{1... | collective-permute-start | bytes 1572872 | tf_op jit(solution)/shard_map/ppermute | solution.py:34
  98.6 21.6 %copy-start.2 = (bf16[4,4,1,1,256,512]{5,4,3,2,1,0:T(8,128)(2,1)S(1)}, bf16[4,4,1,1,256,512]{5,4,3,2,1,0:T(8,128)(2,1)}, u32[]{:S(2)}) copy-start(bf16[4,4,1,1,256,512]{5,4,3,2,1,0:T(8,128)(2,1)} %param.6) | copy-start | bytes 12582916
  98.6 21.5 %collective-permute-start.17 = (bf16[256,512]{1,0:T(8,128)(2,1)S(1)}, bf16[256,512]{1,0:T(8,128)(2,1)S(1)}, u32[]{:S(2)}, u32[]{:S(2)}) collective-permute-start(bf16[256,512]{1,0:T(8,128)(2,1)S(1)} %get-tuple-element.351), channel_id=1, source_target_pairs={{0,4},{1,5},{2,6},{3,7},{4,0},{5,1},{6,2},{7,3},{8,20},{9,21},{10,... | collective-permute-start | bytes 786440 | tf_op jit(solution)/shard_map/ppermute | solution.py:30
  118.0 20.7 %collective-permute-start.14 = (bf16[2,256,512]{2,1,0:T(8,128)(2,1)S(1)}, bf16[2,256,512]{2,1,0:T(8,128)(2,1)S(1)}, u32[]{:S(2)}, u32[]{:S(2)}) collective-permute-start(bf16[2,256,512]{2,1,0:T(8,128)(2,1)S(1)} %shard_map.38.own), channel_id=1, source_target_pairs={{0,128},{16,144},{32,160},{48,176},{64,192},{80,208},{96,224},{112... | collective-permute-start | bytes 1572872 | tf_op jit(solution)/shard_map/ppermute | solution.py:34
  121.3 23.0 %collective-permute-start.22 = (bf16[2,256,512]{2,1,0:T(8,128)(2,1)S(1)}, bf16[2,256,512]{2,1,0:T(8,128)(2,1)S(1)}, u32[]{:S(2)}, u32[]{:S(2)}) collective-permute-start(bf16[2,256,512]{2,1,0:T(8,128)(2,1)S(1)} %shard_map.39.own), channel_id=1, source_target_pairs={{0,128},{16,144},{32,160},{48,176},{64,192},{80,208},{96,224},{112... | collective-permute-start | bytes 1572872 | tf_op jit(solution)/shard_map/ppermute | solution.py:34
  124.1 14.6 %collective-permute-start.15 = (bf16[256,512]{1,0:T(8,128)(2,1)S(1)}, bf16[256,512]{1,0:T(8,128)(2,1)S(1)}, u32[]{:S(2)}, u32[]{:S(2)}) collective-permute-start(bf16[256,512]{1,0:T(8,128)(2,1)S(1)} %get-tuple-element.348), channel_id=1, source_target_pairs={{0,0},{1,1},{2,2},{3,3},{4,4},{5,5},{6,6},{7,7},{8,16},{9,17},{10,... | collective-permute-start | bytes 786440 | tf_op jit(solution)/shard_map/ppermute | solution.py:30
  129.1 15.3 %collective-permute-start.20 = (bf16[256,512]{1,0:T(8,128)(2,1)S(1)}, bf16[256,512]{1,0:T(8,128)(2,1)S(1)}, u32[]{:S(2)}, u32[]{:S(2)}) collective-permute-start(bf16[256,512]{1,0:T(8,128)(2,1)S(1)} %get-tuple-element.375), channel_id=1, source_target_pairs={{0,2},{1,3},{2,0},{3,1},{4,6},{5,7},{6,4},{7,5},{8,18},{9,19},{10,... | collective-permute-start | bytes 786440 | tf_op jit(solution)/shard_map/ppermute | solution.py:30
  130.3 17.5 %collective-permute-start.21 = (bf16[256,512]{1,0:T(8,128)(2,1)S(1)}, bf16[256,512]{1,0:T(8,128)(2,1)S(1)}, u32[]{:S(2)}, u32[]{:S(2)}) collective-permute-start(bf16[256,512]{1,0:T(8,128)(2,1)S(1)} %get-tuple-element.379), channel_id=1, source_target_pairs={{0,6},{1,7},{2,4},{3,5},{4,2},{5,3},{6,0},{7,1},{8,22},{9,23},{10,... | collective-permute-start | bytes 786440 | tf_op jit(solution)/shard_map/ppermute | solution.py:30
  147.9 10.9 %collective-permute-start.23 = (bf16[4,256,512]{2,1,0:T(8,128)(2,1)S(1)}, bf16[4,256,512]{2,1,0:T(8,128)(2,1)S(1)}, u32[]{:S(2)}, u32[]{:S(2)}) collective-permute-start(bf16[4,256,512]{2,1,0:T(8,128)(2,1)S(1)} %pad_maximum_fusion.own), channel_id=1, source_target_pairs={{0,16},{16,0},{32,48},{48,32},{64,80},{80,64},{96,112},{112,96},{1... | collective-permute-start | bytes 3145736 | tf_op jit(solution)/shard_map/ppermute | solution.py:34
  148.0 15.4 %collective-permute-start.24 = (bf16[256,512]{1,0:T(8,128)(2,1)S(1)}, bf16[256,512]{1,0:T(8,128)(2,1)S(1)}, u32[]{:S(2)}, u32[]{:S(2)}) collective-permute-start(bf16[256,512]{1,0:T(8,128)(2,1)S(1)} %get-tuple-element.413), channel_id=1, source_target_pairs={{0,4},{1,5},{2,6},{3,7},{4,0},{5,1},{6,2},{7,3},{8,20},{9,21},{10,... | collective-permute-start | bytes 786440 | tf_op jit(solution)/shard_map/ppermute | solution.py:30
  151.0 14.9 %collective-permute-start.19 = (bf16[256,512]{1,0:T(8,128)(2,1)S(1)}, bf16[256,512]{1,0:T(8,128)(2,1)S(1)}, u32[]{:S(2)}, u32[]{:S(2)}) collective-permute-start(bf16[256,512]{1,0:T(8,128)(2,1)S(1)} %get-tuple-element.373), channel_id=1, source_target_pairs={{0,0},{1,1},{2,2},{3,3},{4,4},{5,5},{6,6},{7,7},{8,16},{9,17},{10,... | collective-permute-start | bytes 786440 | tf_op jit(solution)/shard_map/ppermute | solution.py:30
  154.5 22.1 %collective-permute-start.25 = (bf16[256,512]{1,0:T(8,128)(2,1)S(1)}, bf16[256,512]{1,0:T(8,128)(2,1)S(1)}, u32[]{:S(2)}, u32[]{:S(2)}) collective-permute-start(bf16[256,512]{1,0:T(8,128)(2,1)S(1)} %get-tuple-element.418), channel_id=1, source_target_pairs={{0,2},{1,3},{2,0},{3,1},{4,6},{5,7},{6,4},{7,5},{8,18},{9,19},{10,... | collective-permute-start | bytes 786440 | tf_op jit(solution)/shard_map/ppermute | solution.py:30
  158.9 18.1 %collective-permute-start.26 = (bf16[256,512]{1,0:T(8,128)(2,1)S(1)}, bf16[256,512]{1,0:T(8,128)(2,1)S(1)}, u32[]{:S(2)}, u32[]{:S(2)}) collective-permute-start(bf16[256,512]{1,0:T(8,128)(2,1)S(1)} %get-tuple-element.424), channel_id=1, source_target_pairs={{0,6},{1,7},{2,4},{3,5},{4,2},{5,3},{6,0},{7,1},{8,22},{9,23},{10,... | collective-permute-start | bytes 786440 | tf_op jit(solution)/shard_map/ppermute | solution.py:30
  158.9 1.0 copy-start.14
  177.1 11.2 %collective-permute-start.27 = (bf16[4,256,512]{2,1,0:T(8,128)(2,1)S(1)}, bf16[4,256,512]{2,1,0:T(8,128)(2,1)S(1)}, u32[]{:S(2)}, u32[]{:S(2)}) collective-permute-start(bf16[4,256,512]{2,1,0:T(8,128)(2,1)S(1)} %pad_maximum_fusion.1.own), channel_id=1, source_target_pairs={{0,16},{16,0},{32,48},{48,32},{64,80},{80,64},{96,112},{112,96},{1... | collective-permute-start | bytes 3145736 | tf_op jit(solution)/shard_map/ppermute | solution.py:34
  177.2 18.5 %collective-permute-start.31 = (bf16[256,512]{1,0:T(8,128)(2,1)S(1)}, bf16[256,512]{1,0:T(8,128)(2,1)S(1)}, u32[]{:S(2)}, u32[]{:S(2)}) collective-permute-start(bf16[256,512]{1,0:T(8,128)(2,1)S(1)} %get-tuple-element.457), channel_id=1, source_target_pairs={{0,6},{1,7},{2,4},{3,5},{4,2},{5,3},{6,0},{7,1},{8,22},{9,23},{10,... | collective-permute-start | bytes 786440 | tf_op jit(solution)/shard_map/ppermute | solution.py:30
  180.6 18.5 %collective-permute-start.30 = (bf16[256,512]{1,0:T(8,128)(2,1)S(1)}, bf16[256,512]{1,0:T(8,128)(2,1)S(1)}, u32[]{:S(2)}, u32[]{:S(2)}) collective-permute-start(bf16[256,512]{1,0:T(8,128)(2,1)S(1)} %get-tuple-element.450), channel_id=1, source_target_pairs={{0,2},{1,3},{2,0},{3,1},{4,6},{5,7},{6,4},{7,5},{8,18},{9,19},{10,... | collective-permute-start | bytes 786440 | tf_op jit(solution)/shard_map/ppermute | solution.py:30
  180.6 22.9 %collective-permute-start.29 = (bf16[256,512]{1,0:T(8,128)(2,1)S(1)}, bf16[256,512]{1,0:T(8,128)(2,1)S(1)}, u32[]{:S(2)}, u32[]{:S(2)}) collective-permute-start(bf16[256,512]{1,0:T(8,128)(2,1)S(1)} %get-tuple-element.434), channel_id=1, source_target_pairs={{0,4},{1,5},{2,6},{3,7},{4,0},{5,1},{6,2},{7,3},{8,20},{9,21},{10,... | collective-permute-start | bytes 786440 | tf_op jit(solution)/shard_map/ppermute | solution.py:30
  184.9 27.2 %collective-permute-start.28 = (bf16[256,512]{1,0:T(8,128)(2,1)S(1)}, bf16[256,512]{1,0:T(8,128)(2,1)S(1)}, u32[]{:S(2)}, u32[]{:S(2)}) collective-permute-start(bf16[256,512]{1,0:T(8,128)(2,1)S(1)} %get-tuple-element.433), channel_id=1, source_target_pairs={{0,0},{1,1},{2,2},{3,3},{4,4},{5,5},{6,6},{7,7},{8,16},{9,17},{10,... | collective-permute-start | bytes 786440 | tf_op jit(solution)/shard_map/ppermute | solution.py:30
  188.3 1.0 copy-start.13
  192.8 20.8 %collective-permute-start.36 = (bf16[256,512]{1,0:T(8,128)(2,1)S(1)}, bf16[256,512]{1,0:T(8,128)(2,1)S(1)}, u32[]{:S(2)}, u32[]{:S(2)}) collective-permute-start(bf16[256,512]{1,0:T(8,128)(2,1)S(1)} %get-tuple-element.467), channel_id=1, source_target_pairs={{0,4},{1,5},{2,6},{3,7},{4,0},{5,1},{6,2},{7,3},{8,20},{9,21},{10,... | collective-permute-start | bytes 786440 | tf_op jit(solution)/shard_map/ppermute | solution.py:30
  195.7 20.0 %collective-permute-start.35 = (bf16[256,512]{1,0:T(8,128)(2,1)S(1)}, bf16[256,512]{1,0:T(8,128)(2,1)S(1)}, u32[]{:S(2)}, u32[]{:S(2)}) collective-permute-start(bf16[256,512]{1,0:T(8,128)(2,1)S(1)} %get-tuple-element.466), channel_id=1, source_target_pairs={{0,0},{1,1},{2,2},{3,3},{4,4},{5,5},{6,6},{7,7},{8,16},{9,17},{10,... | collective-permute-start | bytes 786440 | tf_op jit(solution)/shard_map/ppermute | solution.py:30
  199.1 17.3 %collective-permute-start.33 = (bf16[256,512]{1,0:T(8,128)(2,1)S(1)}, bf16[256,512]{1,0:T(8,128)(2,1)S(1)}, u32[]{:S(2)}, u32[]{:S(2)}) collective-permute-start(bf16[256,512]{1,0:T(8,128)(2,1)S(1)} %get-tuple-element.465), channel_id=1, source_target_pairs={{0,6},{1,7},{2,4},{3,5},{4,2},{5,3},{6,0},{7,1},{8,22},{9,23},{10,... | collective-permute-start | bytes 786440 | tf_op jit(solution)/shard_map/ppermute | solution.py:30
  203.5 25.6 %collective-permute-start.32 = (bf16[256,512]{1,0:T(8,128)(2,1)S(1)}, bf16[256,512]{1,0:T(8,128)(2,1)S(1)}, u32[]{:S(2)}, u32[]{:S(2)}) collective-permute-start(bf16[256,512]{1,0:T(8,128)(2,1)S(1)} %get-tuple-element.462), channel_id=1, source_target_pairs={{0,2},{1,3},{2,0},{3,1},{4,6},{5,7},{6,4},{7,5},{8,18},{9,19},{10,... | collective-permute-start | bytes 786440 | tf_op jit(solution)/shard_map/ppermute | solution.py:30
  212.1 18.6 %copy-start = (bf16[4,4,1,1,256,512]{5,4,3,2,1,0:T(8,128)(2,1)S(1)}, bf16[4,4,1,1,256,512]{5,4,3,2,1,0:T(8,128)(2,1)}, u32[]{:S(2)}) copy-start(bf16[4,4,1,1,256,512]{5,4,3,2,1,0:T(8,128)(2,1)} %param.7) | copy-start | bytes 12582916
  212.3 18.5 %collective-permute-start.37 = (bf16[2,256,512]{2,1,0:T(8,128)(2,1)S(1)}, bf16[2,256,512]{2,1,0:T(8,128)(2,1)S(1)}, u32[]{:S(2)}, u32[]{:S(2)}) collective-permute-start(bf16[2,256,512]{2,1,0:T(8,128)(2,1)S(1)} %pad_maximum_fusion.5.own), channel_id=1, source_target_pairs={{0,1},{1,0},{2,3},{3,2},{4,5},{5,4},{6,7},{7,6},{8,9},{9,8},{10,11... | collective-permute-start | bytes 1572872 | tf_op jit(solution)/shard_map/ppermute | solution.py:34
  213.7 24.0 %collective-permute-start.39 = (bf16[2,256,512]{2,1,0:T(8,128)(2,1)S(1)}, bf16[2,256,512]{2,1,0:T(8,128)(2,1)S(1)}, u32[]{:S(2)}, u32[]{:S(2)}) collective-permute-start(bf16[2,256,512]{2,1,0:T(8,128)(2,1)S(1)} %pad_maximum_fusion.4.own), channel_id=1, source_target_pairs={{0,1},{1,0},{2,3},{3,2},{4,5},{5,4},{6,7},{7,6},{8,9},{9,8},{10,11... | collective-permute-start | bytes 1572872 | tf_op jit(solution)/shard_map/ppermute | solution.py:34
  215.8 33.1 %collective-permute-start.38 = (bf16[2,256,512]{2,1,0:T(8,128)(2,1)S(1)}, bf16[2,256,512]{2,1,0:T(8,128)(2,1)S(1)}, u32[]{:S(2)}, u32[]{:S(2)}) collective-permute-start(bf16[2,256,512]{2,1,0:T(8,128)(2,1)S(1)} %pad_maximum_fusion.3.own), channel_id=1, source_target_pairs={{0,1},{1,0},{2,3},{3,2},{4,5},{5,4},{6,7},{7,6},{8,9},{9,8},{10,11... | collective-permute-start | bytes 1572872 | tf_op jit(solution)/shard_map/ppermute | solution.py:34
  229.1 30.0 %collective-permute-start.34 = (bf16[2,256,512]{2,1,0:T(8,128)(2,1)S(1)}, bf16[2,256,512]{2,1,0:T(8,128)(2,1)S(1)}, u32[]{:S(2)}, u32[]{:S(2)}) collective-permute-start(bf16[2,256,512]{2,1,0:T(8,128)(2,1)S(1)} %pad_maximum_fusion.2.own), channel_id=1, source_target_pairs={{0,1},{1,0},{2,3},{3,2},{4,5},{5,4},{6,7},{7,6},{8,9},{9,8},{10,11... | collective-permute-start | bytes 1572872 | tf_op jit(solution)/shard_map/ppermute | solution.py:34

commit v3 on v2

--- a/solution.py
+++ b/solution.py
@@ -241,18 +241,18 @@
     o.start("acore", 0)
     o.done("acore", 0)
     o.work("three", 0)
+    o.start("back", 0, 0)
     o.done("go", 2, 1)
-    o.start("back", 0, 0)
+    o.start("back", 2, 0)
     o.done("go", 0, 1)
-    o.start("back", 2, 0)
     o.done("go", 1, 1)
     o.start("back", 1, 0)
     o.done("go", 3, 1)
+    o.done("back", 2, 0)
     o.start("back", 3, 0)
-    o.start("acore", 1)
-    o.done("back", 2, 0)
     o.done("back", 0, 0)
     o.start("dsend", 0, 0)
+    o.start("acore", 1)
     o.done("acore", 1)
     o.work("three", 1)
     o.start("back", 0, 1)

time: 261 us -> 261 us (level)
  no operation moved by 1% of the time
where the time goes in v3:
time: 261 us
  waiting for transfers between devices  119 us (46%)
  starting transfers between devices  96.5 us (37%)
  Pallas kernels  40.6 us (16%)
  local copies, waits for them, and re-layouts  3.38 us (1%)
    ppermute x20, waiting for transfers between devices, exchange(): return lax.ppermute(value, axis, [(d, d ^ mask) for d in range(16)])  70.8 us
    ppermute x20, starting transfers between devices, swap(): return lax.ppermute(value, ('leaf', 'wide'), SWAPS[step])  65.2 us
    ppermute x20, waiting for transfers between devices, swap(): return lax.ppermute(value, ('leaf', 'wide'), SWAPS[step])  48.6 us
    ppermute x20, starting transfers between devices, exchange(): return lax.ppermute(value, axis, [(d, d ^ mask) for d in range(16)])  31.4 us
    pallas_call x20, Pallas kernels, level_call(): pl.pallas_call(functools.partial(level_body, split), grid_spec=pltpu.Pref...  29 us
    pallas_call x2, Pallas kernels, three_call(): pl.pallas_call(three_body, grid_spec=pltpu.PrefetchScalarGridSpec(num_sca...  7.15 us
  transfers between devices with their start and end apart: 40, of which 25 were waited for; matrix products, arithmetic and copies ran while one was open for 0% of the time, Pallas kernels for 15%

profile of v3, /device:TPU:1, one launch (start us, length us, event | category | flops | bytes accessed | tf_op | source)
XLA Modules:
  0.0 261.1 jit_solution(17512803286023468452)
XLA Ops:
  0.1 1.3 slice.6
  1.4 3.3 %collective-permute-start.9 = (bf16[4,256,512]{2,1,0:T(8,128)(2,1)S(1)}, bf16[4,256,512]{2,1,0:T(8,128)(2,1)S(1)}, u32[]{:S(2)}, u32[]{:S(2)}) collective-permute-start(bf16[4,256,512]{2,1,0:T(8,128)(2,1)S(1)} %slice.6), channel_id=1, source_target_pairs={{0,16},{16,0},{32,48},{48,32},{64,80},{80,64},{96,112},{112,96},{1... | collective-permute-start | bytes 3145736 | tf_op jit(solution)/shard_map/ppermute | solution.py:34
  4.7 4.4 %shard_map.37 = (bf16[3,256,512]{2,1,0:T(8,128)(2,1)}, bf16[3,256,512]{2,1,0:T(8,128)(2,1)}, bf16[3,256,512]{2,1,0:T(8,128)(2,1)S(1)}, bf16[3,256,512]{2,1,0:T(8,128)(2,1)S(1)}) custom-call(s32[2]{0:T(128)S(1)} %get-tuple-element.320.flags, bf16[4,4,256,512]{3,2,1,0:T(8,128)(2,1)} %bitcast.28, bf16[4,4,256,512]{3,2,1,0:T(8,128)(2,1)} %bitcast.29, ...), custom_call_target="tpu_custom_call" | custom-call | flops 1 | bytes 1 | tf_op jit(solution)/shard_map/pallas_call | solution.py:108
  9.7 2.4 collective-permute-done.8
  12.0 4.9 %collective-permute-start.12 = (bf16[3,256,512]{2,1,0:T(8,128)(2,1)}, bf16[3,256,512]{2,1,0:T(8,128)(2,1)S(1)}, u32[]{:S(2)}, u32[]{:S(2)}) collective-permute-start(bf16[3,256,512]{2,1,0:T(8,128)(2,1)} %get-tuple-element.328), channel_id=1, source_target_pairs={{0,2},{1,3},{2,0},{3,1},{4,6},{5,7},{6,4},{7,5},{8,18},{9,19},{10,... | collective-permute-start | bytes 2359304 | tf_op jit(solution)/shard_map/ppermute | solution.py:30
  17.0 3.3 %collective-permute-start.13 = (bf16[3,256,512]{2,1,0:T(8,128)(2,1)}, bf16[3,256,512]{2,1,0:T(8,128)(2,1)S(1)}, u32[]{:S(2)}, u32[]{:S(2)}) collective-permute-start(bf16[3,256,512]{2,1,0:T(8,128)(2,1)} %get-tuple-element.329), channel_id=1, source_target_pairs={{0,0},{1,1},{2,2},{3,3},{4,4},{5,5},{6,6},{7,7},{8,16},{9,17},{10,... | collective-permute-start | bytes 2359304 | tf_op jit(solution)/shard_map/ppermute | solution.py:30
  20.4 3.4 %collective-permute-start.11 = (bf16[3,256,512]{2,1,0:T(8,128)(2,1)}, bf16[3,256,512]{2,1,0:T(8,128)(2,1)S(1)}, u32[]{:S(2)}, u32[]{:S(2)}) collective-permute-start(bf16[3,256,512]{2,1,0:T(8,128)(2,1)} %copy-done.1), channel_id=1, source_target_pairs={{0,4},{1,5},{2,6},{3,7},{4,0},{5,1},{6,2},{7,3},{8,20},{9,21},{10,... | collective-permute-start | bytes 2359304 | tf_op jit(solution)/shard_map/ppermute | solution.py:30
  23.8 69.8 %conditional.1 = (bf16[256,512]{1,0:T(8,128)(2,1)S(1)}, bf16[256,512]{1,0:T(8,128)(2,1)S(1)}, bf16[256,512]{1,0:T(8,128)(2,1)S(1)}, bf16[256,512]{1,0:T(8,128)(2...) conditional(s32[]{:T(128)} %convert_element_type.3, () %tuple.134, ...), branch_computations={%region_0.0_spmd, %region_1.0_spmd} | conditional | flops 12 | bytes 50332180 | solution.py:284
  23.8 2.6 branch_1_fun.12.own
  26.4 3.0 %collective-permute-start = (bf16[2,256,512]{2,1,0:T(8,128)(2,1)S(1)}, bf16[2,256,512]{2,1,0:T(8,128)(2,1)S(1)}, u32[]{:S(2)}, u32[]{:S(2)}) collective-permute-start(bf16[2,256,512]{2,1,0:T(8,128)(2,1)S(1)} %branch_1_fun.12.own), channel_id=1, source_target_pairs={{0,32},{16,48},{32,0},{48,16},{64,96},{80,112},{96,64},{112,80},{1... | collective-permute-start | bytes 1572872 | tf_op jit(solution)/shard_map/cond/branch_1_fun/ppermute | solution.py:34
  33.7 8.3 %collective-permute-done.partner = bf16[2,256,512]{2,1,0:T(8,128)(2,1)S(1)} collective-permute-done((bf16[2,256,512]{2,1,0:T(8,128)(2,1)S(1)}, bf16[2,256,512]{2,1,0:T(8,128)(2,1)S(1)}, u32[]{:S(2)}, u32[]{:S(2)}) %collective-permute-start) | collective-permute-done | bytes 524320 | tf_op jit(solution)/shard_map/cond/branch_1_fun/ppermute | solution.py:34
  43.1 1.3 collective-permute-start.1
  44.4 2.9 %collective-permute-done.2.partner = bf16[2,256,512]{2,1,0:T(8,128)(2,1)S(1)} collective-permute-done((bf16[2,256,512]{2,1,0:T(8,128)(2,1)S(1)}, bf16[2,256,512]{2,1,0:T(8,128)(2,1)S(1)}, u32[]{:S(2)}, u32[]{:S(2)}) %collective-permute-start.2) | collective-permute-done | bytes 524320 | tf_op jit(solution)/shard_map/cond/branch_1_fun/ppermute | solution.py:34
  48.5 1.3 collective-permute-start.3
  49.8 6.5 %collective-permute-done.1.partner = bf16[2,256,512]{2,1,0:T(8,128)(2,1)S(1)} collective-permute-done((bf16[2,256,512]{2,1,0:T(8,128)(2,1)S(1)}, bf16[2,256,512]{2,1,0:T(8,128)(2,1)S(1)}, u32[]{:S(2)}, u32[]{:S(2)}) %collective-permute-start.1) | collective-permute-done | bytes 524320 | tf_op jit(solution)/shard_map/cond/branch_1_fun/ppermute | solution.py:34
  57.5 2.8 %collective-permute-start.4 = (bf16[2,256,512]{2,1,0:T(8,128)(2,1)S(1)}, bf16[2,256,512]{2,1,0:T(8,128)(2,1)S(1)}, u32[]{:S(2)}, u32[]{:S(2)}) collective-permute-start(bf16[2,256,512]{2,1,0:T(8,128)(2,1)S(1)} %branch_1_fun.18.own), channel_id=1, source_target_pairs={{0,128},{16,144},{32,160},{48,176},{64,192},{80,208},{96,224},{112... | collective-permute-start | bytes 1572872 | tf_op jit(solution)/shard_map/cond/branch_1_fun/ppermute | solution.py:34
  60.3 7.2 %collective-permute-done.3.partner = bf16[2,256,512]{2,1,0:T(8,128)(2,1)S(1)} collective-permute-done((bf16[2,256,512]{2,1,0:T(8,128)(2,1)S(1)}, bf16[2,256,512]{2,1,0:T(8,128)(2,1)S(1)}, u32[]{:S(2)}, u32[]{:S(2)}) %collective-permute-start.3) | collective-permute-done | bytes 524320 | tf_op jit(solution)/shard_map/cond/branch_1_fun/ppermute | solution.py:34
  68.7 3.1 %collective-permute-start.6 = (bf16[2,256,512]{2,1,0:T(8,128)(2,1)S(1)}, bf16[2,256,512]{2,1,0:T(8,128)(2,1)S(1)}, u32[]{:S(2)}, u32[]{:S(2)}) collective-permute-start(bf16[2,256,512]{2,1,0:T(8,128)(2,1)S(1)} %branch_1_fun.14.own), channel_id=1, source_target_pairs={{0,32},{16,48},{32,0},{48,16},{64,96},{80,112},{96,64},{112,80},{1... | collective-permute-start | bytes 1572872 | tf_op jit(solution)/shard_map/cond/branch_1_fun/ppermute | solution.py:34
  71.9 4.1 %collective-permute-done.4.partner = bf16[2,256,512]{2,1,0:T(8,128)(2,1)S(1)} collective-permute-done((bf16[2,256,512]{2,1,0:T(8,128)(2,1)S(1)}, bf16[2,256,512]{2,1,0:T(8,128)(2,1)S(1)}, u32[]{:S(2)}, u32[]{:S(2)}) %collective-permute-start.4) | collective-permute-done | bytes 524320 | tf_op jit(solution)/shard_map/cond/branch_1_fun/ppermute | solution.py:34
  75.9 1.2 branch_1_fun.20
  77.1 1.6 collective-permute-done.6.partner
  78.7 2.4 collective-permute-start.5
  82.4 3.3 %collective-permute-start.7 = (bf16[2,256,512]{2,1,0:T(8,128)(2,1)S(1)}, bf16[2,256,512]{2,1,0:T(8,128)(2,1)S(1)}, u32[]{:S(2)}, u32[]{:S(2)}) collective-permute-start(bf16[2,256,512]{2,1,0:T(8,128)(2,1)S(1)} %branch_1_fun.15.own), channel_id=1, source_target_pairs={{0,32},{16,48},{32,0},{48,16},{64,96},{80,112},{96,64},{112,80},{1... | collective-permute-start | bytes 1572872 | tf_op jit(solution)/shard_map/cond/branch_1_fun/ppermute | solution.py:34
  85.7 3.1 %collective-permute-done.5.partner = bf16[2,256,512]{2,1,0:T(8,128)(2,1)S(1)} collective-permute-done((bf16[2,256,512]{2,1,0:T(8,128)(2,1)S(1)}, bf16[2,256,512]{2,1,0:T(8,128)(2,1)S(1)}, u32[]{:S(2)}, u32[]{:S(2)}) %collective-permute-start.5) | collective-permute-done | bytes 524320 | tf_op jit(solution)/shard_map/cond/branch_1_fun/ppermute | solution.py:34
  88.8 1.2 branch_1_fun.22
  90.0 2.4 collective-permute-done.7.partner
  93.6 3.5 %collective-permute-start.18 = (bf16[3,256,512]{2,1,0:T(8,128)(2,1)S(1)}, bf16[3,256,512]{2,1,0:T(8,128)(2,1)S(1)}, u32[]{:S(2)}, u32[]{:S(2)}) collective-permute-start(bf16[3,256,512]{2,1,0:T(8,128)(2,1)S(1)} %get-tuple-element.353), channel_id=1, source_target_pairs={{0,6},{1,7},{2,4},{3,5},{4,2},{5,3},{6,0},{7,1},{8,22},{9,23},{10,... | collective-permute-start | bytes 2359304 | tf_op jit(solution)/shard_map/ppermute | solution.py:30
  99.7 9.7 %collective-permute-done.10.partner = bf16[2,256,512]{2,1,0:T(8,128)(2,1)S(1)} collective-permute-done((bf16[2,256,512]{2,1,0:T(8,128)(2,1)S(1)}, bf16[2,256,512]{2,1,0:T(8,128)(2,1)S(1)}, u32[]{:S(2)}, u32[]{:S(2)}) %collective-permute-start.10) | collective-permute-done | bytes 524320 | tf_op jit(solution)/shard_map/ppermute | solution.py:34
  109.4 2.1 shard_map.38.own
  111.5 6.5 %collective-permute-done.18.refs_3_ = bf16[3,256,512]{2,1,0:T(8,128)(2,1)S(1)} collective-permute-done((bf16[3,256,512]{2,1,0:T(8,128)(2,1)S(1)}, bf16[3,256,512]{2,1,0:T(8,128)(2,1)S(1)}, u32[]{:S(2)}, u32[]{:S(2)}) %collective-permute-start.18) | collective-permute-done | bytes 786464 | tf_op jit(solution)/shard_map/ppermute | solution.py:30
  118.6 1.6 collective-permute-done.17
  121.3 2.7 %collective-permute-start.22 = (bf16[2,256,512]{2,1,0:T(8,128)(2,1)S(1)}, bf16[2,256,512]{2,1,0:T(8,128)(2,1)S(1)}, u32[]{:S(2)}, u32[]{:S(2)}) collective-permute-start(bf16[2,256,512]{2,1,0:T(8,128)(2,1)S(1)} %shard_map.39.own), channel_id=1, source_target_pairs={{0,128},{16,144},{32,160},{48,176},{64,192},{80,208},{96,224},{112... | collective-permute-start | bytes 1572872 | tf_op jit(solution)/shard_map/ppermute | solution.py:34
  124.1 5.0 %collective-permute-start.15 = (bf16[256,512]{1,0:T(8,128)(2,1)S(1)}, bf16[256,512]{1,0:T(8,128)(2,1)S(1)}, u32[]{:S(2)}, u32[]{:S(2)}) collective-permute-start(bf16[256,512]{1,0:T(8,128)(2,1)S(1)} %get-tuple-element.348), channel_id=1, source_target_pairs={{0,0},{1,1},{2,2},{3,3},{4,4},{5,5},{6,6},{7,7},{8,16},{9,17},{10,... | collective-permute-start | bytes 786440 | tf_op jit(solution)/shard_map/ppermute | solution.py:30
  130.3 3.1 %collective-permute-start.21 = (bf16[256,512]{1,0:T(8,128)(2,1)S(1)}, bf16[256,512]{1,0:T(8,128)(2,1)S(1)}, u32[]{:S(2)}, u32[]{:S(2)}) collective-permute-start(bf16[256,512]{1,0:T(8,128)(2,1)S(1)} %get-tuple-element.379), channel_id=1, source_target_pairs={{0,6},{1,7},{2,4},{3,5},{4,2},{5,3},{6,0},{7,1},{8,22},{9,23},{10,... | collective-permute-start | bytes 786440 | tf_op jit(solution)/shard_map/ppermute | solution.py:30
  133.3 5.4 %collective-permute-done.15 = bf16[256,512]{1,0:T(8,128)(2,1)S(1)} collective-permute-done((bf16[256,512]{1,0:T(8,128)(2,1)S(1)}, bf16[256,512]{1,0:T(8,128)(2,1)S(1)}, u32[]{:S(2)}, u32[]{:S(2)}) %collective-permute-start.15) | collective-permute-done | bytes 262176 | tf_op jit(solution)/shard_map/ppermute | solution.py:30
  138.7 1.2 shard_map.40
  139.9 4.5 %collective-permute-done.20 = bf16[256,512]{1,0:T(8,128)(2,1)S(1)} collective-permute-done((bf16[256,512]{1,0:T(8,128)(2,1)S(1)}, bf16[256,512]{1,0:T(8,128)(2,1)S(1)}, u32[]{:S(2)}, u32[]{:S(2)}) %collective-permute-start.20) | collective-permute-done | bytes 262176 | tf_op jit(solution)/shard_map/ppermute | solution.py:30
  144.4 1.2 shard_map.41
  145.6 2.2 collective-permute-done.21
  148.0 3.0 %collective-permute-start.24 = (bf16[256,512]{1,0:T(8,128)(2,1)S(1)}, bf16[256,512]{1,0:T(8,128)(2,1)S(1)}, u32[]{:S(2)}, u32[]{:S(2)}) collective-permute-start(bf16[256,512]{1,0:T(8,128)(2,1)S(1)} %get-tuple-element.413), channel_id=1, source_target_pairs={{0,4},{1,5},{2,6},{3,7},{4,0},{5,1},{6,2},{7,3},{8,20},{9,21},{10,... | collective-permute-start | bytes 786440 | tf_op jit(solution)/shard_map/ppermute | solution.py:30
  151.0 3.5 %collective-permute-start.19 = (bf16[256,512]{1,0:T(8,128)(2,1)S(1)}, bf16[256,512]{1,0:T(8,128)(2,1)S(1)}, u32[]{:S(2)}, u32[]{:S(2)}) collective-permute-start(bf16[256,512]{1,0:T(8,128)(2,1)S(1)} %get-tuple-element.373), channel_id=1, source_target_pairs={{0,0},{1,1},{2,2},{3,3},{4,4},{5,5},{6,6},{7,7},{8,16},{9,17},{10,... | collective-permute-start | bytes 786440 | tf_op jit(solution)/shard_map/ppermute | solution.py:30
  154.5 4.4 %collective-permute-start.25 = (bf16[256,512]{1,0:T(8,128)(2,1)S(1)}, bf16[256,512]{1,0:T(8,128)(2,1)S(1)}, u32[]{:S(2)}, u32[]{:S(2)}) collective-permute-start(bf16[256,512]{1,0:T(8,128)(2,1)S(1)} %get-tuple-element.420), channel_id=1, source_target_pairs={{0,2},{1,3},{2,0},{3,1},{4,6},{5,7},{6,4},{7,5},{8,18},{9,19},{10,... | collective-permute-start | bytes 786440 | tf_op jit(solution)/shard_map/ppermute | solution.py:30
  159.8 3.6 %shard_map.42 = (bf16[256,512]{1,0:T(8,128)(2,1)S(1)}, bf16[256,512]{1,0:T(8,128)(2,1)S(1)}, bf16[256,512]{1,0:T(8,128)(2,1)S(1)}, bf16[256,512]{1,0:T(8,128)(2,1)S(1)}) custom-call(s32[2]{0:T(128)S(1)} %get-tuple-element.479.flags, bf16[4,256,512]{2,1,0:T(8,128)(2,1)S(1)} %pad_maximum_fusion.own, bf16[4,256,512]{2,1,0:T(8,128)(2,1)} %copy-done.14, ...), custom_call_target="tpu_custom_call" | custom-call | flops 1 | bytes 1 | tf_op jit(solution)/shard_map/pallas_call | solution.py:137
  163.4 2.5 collective-permute-done.19
  165.9 10.7 %collective-permute-done.25 = bf16[256,512]{1,0:T(8,128)(2,1)S(1)} collective-permute-done((bf16[256,512]{1,0:T(8,128)(2,1)S(1)}, bf16[256,512]{1,0:T(8,128)(2,1)S(1)}, u32[]{:S(2)}, u32[]{:S(2)}) %collective-permute-start.25) | collective-permute-done | bytes 262176 | tf_op jit(solution)/shard_map/ppermute | solution.py:30
  177.2 3.4 %collective-permute-start.31 = (bf16[256,512]{1,0:T(8,128)(2,1)S(1)}, bf16[256,512]{1,0:T(8,128)(2,1)S(1)}, u32[]{:S(2)}, u32[]{:S(2)}) collective-permute-start(bf16[256,512]{1,0:T(8,128)(2,1)S(1)} %get-tuple-element.457), channel_id=1, source_target_pairs={{0,6},{1,7},{2,4},{3,5},{4,2},{5,3},{6,0},{7,1},{8,22},{9,23},{10,... | collective-permute-start | bytes 786440 | tf_op jit(solution)/shard_map/ppermute | solution.py:30
  180.6 4.3 %collective-permute-start.28 = (bf16[256,512]{1,0:T(8,128)(2,1)S(1)}, bf16[256,512]{1,0:T(8,128)(2,1)S(1)}, u32[]{:S(2)}, u32[]{:S(2)}) collective-permute-start(bf16[256,512]{1,0:T(8,128)(2,1)S(1)} %get-tuple-element.431), channel_id=1, source_target_pairs={{0,4},{1,5},{2,6},{3,7},{4,0},{5,1},{6,2},{7,3},{8,20},{9,21},{10,... | collective-permute-start | bytes 786440 | tf_op jit(solution)/shard_map/ppermute | solution.py:30
  184.9 3.3 %collective-permute-start.27 = (bf16[256,512]{1,0:T(8,128)(2,1)S(1)}, bf16[256,512]{1,0:T(8,128)(2,1)S(1)}, u32[]{:S(2)}, u32[]{:S(2)}) collective-permute-start(bf16[256,512]{1,0:T(8,128)(2,1)S(1)} %get-tuple-element.429), channel_id=1, source_target_pairs={{0,0},{1,1},{2,2},{3,3},{4,4},{5,5},{6,6},{7,7},{8,16},{9,17},{10,... | collective-permute-start | bytes 786440 | tf_op jit(solution)/shard_map/ppermute | solution.py:30
  189.3 3.6 %shard_map.43 = (bf16[256,512]{1,0:T(8,128)(2,1)S(1)}, bf16[256,512]{1,0:T(8,128)(2,1)S(1)}, bf16[256,512]{1,0:T(8,128)(2,1)S(1)}, bf16[256,512]{1,0:T(8,128)(2,1)S(1)}) custom-call(s32[2]{0:T(128)S(1)} %get-tuple-element.479.flags, bf16[4,256,512]{2,1,0:T(8,128)(2,1)S(1)} %pad_maximum_fusion.1.own, bf16[4,256,512]{2,1,0:T(8,128)(2,1)} %copy-done.13, ...), custom_call_target="tpu_custom_call" | custom-call | flops 1 | bytes 1 | tf_op jit(solution)/shard_map/pallas_call | solution.py:137
  192.8 2.8 %collective-permute-start.36 = (bf16[256,512]{1,0:T(8,128)(2,1)S(1)}, bf16[256,512]{1,0:T(8,128)(2,1)S(1)}, u32[]{:S(2)}, u32[]{:S(2)}) collective-permute-start(bf16[256,512]{1,0:T(8,128)(2,1)S(1)} %get-tuple-element.467), channel_id=1, source_target_pairs={{0,4},{1,5},{2,6},{3,7},{4,0},{5,1},{6,2},{7,3},{8,20},{9,21},{10,... | collective-permute-start | bytes 786440 | tf_op jit(solution)/shard_map/ppermute | solution.py:30
  195.7 3.4 %collective-permute-start.35 = (bf16[256,512]{1,0:T(8,128)(2,1)S(1)}, bf16[256,512]{1,0:T(8,128)(2,1)S(1)}, u32[]{:S(2)}, u32[]{:S(2)}) collective-permute-start(bf16[256,512]{1,0:T(8,128)(2,1)S(1)} %get-tuple-element.466), channel_id=1, source_target_pairs={{0,0},{1,1},{2,2},{3,3},{4,4},{5,5},{6,6},{7,7},{8,16},{9,17},{10,... | collective-permute-start | bytes 786440 | tf_op jit(solution)/shard_map/ppermute | solution.py:30
  199.1 2.9 %collective-permute-start.33 = (bf16[256,512]{1,0:T(8,128)(2,1)S(1)}, bf16[256,512]{1,0:T(8,128)(2,1)S(1)}, u32[]{:S(2)}, u32[]{:S(2)}) collective-permute-start(bf16[256,512]{1,0:T(8,128)(2,1)S(1)} %get-tuple-element.465), channel_id=1, source_target_pairs={{0,6},{1,7},{2,4},{3,5},{4,2},{5,3},{6,0},{7,1},{8,22},{9,23},{10,... | collective-permute-start | bytes 786440 | tf_op jit(solution)/shard_map/ppermute | solution.py:30
  202.0 1.5 collective-permute-done.28
  203.5 8.6 %collective-permute-start.32 = (bf16[256,512]{1,0:T(8,128)(2,1)S(1)}, bf16[256,512]{1,0:T(8,128)(2,1)S(1)}, u32[]{:S(2)}, u32[]{:S(2)}) collective-permute-start(bf16[256,512]{1,0:T(8,128)(2,1)S(1)} %get-tuple-element.462), channel_id=1, source_target_pairs={{0,2},{1,3},{2,0},{3,1},{4,6},{5,7},{6,4},{7,5},{8,18},{9,19},{10,... | collective-permute-start | bytes 786440 | tf_op jit(solution)/shard_map/ppermute | solution.py:30
  213.7 2.0 collective-permute-start.39
  216.4 12.7 %collective-permute-done.32 = bf16[256,512]{1,0:T(8,128)(2,1)S(1)} collective-permute-done((bf16[256,512]{1,0:T(8,128)(2,1)S(1)}, bf16[256,512]{1,0:T(8,128)(2,1)S(1)}, u32[]{:S(2)}, u32[]{:S(2)}) %collective-permute-start.32) | collective-permute-done | bytes 262176 | tf_op jit(solution)/shard_map/ppermute | solution.py:30
  229.1 1.6 collective-permute-start.34
  230.7 1.9 shard_map.44.outs_0_
  232.6 5.1 %collective-permute-done.39.partner = bf16[2,256,512]{2,1,0:T(8,128)(2,1)S(1)} collective-permute-done((bf16[2,256,512]{2,1,0:T(8,128)(2,1)S(1)}, bf16[2,256,512]{2,1,0:T(8,128)(2,1)S(1)}, u32[]{:S(2)}, u32[]{:S(2)}) %collective-permute-start.39) | collective-permute-done | bytes 524320 | tf_op jit(solution)/shard_map/ppermute | solution.py:34
  237.7 1.9 shard_map.45.outs_0_
  239.6 9.3 %collective-permute-done.38.partner = bf16[2,256,512]{2,1,0:T(8,128)(2,1)S(1)} collective-permute-done((bf16[2,256,512]{2,1,0:T(8,128)(2,1)S(1)}, bf16[2,256,512]{2,1,0:T(8,128)(2,1)S(1)}, u32[]{:S(2)}, u32[]{:S(2)}) %collective-permute-start.38) | collective-permute-done | bytes 524320 | tf_op jit(solution)/shard_map/ppermute | solution.py:34
  248.9 1.9 shard_map.46.outs_0_
  250.8 8.3 %collective-permute-done.34.partner = bf16[2,256,512]{2,1,0:T(8,128)(2,1)S(1)} collective-permute-done((bf16[2,256,512]{2,1,0:T(8,128)(2,1)S(1)}, bf16[2,256,512]{2,1,0:T(8,128)(2,1)S(1)}, u32[]{:S(2)}, u32[]{:S(2)}) %collective-permute-start.34) | collective-permute-done | bytes 524320 | tf_op jit(solution)/shard_map/ppermute | solution.py:34
  259.2 1.9 shard_map.47
  (82 shorter events, 22.5 us)
Async XLA Ops:
  1.4 7.8 %copy-start.4 = (bf16[4,256,512]{2,1,0:T(8,128)(2,1)}, bf16[4,256,512]{2,1,0:T(8,128)(2,1)S(1)}, u32[]{:S(2)}) copy-start(bf16[4,256,512]{2,1,0:T(8,128)(2,1)S(1)} %slice.6) | copy-start | bytes 3145732
  1.4 8.3 %collective-permute-start.9 = (bf16[4,256,512]{2,1,0:T(8,128)(2,1)S(1)}, bf16[4,256,512]{2,1,0:T(8,128)(2,1)S(1)}, u32[]{:S(2)}, u32[]{:S(2)}) collective-permute-start(bf16[4,256,512]{2,1,0:T(8,128)(2,1)S(1)} %slice.6), channel_id=1, source_target_pairs={{0,16},{16,0},{32,48},{48,32},{64,80},{80,64},{96,112},{112,96},{1... | collective-permute-start | bytes 3145736 | tf_op jit(solution)/shard_map/ppermute | solution.py:34
  4.7 4.4 %copy-start.12 = (bf16[4,1,1,256,1024]{4,3,2,1,0:T(8,128)(2,1)S(1)}, bf16[4,1,1,256,1024]{4,3,2,1,0:T(8,128)(2,1)}, u32[]{:S(2)}) copy-start(bf16[4,1,1,256,1024]{4,3,2,1,0:T(8,128)(2,1)} %param.5) | copy-start | bytes 6291460
  9.2 11.2 %copy-start.1 = (bf16[3,256,512]{2,1,0:T(8,128)(2,1)}, bf16[3,256,512]{2,1,0:T(8,128)(2,1)S(1)}, u32[]{:S(2)}) copy-start(bf16[3,256,512]{2,1,0:T(8,128)(2,1)S(1)} %get-tuple-element.327) | copy-start | bytes 2359300
  9.3 2.8 %copy-start.6 = (bf16[4,256,512]{2,1,0:T(8,128)(2,1)}, bf16[4,256,512]{2,1,0:T(8,128)(2,1)S(1)}, u32[]{:S(2)}) copy-start(bf16[4,256,512]{2,1,0:T(8,128)(2,1)S(1)} %slice.7) | copy-start | bytes 3145732
  9.3 2.7 %collective-permute-start.8 = (bf16[4,256,512]{2,1,0:T(8,128)(2,1)S(1)}, bf16[4,256,512]{2,1,0:T(8,128)(2,1)S(1)}, u32[]{:S(2)}, u32[]{:S(2)}) collective-permute-start(bf16[4,256,512]{2,1,0:T(8,128)(2,1)S(1)} %slice.7), channel_id=1, source_target_pairs={{0,16},{16,0},{32,48},{48,32},{64,80},{80,64},{96,112},{112,96},{1... | collective-permute-start | bytes 3145736 | tf_op jit(solution)/shard_map/ppermute | solution.py:34
  9.7 7.3 %copy-start.8 = (bf16[4,256,512]{2,1,0:T(8,128)(2,1)}, bf16[4,256,512]{2,1,0:T(8,128)(2,1)S(1)}, u32[]{:S(2)}) copy-start(bf16[4,256,512]{2,1,0:T(8,128)(2,1)S(1)} %collective-permute-done.9) | copy-start | bytes 3145732
  12.0 4.9 %copy-start.10 = (bf16[4,256,512]{2,1,0:T(8,128)(2,1)}, bf16[4,256,512]{2,1,0:T(8,128)(2,1)S(1)}, u32[]{:S(2)}) copy-start(bf16[4,256,512]{2,1,0:T(8,128)(2,1)S(1)} %collective-permute-done.8) | copy-start | bytes 3145732
  12.0 85.7 %collective-permute-start.12 = (bf16[3,256,512]{2,1,0:T(8,128)(2,1)}, bf16[3,256,512]{2,1,0:T(8,128)(2,1)S(1)}, u32[]{:S(2)}, u32[]{:S(2)}) collective-permute-start(bf16[3,256,512]{2,1,0:T(8,128)(2,1)} %get-tuple-element.328), channel_id=1, source_target_pairs={{0,2},{1,3},{2,0},{3,1},{4,6},{5,7},{6,4},{7,5},{8,18},{9,19},{10,... | collective-permute-start | bytes 2359304 | tf_op jit(solution)/shard_map/ppermute | solution.py:30
  17.0 81.6 %collective-permute-start.13 = (bf16[3,256,512]{2,1,0:T(8,128)(2,1)}, bf16[3,256,512]{2,1,0:T(8,128)(2,1)S(1)}, u32[]{:S(2)}, u32[]{:S(2)}) collective-permute-start(bf16[3,256,512]{2,1,0:T(8,128)(2,1)} %get-tuple-element.329), channel_id=1, source_target_pairs={{0,0},{1,1},{2,2},{3,3},{4,4},{5,5},{6,6},{7,7},{8,16},{9,17},{10,... | collective-permute-start | bytes 2359304 | tf_op jit(solution)/shard_map/ppermute | solution.py:30
  20.4 79.3 %collective-permute-start.11 = (bf16[3,256,512]{2,1,0:T(8,128)(2,1)}, bf16[3,256,512]{2,1,0:T(8,128)(2,1)S(1)}, u32[]{:S(2)}, u32[]{:S(2)}) collective-permute-start(bf16[3,256,512]{2,1,0:T(8,128)(2,1)} %copy-done.1), channel_id=1, source_target_pairs={{0,4},{1,5},{2,6},{3,7},{4,0},{5,1},{6,2},{7,3},{8,20},{9,21},{10,... | collective-permute-start | bytes 2359304 | tf_op jit(solution)/shard_map/ppermute | solution.py:30
  23.8 5.6 %copy-start.3 = (bf16[4,4,256,512]{3,2,1,0:T(8,128)(2,1)S(1)}, bf16[4,4,256,512]{3,2,1,0:T(8,128)(2,1)}, u32[]{:S(2)}) copy-start(bf16[4,4,256,512]{3,2,1,0:T(8,128)(2,1)} %get-tuple-element.26.factor) | copy-start | bytes 12582916 | tf_op jit(solution)/shard_map/cond
  23.8 5.6 %copy-start.5 = (bf16[4,256,512]{2,1,0:T(8,128)(2,1)S(1)}, bf16[4,256,512]{2,1,0:T(8,128)(2,1)}, u32[]{:S(2)}) copy-start(bf16[4,256,512]{2,1,0:T(8,128)(2,1)} %get-tuple-element.39.own) | copy-start | bytes 3145732 | tf_op jit(solution)/shard_map/cond
  23.8 5.6 %copy-start.9 = (bf16[4,256,512]{2,1,0:T(8,128)(2,1)S(1)}, bf16[4,256,512]{2,1,0:T(8,128)(2,1)}, u32[]{:S(2)}) copy-start(bf16[4,256,512]{2,1,0:T(8,128)(2,1)} %get-tuple-element.33.partner) | copy-start | bytes 3145732 | tf_op jit(solution)/shard_map/cond
  26.4 4.9 %copy-start.7 = (bf16[4,256,512]{2,1,0:T(8,128)(2,1)S(1)}, bf16[4,256,512]{2,1,0:T(8,128)(2,1)}, u32[]{:S(2)}) copy-start(bf16[4,256,512]{2,1,0:T(8,128)(2,1)} %get-tuple-element.46.own) | copy-start | bytes 3145732 | tf_op jit(solution)/shard_map/cond
  26.4 4.9 %copy-start.11 = (bf16[4,256,512]{2,1,0:T(8,128)(2,1)S(1)}, bf16[4,256,512]{2,1,0:T(8,128)(2,1)}, u32[]{:S(2)}) copy-start(bf16[4,256,512]{2,1,0:T(8,128)(2,1)} %get-tuple-element.43.partner) | copy-start | bytes 3145732 | tf_op jit(solution)/shard_map/cond
  26.4 15.5 %collective-permute-start = (bf16[2,256,512]{2,1,0:T(8,128)(2,1)S(1)}, bf16[2,256,512]{2,1,0:T(8,128)(2,1)S(1)}, u32[]{:S(2)}, u32[]{:S(2)}) collective-permute-start(bf16[2,256,512]{2,1,0:T(8,128)(2,1)S(1)} %branch_1_fun.12.own), channel_id=1, source_target_pairs={{0,32},{16,48},{32,0},{48,16},{64,96},{80,112},{96,64},{112,80},{1... | collective-permute-start | bytes 1572872 | tf_op jit(solution)/shard_map/cond/branch_1_fun/ppermute | solution.py:34
  30.6 16.7 %collective-permute-start.2 = (bf16[2,256,512]{2,1,0:T(8,128)(2,1)S(1)}, bf16[2,256,512]{2,1,0:T(8,128)(2,1)S(1)}, u32[]{:S(2)}, u32[]{:S(2)}) collective-permute-start(bf16[2,256,512]{2,1,0:T(8,128)(2,1)S(1)} %branch_1_fun.13.own), channel_id=1, source_target_pairs={{0,32},{16,48},{32,0},{48,16},{64,96},{80,112},{96,64},{112,80},{1... | collective-permute-start | bytes 1572872 | tf_op jit(solution)/shard_map/cond/branch_1_fun/ppermute | solution.py:34
  43.1 13.2 %collective-permute-start.1 = (bf16[2,256,512]{2,1,0:T(8,128)(2,1)S(1)}, bf16[2,256,512]{2,1,0:T(8,128)(2,1)S(1)}, u32[]{:S(2)}, u32[]{:S(2)}) collective-permute-start(bf16[2,256,512]{2,1,0:T(8,128)(2,1)S(1)} %branch_1_fun.16.own), channel_id=1, source_target_pairs={{0,64},{16,80},{32,96},{48,112},{64,0},{80,16},{96,32},{112,48},{1... | collective-permute-start | bytes 1572872 | tf_op jit(solution)/shard_map/cond/branch_1_fun/ppermute | solution.py:34
  48.5 19.1 %collective-permute-start.3 = (bf16[2,256,512]{2,1,0:T(8,128)(2,1)S(1)}, bf16[2,256,512]{2,1,0:T(8,128)(2,1)S(1)}, u32[]{:S(2)}, u32[]{:S(2)}) collective-permute-start(bf16[2,256,512]{2,1,0:T(8,128)(2,1)S(1)} %branch_1_fun.17.own), channel_id=1, source_target_pairs={{0,64},{16,80},{32,96},{48,112},{64,0},{80,16},{96,32},{112,48},{1... | collective-permute-start | bytes 1572872 | tf_op jit(solution)/shard_map/cond/branch_1_fun/ppermute | solution.py:34
  57.5 18.4 %collective-permute-start.4 = (bf16[2,256,512]{2,1,0:T(8,128)(2,1)S(1)}, bf16[2,256,512]{2,1,0:T(8,128)(2,1)S(1)}, u32[]{:S(2)}, u32[]{:S(2)}) collective-permute-start(bf16[2,256,512]{2,1,0:T(8,128)(2,1)S(1)} %branch_1_fun.18.own), channel_id=1, source_target_pairs={{0,128},{16,144},{32,160},{48,176},{64,192},{80,208},{96,224},{112... | collective-permute-start | bytes 1572872 | tf_op jit(solution)/shard_map/cond/branch_1_fun/ppermute | solution.py:34
  68.7 10.0 %collective-permute-start.6 = (bf16[2,256,512]{2,1,0:T(8,128)(2,1)S(1)}, bf16[2,256,512]{2,1,0:T(8,128)(2,1)S(1)}, u32[]{:S(2)}, u32[]{:S(2)}) collective-permute-start(bf16[2,256,512]{2,1,0:T(8,128)(2,1)S(1)} %branch_1_fun.14.own), channel_id=1, source_target_pairs={{0,32},{16,48},{32,0},{48,16},{64,96},{80,112},{96,64},{112,80},{1... | collective-permute-start | bytes 1572872 | tf_op jit(solution)/shard_map/cond/branch_1_fun/ppermute | solution.py:34
  78.7 10.0 %collective-permute-start.5 = (bf16[2,256,512]{2,1,0:T(8,128)(2,1)S(1)}, bf16[2,256,512]{2,1,0:T(8,128)(2,1)S(1)}, u32[]{:S(2)}, u32[]{:S(2)}) collective-permute-start(bf16[2,256,512]{2,1,0:T(8,128)(2,1)S(1)} %branch_1_fun.19.own), channel_id=1, source_target_pairs={{0,128},{16,144},{32,160},{48,176},{64,192},{80,208},{96,224},{112... | collective-permute-start | bytes 1572872 | tf_op jit(solution)/shard_map/cond/branch_1_fun/ppermute | solution.py:34
  82.4 10.1 %collective-permute-start.7 = (bf16[2,256,512]{2,1,0:T(8,128)(2,1)S(1)}, bf16[2,256,512]{2,1,0:T(8,128)(2,1)S(1)}, u32[]{:S(2)}, u32[]{:S(2)}) collective-permute-start(bf16[2,256,512]{2,1,0:T(8,128)(2,1)S(1)} %branch_1_fun.15.own), channel_id=1, source_target_pairs={{0,32},{16,48},{32,0},{48,16},{64,96},{80,112},{96,64},{112,80},{1... | collective-permute-start | bytes 1572872 | tf_op jit(solution)/shard_map/cond/branch_1_fun/ppermute | solution.py:34
  93.6 24.4 %collective-permute-start.18 = (bf16[3,256,512]{2,1,0:T(8,128)(2,1)S(1)}, bf16[3,256,512]{2,1,0:T(8,128)(2,1)S(1)}, u32[]{:S(2)}, u32[]{:S(2)}) collective-permute-start(bf16[3,256,512]{2,1,0:T(8,128)(2,1)S(1)} %get-tuple-element.353), channel_id=1, source_target_pairs={{0,6},{1,7},{2,4},{3,5},{4,2},{5,3},{6,0},{7,1},{8,22},{9,23},{10,... | collective-permute-start | bytes 2359304 | tf_op jit(solution)/shard_map/ppermute | solution.py:30
  97.1 12.3 %collective-permute-start.10 = (bf16[2,256,512]{2,1,0:T(8,128)(2,1)S(1)}, bf16[2,256,512]{2,1,0:T(8,128)(2,1)S(1)}, u32[]{:S(2)}, u32[]{:S(2)}) collective-permute-start(bf16[2,256,512]{2,1,0:T(8,128)(2,1)S(1)} %get-tuple-element.343.own), channel_id=1, source_target_pairs={{0,64},{16,80},{32,96},{48,112},{64,0},{80,16},{96,32},{112,48},{1... | collective-permute-start | bytes 1572872 | tf_op jit(solution)/shard_map/ppermute | solution.py:34
  97.7 22.4 %collective-permute-start.16 = (bf16[2,256,512]{2,1,0:T(8,128)(2,1)S(1)}, bf16[2,256,512]{2,1,0:T(8,128)(2,1)S(1)}, u32[]{:S(2)}, u32[]{:S(2)}) collective-permute-start(bf16[2,256,512]{2,1,0:T(8,128)(2,1)S(1)} %get-tuple-element.360.own), channel_id=1, source_target_pairs={{0,64},{16,80},{32,96},{48,112},{64,0},{80,16},{96,32},{112,48},{1... | collective-permute-start | bytes 1572872 | tf_op jit(solution)/shard_map/ppermute | solution.py:34
  98.6 21.6 %copy-start.2 = (bf16[4,4,1,1,256,512]{5,4,3,2,1,0:T(8,128)(2,1)S(1)}, bf16[4,4,1,1,256,512]{5,4,3,2,1,0:T(8,128)(2,1)}, u32[]{:S(2)}) copy-start(bf16[4,4,1,1,256,512]{5,4,3,2,1,0:T(8,128)(2,1)} %param.6) | copy-start | bytes 12582916
  98.6 21.5 %collective-permute-start.17 = (bf16[256,512]{1,0:T(8,128)(2,1)S(1)}, bf16[256,512]{1,0:T(8,128)(2,1)S(1)}, u32[]{:S(2)}, u32[]{:S(2)}) collective-permute-start(bf16[256,512]{1,0:T(8,128)(2,1)S(1)} %get-tuple-element.351), channel_id=1, source_target_pairs={{0,4},{1,5},{2,6},{3,7},{4,0},{5,1},{6,2},{7,3},{8,20},{9,21},{10,... | collective-permute-start | bytes 786440 | tf_op jit(solution)/shard_map/ppermute | solution.py:30
  118.0 20.7 %collective-permute-start.14 = (bf16[2,256,512]{2,1,0:T(8,128)(2,1)S(1)}, bf16[2,256,512]{2,1,0:T(8,128)(2,1)S(1)}, u32[]{:S(2)}, u32[]{:S(2)}) collective-permute-start(bf16[2,256,512]{2,1,0:T(8,128)(2,1)S(1)} %shard_map.38.own), channel_id=1, source_target_pairs={{0,128},{16,144},{32,160},{48,176},{64,192},{80,208},{96,224},{112... | collective-permute-start | bytes 1572872 | tf_op jit(solution)/shard_map/ppermute | solution.py:34
  121.3 23.0 %collective-permute-start.22 = (bf16[2,256,512]{2,1,0:T(8,128)(2,1)S(1)}, bf16[2,256,512]{2,1,0:T(8,128)(2,1)S(1)}, u32[]{:S(2)}, u32[]{:S(2)}) collective-permute-start(bf16[2,256,512]{2,1,0:T(8,128)(2,1)S(1)} %shard_map.39.own), channel_id=1, source_target_pairs={{0,128},{16,144},{32,160},{48,176},{64,192},{80,208},{96,224},{112... | collective-permute-start | bytes 1572872 | tf_op jit(solution)/shard_map/ppermute | solution.py:34
  124.1 14.6 %collective-permute-start.15 = (bf16[256,512]{1,0:T(8,128)(2,1)S(1)}, bf16[256,512]{1,0:T(8,128)(2,1)S(1)}, u32[]{:S(2)}, u32[]{:S(2)}) collective-permute-start(bf16[256,512]{1,0:T(8,128)(2,1)S(1)} %get-tuple-element.348), channel_id=1, source_target_pairs={{0,0},{1,1},{2,2},{3,3},{4,4},{5,5},{6,6},{7,7},{8,16},{9,17},{10,... | collective-permute-start | bytes 786440 | tf_op jit(solution)/shard_map/ppermute | solution.py:30
  129.1 15.3 %collective-permute-start.20 = (bf16[256,512]{1,0:T(8,128)(2,1)S(1)}, bf16[256,512]{1,0:T(8,128)(2,1)S(1)}, u32[]{:S(2)}, u32[]{:S(2)}) collective-permute-start(bf16[256,512]{1,0:T(8,128)(2,1)S(1)} %get-tuple-element.375), channel_id=1, source_target_pairs={{0,2},{1,3},{2,0},{3,1},{4,6},{5,7},{6,4},{7,5},{8,18},{9,19},{10,... | collective-permute-start | bytes 786440 | tf_op jit(solution)/shard_map/ppermute | solution.py:30
  130.3 17.5 %collective-permute-start.21 = (bf16[256,512]{1,0:T(8,128)(2,1)S(1)}, bf16[256,512]{1,0:T(8,128)(2,1)S(1)}, u32[]{:S(2)}, u32[]{:S(2)}) collective-permute-start(bf16[256,512]{1,0:T(8,128)(2,1)S(1)} %get-tuple-element.379), channel_id=1, source_target_pairs={{0,6},{1,7},{2,4},{3,5},{4,2},{5,3},{6,0},{7,1},{8,22},{9,23},{10,... | collective-permute-start | bytes 786440 | tf_op jit(solution)/shard_map/ppermute | solution.py:30
  147.9 10.9 %collective-permute-start.23 = (bf16[4,256,512]{2,1,0:T(8,128)(2,1)S(1)}, bf16[4,256,512]{2,1,0:T(8,128)(2,1)S(1)}, u32[]{:S(2)}, u32[]{:S(2)}) collective-permute-start(bf16[4,256,512]{2,1,0:T(8,128)(2,1)S(1)} %pad_maximum_fusion.own), channel_id=1, source_target_pairs={{0,16},{16,0},{32,48},{48,32},{64,80},{80,64},{96,112},{112,96},{1... | collective-permute-start | bytes 3145736 | tf_op jit(solution)/shard_map/ppermute | solution.py:34
  148.0 15.4 %collective-permute-start.24 = (bf16[256,512]{1,0:T(8,128)(2,1)S(1)}, bf16[256,512]{1,0:T(8,128)(2,1)S(1)}, u32[]{:S(2)}, u32[]{:S(2)}) collective-permute-start(bf16[256,512]{1,0:T(8,128)(2,1)S(1)} %get-tuple-element.413), channel_id=1, source_target_pairs={{0,4},{1,5},{2,6},{3,7},{4,0},{5,1},{6,2},{7,3},{8,20},{9,21},{10,... | collective-permute-start | bytes 786440 | tf_op jit(solution)/shard_map/ppermute | solution.py:30
  151.0 14.9 %collective-permute-start.19 = (bf16[256,512]{1,0:T(8,128)(2,1)S(1)}, bf16[256,512]{1,0:T(8,128)(2,1)S(1)}, u32[]{:S(2)}, u32[]{:S(2)}) collective-permute-start(bf16[256,512]{1,0:T(8,128)(2,1)S(1)} %get-tuple-element.373), channel_id=1, source_target_pairs={{0,0},{1,1},{2,2},{3,3},{4,4},{5,5},{6,6},{7,7},{8,16},{9,17},{10,... | collective-permute-start | bytes 786440 | tf_op jit(solution)/shard_map/ppermute | solution.py:30
  154.5 22.1 %collective-permute-start.25 = (bf16[256,512]{1,0:T(8,128)(2,1)S(1)}, bf16[256,512]{1,0:T(8,128)(2,1)S(1)}, u32[]{:S(2)}, u32[]{:S(2)}) collective-permute-start(bf16[256,512]{1,0:T(8,128)(2,1)S(1)} %get-tuple-element.420), channel_id=1, source_target_pairs={{0,2},{1,3},{2,0},{3,1},{4,6},{5,7},{6,4},{7,5},{8,18},{9,19},{10,... | collective-permute-start | bytes 786440 | tf_op jit(solution)/shard_map/ppermute | solution.py:30
  158.9 18.1 %collective-permute-start.26 = (bf16[256,512]{1,0:T(8,128)(2,1)S(1)}, bf16[256,512]{1,0:T(8,128)(2,1)S(1)}, u32[]{:S(2)}, u32[]{:S(2)}) collective-permute-start(bf16[256,512]{1,0:T(8,128)(2,1)S(1)} %get-tuple-element.424), channel_id=1, source_target_pairs={{0,6},{1,7},{2,4},{3,5},{4,2},{5,3},{6,0},{7,1},{8,22},{9,23},{10,... | collective-permute-start | bytes 786440 | tf_op jit(solution)/shard_map/ppermute | solution.py:30
  158.9 1.0 copy-start.14
  177.1 11.2 %collective-permute-start.29 = (bf16[4,256,512]{2,1,0:T(8,128)(2,1)S(1)}, bf16[4,256,512]{2,1,0:T(8,128)(2,1)S(1)}, u32[]{:S(2)}, u32[]{:S(2)}) collective-permute-start(bf16[4,256,512]{2,1,0:T(8,128)(2,1)S(1)} %pad_maximum_fusion.1.own), channel_id=1, source_target_pairs={{0,16},{16,0},{32,48},{48,32},{64,80},{80,64},{96,112},{112,96},{1... | collective-permute-start | bytes 3145736 | tf_op jit(solution)/shard_map/ppermute | solution.py:34
  177.2 18.5 %collective-permute-start.31 = (bf16[256,512]{1,0:T(8,128)(2,1)S(1)}, bf16[256,512]{1,0:T(8,128)(2,1)S(1)}, u32[]{:S(2)}, u32[]{:S(2)}) collective-permute-start(bf16[256,512]{1,0:T(8,128)(2,1)S(1)} %get-tuple-element.457), channel_id=1, source_target_pairs={{0,6},{1,7},{2,4},{3,5},{4,2},{5,3},{6,0},{7,1},{8,22},{9,23},{10,... | collective-permute-start | bytes 786440 | tf_op jit(solution)/shard_map/ppermute | solution.py:30
  180.6 18.5 %collective-permute-start.30 = (bf16[256,512]{1,0:T(8,128)(2,1)S(1)}, bf16[256,512]{1,0:T(8,128)(2,1)S(1)}, u32[]{:S(2)}, u32[]{:S(2)}) collective-permute-start(bf16[256,512]{1,0:T(8,128)(2,1)S(1)} %get-tuple-element.450), channel_id=1, source_target_pairs={{0,2},{1,3},{2,0},{3,1},{4,6},{5,7},{6,4},{7,5},{8,18},{9,19},{10,... | collective-permute-start | bytes 786440 | tf_op jit(solution)/shard_map/ppermute | solution.py:30
  180.6 22.9 %collective-permute-start.28 = (bf16[256,512]{1,0:T(8,128)(2,1)S(1)}, bf16[256,512]{1,0:T(8,128)(2,1)S(1)}, u32[]{:S(2)}, u32[]{:S(2)}) collective-permute-start(bf16[256,512]{1,0:T(8,128)(2,1)S(1)} %get-tuple-element.431), channel_id=1, source_target_pairs={{0,4},{1,5},{2,6},{3,7},{4,0},{5,1},{6,2},{7,3},{8,20},{9,21},{10,... | collective-permute-start | bytes 786440 | tf_op jit(solution)/shard_map/ppermute | solution.py:30
  184.9 27.2 %collective-permute-start.27 = (bf16[256,512]{1,0:T(8,128)(2,1)S(1)}, bf16[256,512]{1,0:T(8,128)(2,1)S(1)}, u32[]{:S(2)}, u32[]{:S(2)}) collective-permute-start(bf16[256,512]{1,0:T(8,128)(2,1)S(1)} %get-tuple-element.429), channel_id=1, source_target_pairs={{0,0},{1,1},{2,2},{3,3},{4,4},{5,5},{6,6},{7,7},{8,16},{9,17},{10,... | collective-permute-start | bytes 786440 | tf_op jit(solution)/shard_map/ppermute | solution.py:30
  188.3 1.0 copy-start.13
  192.8 20.8 %collective-permute-start.36 = (bf16[256,512]{1,0:T(8,128)(2,1)S(1)}, bf16[256,512]{1,0:T(8,128)(2,1)S(1)}, u32[]{:S(2)}, u32[]{:S(2)}) collective-permute-start(bf16[256,512]{1,0:T(8,128)(2,1)S(1)} %get-tuple-element.467), channel_id=1, source_target_pairs={{0,4},{1,5},{2,6},{3,7},{4,0},{5,1},{6,2},{7,3},{8,20},{9,21},{10,... | collective-permute-start | bytes 786440 | tf_op jit(solution)/shard_map/ppermute | solution.py:30
  195.7 20.0 %collective-permute-start.35 = (bf16[256,512]{1,0:T(8,128)(2,1)S(1)}, bf16[256,512]{1,0:T(8,128)(2,1)S(1)}, u32[]{:S(2)}, u32[]{:S(2)}) collective-permute-start(bf16[256,512]{1,0:T(8,128)(2,1)S(1)} %get-tuple-element.466), channel_id=1, source_target_pairs={{0,0},{1,1},{2,2},{3,3},{4,4},{5,5},{6,6},{7,7},{8,16},{9,17},{10,... | collective-permute-start | bytes 786440 | tf_op jit(solution)/shard_map/ppermute | solution.py:30
  199.1 17.3 %collective-permute-start.33 = (bf16[256,512]{1,0:T(8,128)(2,1)S(1)}, bf16[256,512]{1,0:T(8,128)(2,1)S(1)}, u32[]{:S(2)}, u32[]{:S(2)}) collective-permute-start(bf16[256,512]{1,0:T(8,128)(2,1)S(1)} %get-tuple-element.465), channel_id=1, source_target_pairs={{0,6},{1,7},{2,4},{3,5},{4,2},{5,3},{6,0},{7,1},{8,22},{9,23},{10,... | collective-permute-start | bytes 786440 | tf_op jit(solution)/shard_map/ppermute | solution.py:30
  203.5 25.6 %collective-permute-start.32 = (bf16[256,512]{1,0:T(8,128)(2,1)S(1)}, bf16[256,512]{1,0:T(8,128)(2,1)S(1)}, u32[]{:S(2)}, u32[]{:S(2)}) collective-permute-start(bf16[256,512]{1,0:T(8,128)(2,1)S(1)} %get-tuple-element.462), channel_id=1, source_target_pairs={{0,2},{1,3},{2,0},{3,1},{4,6},{5,7},{6,4},{7,5},{8,18},{9,19},{10,... | collective-permute-start | bytes 786440 | tf_op jit(solution)/shard_map/ppermute | solution.py:30
  212.1 18.6 %copy-start = (bf16[4,4,1,1,256,512]{5,4,3,2,1,0:T(8,128)(2,1)S(1)}, bf16[4,4,1,1,256,512]{5,4,3,2,1,0:T(8,128)(2,1)}, u32[]{:S(2)}) copy-start(bf16[4,4,1,1,256,512]{5,4,3,2,1,0:T(8,128)(2,1)} %param.7) | copy-start | bytes 12582916
  212.3 18.5 %collective-permute-start.37 = (bf16[2,256,512]{2,1,0:T(8,128)(2,1)S(1)}, bf16[2,256,512]{2,1,0:T(8,128)(2,1)S(1)}, u32[]{:S(2)}, u32[]{:S(2)}) collective-permute-start(bf16[2,256,512]{2,1,0:T(8,128)(2,1)S(1)} %pad_maximum_fusion.5.own), channel_id=1, source_target_pairs={{0,1},{1,0},{2,3},{3,2},{4,5},{5,4},{6,7},{7,6},{8,9},{9,8},{10,11... | collective-permute-start | bytes 1572872 | tf_op jit(solution)/shard_map/ppermute | solution.py:34
  213.7 24.0 %collective-permute-start.39 = (bf16[2,256,512]{2,1,0:T(8,128)(2,1)S(1)}, bf16[2,256,512]{2,1,0:T(8,128)(2,1)S(1)}, u32[]{:S(2)}, u32[]{:S(2)}) collective-permute-start(bf16[2,256,512]{2,1,0:T(8,128)(2,1)S(1)} %pad_maximum_fusion.4.own), channel_id=1, source_target_pairs={{0,1},{1,0},{2,3},{3,2},{4,5},{5,4},{6,7},{7,6},{8,9},{9,8},{10,11... | collective-permute-start | bytes 1572872 | tf_op jit(solution)/shard_map/ppermute | solution.py:34
  215.8 33.1 %collective-permute-start.38 = (bf16[2,256,512]{2,1,0:T(8,128)(2,1)S(1)}, bf16[2,256,512]{2,1,0:T(8,128)(2,1)S(1)}, u32[]{:S(2)}, u32[]{:S(2)}) collective-permute-start(bf16[2,256,512]{2,1,0:T(8,128)(2,1)S(1)} %pad_maximum_fusion.3.own), channel_id=1, source_target_pairs={{0,1},{1,0},{2,3},{3,2},{4,5},{5,4},{6,7},{7,6},{8,9},{9,8},{10,11... | collective-permute-start | bytes 1572872 | tf_op jit(solution)/shard_map/ppermute | solution.py:34
  229.1 30.0 %collective-permute-start.34 = (bf16[2,256,512]{2,1,0:T(8,128)(2,1)S(1)}, bf16[2,256,512]{2,1,0:T(8,128)(2,1)S(1)}, u32[]{:S(2)}, u32[]{:S(2)}) collective-permute-start(bf16[2,256,512]{2,1,0:T(8,128)(2,1)S(1)} %pad_maximum_fusion.2.own), channel_id=1, source_target_pairs={{0,1},{1,0},{2,3},{3,2},{4,5},{5,4},{6,7},{7,6},{8,9},{9,8},{10,11... | collective-permute-start | bytes 1572872 | tf_op jit(solution)/shard_map/ppermute | solution.py:34

commit v4 on v3

--- a/solution.py
+++ b/solution.py
@@ -9,7 +9,7 @@
 
 WIDTHS = (512, 512)
 RANK = 256
-VMEM = 48 * 2**20
+VMEM = 16 * 2**20
 
 
 def swap_dest(step):

time: 261 us -> 262 us (level)
  waiting for transfers between devices: 119 us -> 125 us
  Pallas kernels: 40.6 us -> 36.1 us
    ppermute x20, waiting for transfers between devices: 48.6 us -> 53.8 us  [swap(): return lax.ppermute(value, ('leaf', 'wide'), SWAPS[step])]
  transfers between devices with their start and end apart: 40 -> 40, of which waited for: 25 -> 25; matrix products, arithmetic and copies ran while one was open for 0% -> 0% of each run, Pallas kernels for 15% -> 13%
where the time goes in v4:
time: 262 us; the launch traced here: 261 us
  waiting for transfers between devices  125 us (48%)
  starting transfers between devices  95.8 us (37%)
  Pallas kernels  36.1 us (14%)
  local copies, waits for them, and re-layouts  3.64 us (1%)
    ppermute x20, waiting for transfers between devices, exchange(): return lax.ppermute(value, axis, [(d, d ^ mask) for d in range(16)])  71.1 us
    ppermute x20, starting transfers between devices, swap(): return lax.ppermute(value, ('leaf', 'wide'), SWAPS[step])  64.2 us
    ppermute x20, waiting for transfers between devices, swap(): return lax.ppermute(value, ('leaf', 'wide'), SWAPS[step])  53.8 us
    ppermute x20, starting transfers between devices, exchange(): return lax.ppermute(value, axis, [(d, d ^ mask) for d in range(16)])  31.6 us
    pallas_call x20, Pallas kernels, level_call(): pl.pallas_call(functools.partial(level_body, split), grid_spec=pltpu.Pref...  29 us
  transfers between devices with their start and end apart: 40, of which 25 were waited for; matrix products, arithmetic and copies ran while one was open for 0% of the time, Pallas kernels for 13%

profile of v4, /device:TPU:1, one launch (start us, length us, event | category | flops | bytes accessed | tf_op | source)
XLA Modules:
  0.0 261.5 jit_solution(822100874571973278)
XLA Ops:
  0.1 1.3 slice.6
  1.4 3.3 %collective-permute-start.9 = (bf16[4,256,512]{2,1,0:T(8,128)(2,1)S(1)}, bf16[4,256,512]{2,1,0:T(8,128)(2,1)S(1)}, u32[]{:S(2)}, u32[]{:S(2)}) collective-permute-start(bf16[4,256,512]{2,1,0:T(8,128)(2,1)S(1)} %slice.6), channel_id=1, source_target_pairs={{0,16},{16,0},{32,48},{48,32},{64,80},{80,64},{96,112},{112,96},{1... | collective-permute-start | bytes 3145736 | tf_op jit(solution)/shard_map/ppermute | solution.py:34
  4.7 2.2 copy-done
  6.9 2.3 shard_map.37
  9.8 2.4 collective-permute-done.8
  12.1 4.9 %collective-permute-start.12 = (bf16[3,256,512]{2,1,0:T(8,128)(2,1)}, bf16[3,256,512]{2,1,0:T(8,128)(2,1)S(1)}, u32[]{:S(2)}, u32[]{:S(2)}) collective-permute-start(bf16[3,256,512]{2,1,0:T(8,128)(2,1)} %get-tuple-element.328), channel_id=1, source_target_pairs={{0,2},{1,3},{2,0},{3,1},{4,6},{5,7},{6,4},{7,5},{8,18},{9,19},{10,... | collective-permute-start | bytes 2359304 | tf_op jit(solution)/shard_map/ppermute | solution.py:30
  17.0 3.3 %collective-permute-start.13 = (bf16[3,256,512]{2,1,0:T(8,128)(2,1)}, bf16[3,256,512]{2,1,0:T(8,128)(2,1)S(1)}, u32[]{:S(2)}, u32[]{:S(2)}) collective-permute-start(bf16[3,256,512]{2,1,0:T(8,128)(2,1)} %get-tuple-element.329), channel_id=1, source_target_pairs={{0,0},{1,1},{2,2},{3,3},{4,4},{5,5},{6,6},{7,7},{8,16},{9,17},{10,... | collective-permute-start | bytes 2359304 | tf_op jit(solution)/shard_map/ppermute | solution.py:30
  20.5 3.4 %collective-permute-start.11 = (bf16[3,256,512]{2,1,0:T(8,128)(2,1)}, bf16[3,256,512]{2,1,0:T(8,128)(2,1)S(1)}, u32[]{:S(2)}, u32[]{:S(2)}) collective-permute-start(bf16[3,256,512]{2,1,0:T(8,128)(2,1)} %copy-done.2), channel_id=1, source_target_pairs={{0,4},{1,5},{2,6},{3,7},{4,0},{5,1},{6,2},{7,3},{8,20},{9,21},{10,... | collective-permute-start | bytes 2359304 | tf_op jit(solution)/shard_map/ppermute | solution.py:30
  23.9 69.8 %conditional.1 = (bf16[256,512]{1,0:T(8,128)(2,1)S(1)}, bf16[256,512]{1,0:T(8,128)(2,1)S(1)}, bf16[256,512]{1,0:T(8,128)(2,1)S(1)}, bf16[256,512]{1,0:T(8,128)(2...) conditional(s32[]{:T(128)} %convert_element_type.3, () %tuple.134, ...), branch_computations={%region_0.0_spmd, %region_1.0_spmd} | conditional | flops 12 | bytes 50332180 | solution.py:284
  23.9 2.6 branch_1_fun.12.own
  26.5 3.0 %collective-permute-start = (bf16[2,256,512]{2,1,0:T(8,128)(2,1)S(1)}, bf16[2,256,512]{2,1,0:T(8,128)(2,1)S(1)}, u32[]{:S(2)}, u32[]{:S(2)}) collective-permute-start(bf16[2,256,512]{2,1,0:T(8,128)(2,1)S(1)} %branch_1_fun.12.own), channel_id=1, source_target_pairs={{0,32},{16,48},{32,0},{48,16},{64,96},{80,112},{96,64},{112,80},{1... | collective-permute-start | bytes 1572872 | tf_op jit(solution)/shard_map/cond/branch_1_fun/ppermute | solution.py:34
  33.7 8.3 %collective-permute-done.partner = bf16[2,256,512]{2,1,0:T(8,128)(2,1)S(1)} collective-permute-done((bf16[2,256,512]{2,1,0:T(8,128)(2,1)S(1)}, bf16[2,256,512]{2,1,0:T(8,128)(2,1)S(1)}, u32[]{:S(2)}, u32[]{:S(2)}) %collective-permute-start) | collective-permute-done | bytes 524320 | tf_op jit(solution)/shard_map/cond/branch_1_fun/ppermute | solution.py:34
  43.2 1.3 collective-permute-start.1
  44.5 2.9 %collective-permute-done.2.partner = bf16[2,256,512]{2,1,0:T(8,128)(2,1)S(1)} collective-permute-done((bf16[2,256,512]{2,1,0:T(8,128)(2,1)S(1)}, bf16[2,256,512]{2,1,0:T(8,128)(2,1)S(1)}, u32[]{:S(2)}, u32[]{:S(2)}) %collective-permute-start.2) | collective-permute-done | bytes 524320 | tf_op jit(solution)/shard_map/cond/branch_1_fun/ppermute | solution.py:34
  48.6 1.3 collective-permute-start.3
  49.9 6.5 %collective-permute-done.1.partner = bf16[2,256,512]{2,1,0:T(8,128)(2,1)S(1)} collective-permute-done((bf16[2,256,512]{2,1,0:T(8,128)(2,1)S(1)}, bf16[2,256,512]{2,1,0:T(8,128)(2,1)S(1)}, u32[]{:S(2)}, u32[]{:S(2)}) %collective-permute-start.1) | collective-permute-done | bytes 524320 | tf_op jit(solution)/shard_map/cond/branch_1_fun/ppermute | solution.py:34
  57.6 2.8 %collective-permute-start.4 = (bf16[2,256,512]{2,1,0:T(8,128)(2,1)S(1)}, bf16[2,256,512]{2,1,0:T(8,128)(2,1)S(1)}, u32[]{:S(2)}, u32[]{:S(2)}) collective-permute-start(bf16[2,256,512]{2,1,0:T(8,128)(2,1)S(1)} %branch_1_fun.18.own), channel_id=1, source_target_pairs={{0,128},{16,144},{32,160},{48,176},{64,192},{80,208},{96,224},{112... | collective-permute-start | bytes 1572872 | tf_op jit(solution)/shard_map/cond/branch_1_fun/ppermute | solution.py:34
  60.4 7.2 %collective-permute-done.3.partner = bf16[2,256,512]{2,1,0:T(8,128)(2,1)S(1)} collective-permute-done((bf16[2,256,512]{2,1,0:T(8,128)(2,1)S(1)}, bf16[2,256,512]{2,1,0:T(8,128)(2,1)S(1)}, u32[]{:S(2)}, u32[]{:S(2)}) %collective-permute-start.3) | collective-permute-done | bytes 524320 | tf_op jit(solution)/shard_map/cond/branch_1_fun/ppermute | solution.py:34
  68.8 3.1 %collective-permute-start.6 = (bf16[2,256,512]{2,1,0:T(8,128)(2,1)S(1)}, bf16[2,256,512]{2,1,0:T(8,128)(2,1)S(1)}, u32[]{:S(2)}, u32[]{:S(2)}) collective-permute-start(bf16[2,256,512]{2,1,0:T(8,128)(2,1)S(1)} %branch_1_fun.14.own), channel_id=1, source_target_pairs={{0,32},{16,48},{32,0},{48,16},{64,96},{80,112},{96,64},{112,80},{1... | collective-permute-start | bytes 1572872 | tf_op jit(solution)/shard_map/cond/branch_1_fun/ppermute | solution.py:34
  71.9 4.1 %collective-permute-done.4.partner = bf16[2,256,512]{2,1,0:T(8,128)(2,1)S(1)} collective-permute-done((bf16[2,256,512]{2,1,0:T(8,128)(2,1)S(1)}, bf16[2,256,512]{2,1,0:T(8,128)(2,1)S(1)}, u32[]{:S(2)}, u32[]{:S(2)}) %collective-permute-start.4) | collective-permute-done | bytes 524320 | tf_op jit(solution)/shard_map/cond/branch_1_fun/ppermute | solution.py:34
  77.2 1.6 collective-permute-done.6.partner
  78.8 2.4 collective-permute-start.5
  82.4 3.3 %collective-permute-start.7 = (bf16[2,256,512]{2,1,0:T(8,128)(2,1)S(1)}, bf16[2,256,512]{2,1,0:T(8,128)(2,1)S(1)}, u32[]{:S(2)}, u32[]{:S(2)}) collective-permute-start(bf16[2,256,512]{2,1,0:T(8,128)(2,1)S(1)} %branch_1_fun.15.own), channel_id=1, source_target_pairs={{0,32},{16,48},{32,0},{48,16},{64,96},{80,112},{96,64},{112,80},{1... | collective-permute-start | bytes 1572872 | tf_op jit(solution)/shard_map/cond/branch_1_fun/ppermute | solution.py:34
  85.8 3.1 %collective-permute-done.5.partner = bf16[2,256,512]{2,1,0:T(8,128)(2,1)S(1)} collective-permute-done((bf16[2,256,512]{2,1,0:T(8,128)(2,1)S(1)}, bf16[2,256,512]{2,1,0:T(8,128)(2,1)S(1)}, u32[]{:S(2)}, u32[]{:S(2)}) %collective-permute-start.5) | collective-permute-done | bytes 524320 | tf_op jit(solution)/shard_map/cond/branch_1_fun/ppermute | solution.py:34
  88.8 1.2 branch_1_fun.22
  90.1 2.4 collective-permute-done.7.partner
  93.7 3.5 %collective-permute-start.18 = (bf16[3,256,512]{2,1,0:T(8,128)(2,1)S(1)}, bf16[3,256,512]{2,1,0:T(8,128)(2,1)S(1)}, u32[]{:S(2)}, u32[]{:S(2)}) collective-permute-start(bf16[3,256,512]{2,1,0:T(8,128)(2,1)S(1)} %get-tuple-element.353), channel_id=1, source_target_pairs={{0,6},{1,7},{2,4},{3,5},{4,2},{5,3},{6,0},{7,1},{8,22},{9,23},{10,... | collective-permute-start | bytes 2359304 | tf_op jit(solution)/shard_map/ppermute | solution.py:30
  99.8 9.7 %collective-permute-done.10.partner = bf16[2,256,512]{2,1,0:T(8,128)(2,1)S(1)} collective-permute-done((bf16[2,256,512]{2,1,0:T(8,128)(2,1)S(1)}, bf16[2,256,512]{2,1,0:T(8,128)(2,1)S(1)}, u32[]{:S(2)}, u32[]{:S(2)}) %collective-permute-start.10) | collective-permute-done | bytes 524320 | tf_op jit(solution)/shard_map/ppermute | solution.py:34
  109.5 2.1 shard_map.38.own
  111.6 6.5 %collective-permute-done.18.refs_3_ = bf16[3,256,512]{2,1,0:T(8,128)(2,1)S(1)} collective-permute-done((bf16[3,256,512]{2,1,0:T(8,128)(2,1)S(1)}, bf16[3,256,512]{2,1,0:T(8,128)(2,1)S(1)}, u32[]{:S(2)}, u32[]{:S(2)}) %collective-permute-start.18) | collective-permute-done | bytes 786464 | tf_op jit(solution)/shard_map/ppermute | solution.py:30
  118.7 1.6 collective-permute-done.17
  121.4 2.7 %collective-permute-start.22 = (bf16[2,256,512]{2,1,0:T(8,128)(2,1)S(1)}, bf16[2,256,512]{2,1,0:T(8,128)(2,1)S(1)}, u32[]{:S(2)}, u32[]{:S(2)}) collective-permute-start(bf16[2,256,512]{2,1,0:T(8,128)(2,1)S(1)} %shard_map.39.own), channel_id=1, source_target_pairs={{0,128},{16,144},{32,160},{48,176},{64,192},{80,208},{96,224},{112... | collective-permute-start | bytes 1572872 | tf_op jit(solution)/shard_map/ppermute | solution.py:34
  124.2 5.0 %collective-permute-start.15 = (bf16[256,512]{1,0:T(8,128)(2,1)S(1)}, bf16[256,512]{1,0:T(8,128)(2,1)S(1)}, u32[]{:S(2)}, u32[]{:S(2)}) collective-permute-start(bf16[256,512]{1,0:T(8,128)(2,1)S(1)} %get-tuple-element.348), channel_id=1, source_target_pairs={{0,0},{1,1},{2,2},{3,3},{4,4},{5,5},{6,6},{7,7},{8,16},{9,17},{10,... | collective-permute-start | bytes 786440 | tf_op jit(solution)/shard_map/ppermute | solution.py:30
  130.3 3.1 %collective-permute-start.21 = (bf16[256,512]{1,0:T(8,128)(2,1)S(1)}, bf16[256,512]{1,0:T(8,128)(2,1)S(1)}, u32[]{:S(2)}, u32[]{:S(2)}) collective-permute-start(bf16[256,512]{1,0:T(8,128)(2,1)S(1)} %get-tuple-element.379), channel_id=1, source_target_pairs={{0,6},{1,7},{2,4},{3,5},{4,2},{5,3},{6,0},{7,1},{8,22},{9,23},{10,... | collective-permute-start | bytes 786440 | tf_op jit(solution)/shard_map/ppermute | solution.py:30
  133.4 5.3 %collective-permute-done.15 = bf16[256,512]{1,0:T(8,128)(2,1)S(1)} collective-permute-done((bf16[256,512]{1,0:T(8,128)(2,1)S(1)}, bf16[256,512]{1,0:T(8,128)(2,1)S(1)}, u32[]{:S(2)}, u32[]{:S(2)}) %collective-permute-start.15) | collective-permute-done | bytes 262176 | tf_op jit(solution)/shard_map/ppermute | solution.py:30
  138.7 1.2 shard_map.40
  140.0 4.5 %collective-permute-done.20 = bf16[256,512]{1,0:T(8,128)(2,1)S(1)} collective-permute-done((bf16[256,512]{1,0:T(8,128)(2,1)S(1)}, bf16[256,512]{1,0:T(8,128)(2,1)S(1)}, u32[]{:S(2)}, u32[]{:S(2)}) %collective-permute-start.20) | collective-permute-done | bytes 262176 | tf_op jit(solution)/shard_map/ppermute | solution.py:30
  145.7 2.2 collective-permute-done.21
  148.1 3.0 %collective-permute-start.24 = (bf16[256,512]{1,0:T(8,128)(2,1)S(1)}, bf16[256,512]{1,0:T(8,128)(2,1)S(1)}, u32[]{:S(2)}, u32[]{:S(2)}) collective-permute-start(bf16[256,512]{1,0:T(8,128)(2,1)S(1)} %get-tuple-element.413), channel_id=1, source_target_pairs={{0,4},{1,5},{2,6},{3,7},{4,0},{5,1},{6,2},{7,3},{8,20},{9,21},{10,... | collective-permute-start | bytes 786440 | tf_op jit(solution)/shard_map/ppermute | solution.py:30
  151.1 3.5 %collective-permute-start.19 = (bf16[256,512]{1,0:T(8,128)(2,1)S(1)}, bf16[256,512]{1,0:T(8,128)(2,1)S(1)}, u32[]{:S(2)}, u32[]{:S(2)}) collective-permute-start(bf16[256,512]{1,0:T(8,128)(2,1)S(1)} %get-tuple-element.373), channel_id=1, source_target_pairs={{0,0},{1,1},{2,2},{3,3},{4,4},{5,5},{6,6},{7,7},{8,16},{9,17},{10,... | collective-permute-start | bytes 786440 | tf_op jit(solution)/shard_map/ppermute | solution.py:30
  154.6 4.4 %collective-permute-start.25 = (bf16[256,512]{1,0:T(8,128)(2,1)S(1)}, bf16[256,512]{1,0:T(8,128)(2,1)S(1)}, u32[]{:S(2)}, u32[]{:S(2)}) collective-permute-start(bf16[256,512]{1,0:T(8,128)(2,1)S(1)} %get-tuple-element.420), channel_id=1, source_target_pairs={{0,2},{1,3},{2,0},{3,1},{4,6},{5,7},{6,4},{7,5},{8,18},{9,19},{10,... | collective-permute-start | bytes 786440 | tf_op jit(solution)/shard_map/ppermute | solution.py:30
  158.9 2.4 shard_map.42
  161.3 4.7 %collective-permute-done.19 = bf16[256,512]{1,0:T(8,128)(2,1)S(1)} collective-permute-done((bf16[256,512]{1,0:T(8,128)(2,1)S(1)}, bf16[256,512]{1,0:T(8,128)(2,1)S(1)}, u32[]{:S(2)}, u32[]{:S(2)}) %collective-permute-start.19) | collective-permute-done | bytes 262176 | tf_op jit(solution)/shard_map/ppermute | solution.py:30
  166.0 10.7 %collective-permute-done.25 = bf16[256,512]{1,0:T(8,128)(2,1)S(1)} collective-permute-done((bf16[256,512]{1,0:T(8,128)(2,1)S(1)}, bf16[256,512]{1,0:T(8,128)(2,1)S(1)}, u32[]{:S(2)}, u32[]{:S(2)}) %collective-permute-start.25) | collective-permute-done | bytes 262176 | tf_op jit(solution)/shard_map/ppermute | solution.py:30
  177.2 3.5 %collective-permute-start.31 = (bf16[256,512]{1,0:T(8,128)(2,1)S(1)}, bf16[256,512]{1,0:T(8,128)(2,1)S(1)}, u32[]{:S(2)}, u32[]{:S(2)}) collective-permute-start(bf16[256,512]{1,0:T(8,128)(2,1)S(1)} %get-tuple-element.457), channel_id=1, source_target_pairs={{0,6},{1,7},{2,4},{3,5},{4,2},{5,3},{6,0},{7,1},{8,22},{9,23},{10,... | collective-permute-start | bytes 786440 | tf_op jit(solution)/shard_map/ppermute | solution.py:30
  180.7 4.3 %collective-permute-start.28 = (bf16[256,512]{1,0:T(8,128)(2,1)S(1)}, bf16[256,512]{1,0:T(8,128)(2,1)S(1)}, u32[]{:S(2)}, u32[]{:S(2)}) collective-permute-start(bf16[256,512]{1,0:T(8,128)(2,1)S(1)} %get-tuple-element.431), channel_id=1, source_target_pairs={{0,4},{1,5},{2,6},{3,7},{4,0},{5,1},{6,2},{7,3},{8,20},{9,21},{10,... | collective-permute-start | bytes 786440 | tf_op jit(solution)/shard_map/ppermute | solution.py:30
  185.0 3.3 %collective-permute-start.27 = (bf16[256,512]{1,0:T(8,128)(2,1)S(1)}, bf16[256,512]{1,0:T(8,128)(2,1)S(1)}, u32[]{:S(2)}, u32[]{:S(2)}) collective-permute-start(bf16[256,512]{1,0:T(8,128)(2,1)S(1)} %get-tuple-element.429), channel_id=1, source_target_pairs={{0,0},{1,1},{2,2},{3,3},{4,4},{5,5},{6,6},{7,7},{8,16},{9,17},{10,... | collective-permute-start | bytes 786440 | tf_op jit(solution)/shard_map/ppermute | solution.py:30
  188.4 2.4 shard_map.43
  190.7 2.8 %collective-permute-start.36 = (bf16[256,512]{1,0:T(8,128)(2,1)S(1)}, bf16[256,512]{1,0:T(8,128)(2,1)S(1)}, u32[]{:S(2)}, u32[]{:S(2)}) collective-permute-start(bf16[256,512]{1,0:T(8,128)(2,1)S(1)} %get-tuple-element.467), channel_id=1, source_target_pairs={{0,4},{1,5},{2,6},{3,7},{4,0},{5,1},{6,2},{7,3},{8,20},{9,21},{10,... | collective-permute-start | bytes 786440 | tf_op jit(solution)/shard_map/ppermute | solution.py:30
  193.6 3.4 %collective-permute-start.35 = (bf16[256,512]{1,0:T(8,128)(2,1)S(1)}, bf16[256,512]{1,0:T(8,128)(2,1)S(1)}, u32[]{:S(2)}, u32[]{:S(2)}) collective-permute-start(bf16[256,512]{1,0:T(8,128)(2,1)S(1)} %get-tuple-element.466), channel_id=1, source_target_pairs={{0,0},{1,1},{2,2},{3,3},{4,4},{5,5},{6,6},{7,7},{8,16},{9,17},{10,... | collective-permute-start | bytes 786440 | tf_op jit(solution)/shard_map/ppermute | solution.py:30
  197.8 2.1 collective-permute-start.33
  199.9 3.6 %collective-permute-done.28 = bf16[256,512]{1,0:T(8,128)(2,1)S(1)} collective-permute-done((bf16[256,512]{1,0:T(8,128)(2,1)S(1)}, bf16[256,512]{1,0:T(8,128)(2,1)S(1)}, u32[]{:S(2)}, u32[]{:S(2)}) %collective-permute-start.28) | collective-permute-done | bytes 262176 | tf_op jit(solution)/shard_map/ppermute | solution.py:30
  203.6 8.5 %collective-permute-start.32 = (bf16[256,512]{1,0:T(8,128)(2,1)S(1)}, bf16[256,512]{1,0:T(8,128)(2,1)S(1)}, u32[]{:S(2)}, u32[]{:S(2)}) collective-permute-start(bf16[256,512]{1,0:T(8,128)(2,1)S(1)} %get-tuple-element.462), channel_id=1, source_target_pairs={{0,2},{1,3},{2,0},{3,1},{4,6},{5,7},{6,4},{7,5},{8,18},{9,19},{10,... | collective-permute-start | bytes 786440 | tf_op jit(solution)/shard_map/ppermute | solution.py:30
  212.1 1.5 collective-permute-start.37
  213.9 1.9 collective-permute-start.39
  216.0 13.2 %collective-permute-done.32 = bf16[256,512]{1,0:T(8,128)(2,1)S(1)} collective-permute-done((bf16[256,512]{1,0:T(8,128)(2,1)S(1)}, bf16[256,512]{1,0:T(8,128)(2,1)S(1)}, u32[]{:S(2)}, u32[]{:S(2)}) %collective-permute-start.32) | collective-permute-done | bytes 262176 | tf_op jit(solution)/shard_map/ppermute | solution.py:30
  229.3 1.6 collective-permute-start.34
  230.8 1.9 shard_map.44.outs_0_
  232.7 4.9 %collective-permute-done.39.partner = bf16[2,256,512]{2,1,0:T(8,128)(2,1)S(1)} collective-permute-done((bf16[2,256,512]{2,1,0:T(8,128)(2,1)S(1)}, bf16[2,256,512]{2,1,0:T(8,128)(2,1)S(1)}, u32[]{:S(2)}, u32[]{:S(2)}) %collective-permute-start.39) | collective-permute-done | bytes 524320 | tf_op jit(solution)/shard_map/ppermute | solution.py:34
  237.6 1.9 shard_map.45.outs_0_
  239.5 9.3 %collective-permute-done.38.partner = bf16[2,256,512]{2,1,0:T(8,128)(2,1)S(1)} collective-permute-done((bf16[2,256,512]{2,1,0:T(8,128)(2,1)S(1)}, bf16[2,256,512]{2,1,0:T(8,128)(2,1)S(1)}, u32[]{:S(2)}, u32[]{:S(2)}) %collective-permute-start.38) | collective-permute-done | bytes 524320 | tf_op jit(solution)/shard_map/ppermute | solution.py:34
  248.9 1.9 shard_map.46.outs_0_
  250.7 8.8 %collective-permute-done.34.partner = bf16[2,256,512]{2,1,0:T(8,128)(2,1)S(1)} collective-permute-done((bf16[2,256,512]{2,1,0:T(8,128)(2,1)S(1)}, bf16[2,256,512]{2,1,0:T(8,128)(2,1)S(1)}, u32[]{:S(2)}, u32[]{:S(2)}) %collective-permute-start.34) | collective-permute-done | bytes 524320 | tf_op jit(solution)/shard_map/ppermute | solution.py:34
  259.6 1.9 shard_map.47
  (80 shorter events, 22.3 us)
Async XLA Ops:
  1.4 7.9 %copy-start.5 = (bf16[4,256,512]{2,1,0:T(8,128)(2,1)}, bf16[4,256,512]{2,1,0:T(8,128)(2,1)S(1)}, u32[]{:S(2)}) copy-start(bf16[4,256,512]{2,1,0:T(8,128)(2,1)S(1)} %slice.6) | copy-start | bytes 3145732
  1.4 8.4 %collective-permute-start.9 = (bf16[4,256,512]{2,1,0:T(8,128)(2,1)S(1)}, bf16[4,256,512]{2,1,0:T(8,128)(2,1)S(1)}, u32[]{:S(2)}, u32[]{:S(2)}) collective-permute-start(bf16[4,256,512]{2,1,0:T(8,128)(2,1)S(1)} %slice.6), channel_id=1, source_target_pairs={{0,16},{16,0},{32,48},{48,32},{64,80},{80,64},{96,112},{112,96},{1... | collective-permute-start | bytes 3145736 | tf_op jit(solution)/shard_map/ppermute | solution.py:34
  4.7 2.2 copy-start
  6.9 2.3 copy-start.13
  9.2 11.2 %copy-start.2 = (bf16[3,256,512]{2,1,0:T(8,128)(2,1)}, bf16[3,256,512]{2,1,0:T(8,128)(2,1)S(1)}, u32[]{:S(2)}) copy-start(bf16[3,256,512]{2,1,0:T(8,128)(2,1)S(1)} %get-tuple-element.327) | copy-start | bytes 2359300
  9.4 2.8 %copy-start.7 = (bf16[4,256,512]{2,1,0:T(8,128)(2,1)}, bf16[4,256,512]{2,1,0:T(8,128)(2,1)S(1)}, u32[]{:S(2)}) copy-start(bf16[4,256,512]{2,1,0:T(8,128)(2,1)S(1)} %slice.7) | copy-start | bytes 3145732
  9.4 2.7 %collective-permute-start.8 = (bf16[4,256,512]{2,1,0:T(8,128)(2,1)S(1)}, bf16[4,256,512]{2,1,0:T(8,128)(2,1)S(1)}, u32[]{:S(2)}, u32[]{:S(2)}) collective-permute-start(bf16[4,256,512]{2,1,0:T(8,128)(2,1)S(1)} %slice.7), channel_id=1, source_target_pairs={{0,16},{16,0},{32,48},{48,32},{64,80},{80,64},{96,112},{112,96},{1... | collective-permute-start | bytes 3145736 | tf_op jit(solution)/shard_map/ppermute | solution.py:34
  9.8 7.3 %copy-start.9 = (bf16[4,256,512]{2,1,0:T(8,128)(2,1)}, bf16[4,256,512]{2,1,0:T(8,128)(2,1)S(1)}, u32[]{:S(2)}) copy-start(bf16[4,256,512]{2,1,0:T(8,128)(2,1)S(1)} %collective-permute-done.9) | copy-start | bytes 3145732
  12.1 4.9 %copy-start.11 = (bf16[4,256,512]{2,1,0:T(8,128)(2,1)}, bf16[4,256,512]{2,1,0:T(8,128)(2,1)S(1)}, u32[]{:S(2)}) copy-start(bf16[4,256,512]{2,1,0:T(8,128)(2,1)S(1)} %collective-permute-done.8) | copy-start | bytes 3145732
  12.1 85.7 %collective-permute-start.12 = (bf16[3,256,512]{2,1,0:T(8,128)(2,1)}, bf16[3,256,512]{2,1,0:T(8,128)(2,1)S(1)}, u32[]{:S(2)}, u32[]{:S(2)}) collective-permute-start(bf16[3,256,512]{2,1,0:T(8,128)(2,1)} %get-tuple-element.328), channel_id=1, source_target_pairs={{0,2},{1,3},{2,0},{3,1},{4,6},{5,7},{6,4},{7,5},{8,18},{9,19},{10,... | collective-permute-start | bytes 2359304 | tf_op jit(solution)/shard_map/ppermute | solution.py:30
  17.0 81.7 %collective-permute-start.13 = (bf16[3,256,512]{2,1,0:T(8,128)(2,1)}, bf16[3,256,512]{2,1,0:T(8,128)(2,1)S(1)}, u32[]{:S(2)}, u32[]{:S(2)}) collective-permute-start(bf16[3,256,512]{2,1,0:T(8,128)(2,1)} %get-tuple-element.329), channel_id=1, source_target_pairs={{0,0},{1,1},{2,2},{3,3},{4,4},{5,5},{6,6},{7,7},{8,16},{9,17},{10,... | collective-permute-start | bytes 2359304 | tf_op jit(solution)/shard_map/ppermute | solution.py:30
  20.5 79.3 %collective-permute-start.11 = (bf16[3,256,512]{2,1,0:T(8,128)(2,1)}, bf16[3,256,512]{2,1,0:T(8,128)(2,1)S(1)}, u32[]{:S(2)}, u32[]{:S(2)}) collective-permute-start(bf16[3,256,512]{2,1,0:T(8,128)(2,1)} %copy-done.2), channel_id=1, source_target_pairs={{0,4},{1,5},{2,6},{3,7},{4,0},{5,1},{6,2},{7,3},{8,20},{9,21},{10,... | collective-permute-start | bytes 2359304 | tf_op jit(solution)/shard_map/ppermute | solution.py:30
  23.9 5.6 %copy-start.4 = (bf16[4,4,256,512]{3,2,1,0:T(8,128)(2,1)S(1)}, bf16[4,4,256,512]{3,2,1,0:T(8,128)(2,1)}, u32[]{:S(2)}) copy-start(bf16[4,4,256,512]{3,2,1,0:T(8,128)(2,1)} %get-tuple-element.26.factor) | copy-start | bytes 12582916 | tf_op jit(solution)/shard_map/cond
  23.9 5.6 %copy-start.6 = (bf16[4,256,512]{2,1,0:T(8,128)(2,1)S(1)}, bf16[4,256,512]{2,1,0:T(8,128)(2,1)}, u32[]{:S(2)}) copy-start(bf16[4,256,512]{2,1,0:T(8,128)(2,1)} %get-tuple-element.39.own) | copy-start | bytes 3145732 | tf_op jit(solution)/shard_map/cond
  23.9 5.6 %copy-start.10 = (bf16[4,256,512]{2,1,0:T(8,128)(2,1)S(1)}, bf16[4,256,512]{2,1,0:T(8,128)(2,1)}, u32[]{:S(2)}) copy-start(bf16[4,256,512]{2,1,0:T(8,128)(2,1)} %get-tuple-element.33.partner) | copy-start | bytes 3145732 | tf_op jit(solution)/shard_map/cond
  26.5 4.9 %copy-start.8 = (bf16[4,256,512]{2,1,0:T(8,128)(2,1)S(1)}, bf16[4,256,512]{2,1,0:T(8,128)(2,1)}, u32[]{:S(2)}) copy-start(bf16[4,256,512]{2,1,0:T(8,128)(2,1)} %get-tuple-element.46.own) | copy-start | bytes 3145732 | tf_op jit(solution)/shard_map/cond
  26.5 4.9 %copy-start.12 = (bf16[4,256,512]{2,1,0:T(8,128)(2,1)S(1)}, bf16[4,256,512]{2,1,0:T(8,128)(2,1)}, u32[]{:S(2)}) copy-start(bf16[4,256,512]{2,1,0:T(8,128)(2,1)} %get-tuple-element.43.partner) | copy-start | bytes 3145732 | tf_op jit(solution)/shard_map/cond
  26.5 15.5 %collective-permute-start = (bf16[2,256,512]{2,1,0:T(8,128)(2,1)S(1)}, bf16[2,256,512]{2,1,0:T(8,128)(2,1)S(1)}, u32[]{:S(2)}, u32[]{:S(2)}) collective-permute-start(bf16[2,256,512]{2,1,0:T(8,128)(2,1)S(1)} %branch_1_fun.12.own), channel_id=1, source_target_pairs={{0,32},{16,48},{32,0},{48,16},{64,96},{80,112},{96,64},{112,80},{1... | collective-permute-start | bytes 1572872 | tf_op jit(solution)/shard_map/cond/branch_1_fun/ppermute | solution.py:34
  30.7 16.7 %collective-permute-start.2 = (bf16[2,256,512]{2,1,0:T(8,128)(2,1)S(1)}, bf16[2,256,512]{2,1,0:T(8,128)(2,1)S(1)}, u32[]{:S(2)}, u32[]{:S(2)}) collective-permute-start(bf16[2,256,512]{2,1,0:T(8,128)(2,1)S(1)} %branch_1_fun.13.own), channel_id=1, source_target_pairs={{0,32},{16,48},{32,0},{48,16},{64,96},{80,112},{96,64},{112,80},{1... | collective-permute-start | bytes 1572872 | tf_op jit(solution)/shard_map/cond/branch_1_fun/ppermute | solution.py:34
  43.2 13.2 %collective-permute-start.1 = (bf16[2,256,512]{2,1,0:T(8,128)(2,1)S(1)}, bf16[2,256,512]{2,1,0:T(8,128)(2,1)S(1)}, u32[]{:S(2)}, u32[]{:S(2)}) collective-permute-start(bf16[2,256,512]{2,1,0:T(8,128)(2,1)S(1)} %branch_1_fun.16.own), channel_id=1, source_target_pairs={{0,64},{16,80},{32,96},{48,112},{64,0},{80,16},{96,32},{112,48},{1... | collective-permute-start | bytes 1572872 | tf_op jit(solution)/shard_map/cond/branch_1_fun/ppermute | solution.py:34
  48.6 19.1 %collective-permute-start.3 = (bf16[2,256,512]{2,1,0:T(8,128)(2,1)S(1)}, bf16[2,256,512]{2,1,0:T(8,128)(2,1)S(1)}, u32[]{:S(2)}, u32[]{:S(2)}) collective-permute-start(bf16[2,256,512]{2,1,0:T(8,128)(2,1)S(1)} %branch_1_fun.17.own), channel_id=1, source_target_pairs={{0,64},{16,80},{32,96},{48,112},{64,0},{80,16},{96,32},{112,48},{1... | collective-permute-start | bytes 1572872 | tf_op jit(solution)/shard_map/cond/branch_1_fun/ppermute | solution.py:34
  57.6 18.4 %collective-permute-start.4 = (bf16[2,256,512]{2,1,0:T(8,128)(2,1)S(1)}, bf16[2,256,512]{2,1,0:T(8,128)(2,1)S(1)}, u32[]{:S(2)}, u32[]{:S(2)}) collective-permute-start(bf16[2,256,512]{2,1,0:T(8,128)(2,1)S(1)} %branch_1_fun.18.own), channel_id=1, source_target_pairs={{0,128},{16,144},{32,160},{48,176},{64,192},{80,208},{96,224},{112... | collective-permute-start | bytes 1572872 | tf_op jit(solution)/shard_map/cond/branch_1_fun/ppermute | solution.py:34
  68.8 10.0 %collective-permute-start.6 = (bf16[2,256,512]{2,1,0:T(8,128)(2,1)S(1)}, bf16[2,256,512]{2,1,0:T(8,128)(2,1)S(1)}, u32[]{:S(2)}, u32[]{:S(2)}) collective-permute-start(bf16[2,256,512]{2,1,0:T(8,128)(2,1)S(1)} %branch_1_fun.14.own), channel_id=1, source_target_pairs={{0,32},{16,48},{32,0},{48,16},{64,96},{80,112},{96,64},{112,80},{1... | collective-permute-start | bytes 1572872 | tf_op jit(solution)/shard_map/cond/branch_1_fun/ppermute | solution.py:34
  78.8 10.0 %collective-permute-start.5 = (bf16[2,256,512]{2,1,0:T(8,128)(2,1)S(1)}, bf16[2,256,512]{2,1,0:T(8,128)(2,1)S(1)}, u32[]{:S(2)}, u32[]{:S(2)}) collective-permute-start(bf16[2,256,512]{2,1,0:T(8,128)(2,1)S(1)} %branch_1_fun.19.own), channel_id=1, source_target_pairs={{0,128},{16,144},{32,160},{48,176},{64,192},{80,208},{96,224},{112... | collective-permute-start | bytes 1572872 | tf_op jit(solution)/shard_map/cond/branch_1_fun/ppermute | solution.py:34
  82.4 10.1 %collective-permute-start.7 = (bf16[2,256,512]{2,1,0:T(8,128)(2,1)S(1)}, bf16[2,256,512]{2,1,0:T(8,128)(2,1)S(1)}, u32[]{:S(2)}, u32[]{:S(2)}) collective-permute-start(bf16[2,256,512]{2,1,0:T(8,128)(2,1)S(1)} %branch_1_fun.15.own), channel_id=1, source_target_pairs={{0,32},{16,48},{32,0},{48,16},{64,96},{80,112},{96,64},{112,80},{1... | collective-permute-start | bytes 1572872 | tf_op jit(solution)/shard_map/cond/branch_1_fun/ppermute | solution.py:34
  93.7 24.4 %collective-permute-start.18 = (bf16[3,256,512]{2,1,0:T(8,128)(2,1)S(1)}, bf16[3,256,512]{2,1,0:T(8,128)(2,1)S(1)}, u32[]{:S(2)}, u32[]{:S(2)}) collective-permute-start(bf16[3,256,512]{2,1,0:T(8,128)(2,1)S(1)} %get-tuple-element.353), channel_id=1, source_target_pairs={{0,6},{1,7},{2,4},{3,5},{4,2},{5,3},{6,0},{7,1},{8,22},{9,23},{10,... | collective-permute-start | bytes 2359304 | tf_op jit(solution)/shard_map/ppermute | solution.py:30
  97.2 12.3 %collective-permute-start.10 = (bf16[2,256,512]{2,1,0:T(8,128)(2,1)S(1)}, bf16[2,256,512]{2,1,0:T(8,128)(2,1)S(1)}, u32[]{:S(2)}, u32[]{:S(2)}) collective-permute-start(bf16[2,256,512]{2,1,0:T(8,128)(2,1)S(1)} %get-tuple-element.343.own), channel_id=1, source_target_pairs={{0,64},{16,80},{32,96},{48,112},{64,0},{80,16},{96,32},{112,48},{1... | collective-permute-start | bytes 1572872 | tf_op jit(solution)/shard_map/ppermute | solution.py:34
  97.8 22.4 %collective-permute-start.16 = (bf16[2,256,512]{2,1,0:T(8,128)(2,1)S(1)}, bf16[2,256,512]{2,1,0:T(8,128)(2,1)S(1)}, u32[]{:S(2)}, u32[]{:S(2)}) collective-permute-start(bf16[2,256,512]{2,1,0:T(8,128)(2,1)S(1)} %get-tuple-element.360.own), channel_id=1, source_target_pairs={{0,64},{16,80},{32,96},{48,112},{64,0},{80,16},{96,32},{112,48},{1... | collective-permute-start | bytes 1572872 | tf_op jit(solution)/shard_map/ppermute | solution.py:34
  98.7 21.6 %copy-start.3 = (bf16[4,4,1,1,256,512]{5,4,3,2,1,0:T(8,128)(2,1)S(1)}, bf16[4,4,1,1,256,512]{5,4,3,2,1,0:T(8,128)(2,1)}, u32[]{:S(2)}) copy-start(bf16[4,4,1,1,256,512]{5,4,3,2,1,0:T(8,128)(2,1)} %param.6) | copy-start | bytes 12582916
  98.7 21.5 %collective-permute-start.17 = (bf16[256,512]{1,0:T(8,128)(2,1)S(1)}, bf16[256,512]{1,0:T(8,128)(2,1)S(1)}, u32[]{:S(2)}, u32[]{:S(2)}) collective-permute-start(bf16[256,512]{1,0:T(8,128)(2,1)S(1)} %get-tuple-element.351), channel_id=1, source_target_pairs={{0,4},{1,5},{2,6},{3,7},{4,0},{5,1},{6,2},{7,3},{8,20},{9,21},{10,... | collective-permute-start | bytes 786440 | tf_op jit(solution)/shard_map/ppermute | solution.py:30
  118.1 20.6 %collective-permute-start.14 = (bf16[2,256,512]{2,1,0:T(8,128)(2,1)S(1)}, bf16[2,256,512]{2,1,0:T(8,128)(2,1)S(1)}, u32[]{:S(2)}, u32[]{:S(2)}) collective-permute-start(bf16[2,256,512]{2,1,0:T(8,128)(2,1)S(1)} %shard_map.38.own), channel_id=1, source_target_pairs={{0,128},{16,144},{32,160},{48,176},{64,192},{80,208},{96,224},{112... | collective-permute-start | bytes 1572872 | tf_op jit(solution)/shard_map/ppermute | solution.py:34
  121.4 23.0 %collective-permute-start.22 = (bf16[2,256,512]{2,1,0:T(8,128)(2,1)S(1)}, bf16[2,256,512]{2,1,0:T(8,128)(2,1)S(1)}, u32[]{:S(2)}, u32[]{:S(2)}) collective-permute-start(bf16[2,256,512]{2,1,0:T(8,128)(2,1)S(1)} %shard_map.39.own), channel_id=1, source_target_pairs={{0,128},{16,144},{32,160},{48,176},{64,192},{80,208},{96,224},{112... | collective-permute-start | bytes 1572872 | tf_op jit(solution)/shard_map/ppermute | solution.py:34
  124.2 14.5 %collective-permute-start.15 = (bf16[256,512]{1,0:T(8,128)(2,1)S(1)}, bf16[256,512]{1,0:T(8,128)(2,1)S(1)}, u32[]{:S(2)}, u32[]{:S(2)}) collective-permute-start(bf16[256,512]{1,0:T(8,128)(2,1)S(1)} %get-tuple-element.348), channel_id=1, source_target_pairs={{0,0},{1,1},{2,2},{3,3},{4,4},{5,5},{6,6},{7,7},{8,16},{9,17},{10,... | collective-permute-start | bytes 786440 | tf_op jit(solution)/shard_map/ppermute | solution.py:30
  129.2 15.3 %collective-permute-start.20 = (bf16[256,512]{1,0:T(8,128)(2,1)S(1)}, bf16[256,512]{1,0:T(8,128)(2,1)S(1)}, u32[]{:S(2)}, u32[]{:S(2)}) collective-permute-start(bf16[256,512]{1,0:T(8,128)(2,1)S(1)} %get-tuple-element.375), channel_id=1, source_target_pairs={{0,2},{1,3},{2,0},{3,1},{4,6},{5,7},{6,4},{7,5},{8,18},{9,19},{10,... | collective-permute-start | bytes 786440 | tf_op jit(solution)/shard_map/ppermute | solution.py:30
  130.3 17.5 %collective-permute-start.21 = (bf16[256,512]{1,0:T(8,128)(2,1)S(1)}, bf16[256,512]{1,0:T(8,128)(2,1)S(1)}, u32[]{:S(2)}, u32[]{:S(2)}) collective-permute-start(bf16[256,512]{1,0:T(8,128)(2,1)S(1)} %get-tuple-element.379), channel_id=1, source_target_pairs={{0,6},{1,7},{2,4},{3,5},{4,2},{5,3},{6,0},{7,1},{8,22},{9,23},{10,... | collective-permute-start | bytes 786440 | tf_op jit(solution)/shard_map/ppermute | solution.py:30
  148.0 10.9 %collective-permute-start.23 = (bf16[4,256,512]{2,1,0:T(8,128)(2,1)S(1)}, bf16[4,256,512]{2,1,0:T(8,128)(2,1)S(1)}, u32[]{:S(2)}, u32[]{:S(2)}) collective-permute-start(bf16[4,256,512]{2,1,0:T(8,128)(2,1)S(1)} %pad_maximum_fusion.own), channel_id=1, source_target_pairs={{0,16},{16,0},{32,48},{48,32},{64,80},{80,64},{96,112},{112,96},{1... | collective-permute-start | bytes 3145736 | tf_op jit(solution)/shard_map/ppermute | solution.py:34
  148.1 13.2 %collective-permute-start.24 = (bf16[256,512]{1,0:T(8,128)(2,1)S(1)}, bf16[256,512]{1,0:T(8,128)(2,1)S(1)}, u32[]{:S(2)}, u32[]{:S(2)}) collective-permute-start(bf16[256,512]{1,0:T(8,128)(2,1)S(1)} %get-tuple-element.413), channel_id=1, source_target_pairs={{0,4},{1,5},{2,6},{3,7},{4,0},{5,1},{6,2},{7,3},{8,20},{9,21},{10,... | collective-permute-start | bytes 786440 | tf_op jit(solution)/shard_map/ppermute | solution.py:30
  151.1 14.9 %collective-permute-start.19 = (bf16[256,512]{1,0:T(8,128)(2,1)S(1)}, bf16[256,512]{1,0:T(8,128)(2,1)S(1)}, u32[]{:S(2)}, u32[]{:S(2)}) collective-permute-start(bf16[256,512]{1,0:T(8,128)(2,1)S(1)} %get-tuple-element.373), channel_id=1, source_target_pairs={{0,0},{1,1},{2,2},{3,3},{4,4},{5,5},{6,6},{7,7},{8,16},{9,17},{10,... | collective-permute-start | bytes 786440 | tf_op jit(solution)/shard_map/ppermute | solution.py:30
  154.6 22.1 %collective-permute-start.25 = (bf16[256,512]{1,0:T(8,128)(2,1)S(1)}, bf16[256,512]{1,0:T(8,128)(2,1)S(1)}, u32[]{:S(2)}, u32[]{:S(2)}) collective-permute-start(bf16[256,512]{1,0:T(8,128)(2,1)S(1)} %get-tuple-element.420), channel_id=1, source_target_pairs={{0,2},{1,3},{2,0},{3,1},{4,6},{5,7},{6,4},{7,5},{8,18},{9,19},{10,... | collective-permute-start | bytes 786440 | tf_op jit(solution)/shard_map/ppermute | solution.py:30
  158.9 18.1 %collective-permute-start.26 = (bf16[256,512]{1,0:T(8,128)(2,1)S(1)}, bf16[256,512]{1,0:T(8,128)(2,1)S(1)}, u32[]{:S(2)}, u32[]{:S(2)}) collective-permute-start(bf16[256,512]{1,0:T(8,128)(2,1)S(1)} %get-tuple-element.424), channel_id=1, source_target_pairs={{0,6},{1,7},{2,4},{3,5},{4,2},{5,3},{6,0},{7,1},{8,22},{9,23},{10,... | collective-permute-start | bytes 786440 | tf_op jit(solution)/shard_map/ppermute | solution.py:30
  177.1 11.2 %collective-permute-start.29 = (bf16[4,256,512]{2,1,0:T(8,128)(2,1)S(1)}, bf16[4,256,512]{2,1,0:T(8,128)(2,1)S(1)}, u32[]{:S(2)}, u32[]{:S(2)}) collective-permute-start(bf16[4,256,512]{2,1,0:T(8,128)(2,1)S(1)} %pad_maximum_fusion.1.own), channel_id=1, source_target_pairs={{0,16},{16,0},{32,48},{48,32},{64,80},{80,64},{96,112},{112,96},{1... | collective-permute-start | bytes 3145736 | tf_op jit(solution)/shard_map/ppermute | solution.py:34
  177.2 16.3 %collective-permute-start.31 = (bf16[256,512]{1,0:T(8,128)(2,1)S(1)}, bf16[256,512]{1,0:T(8,128)(2,1)S(1)}, u32[]{:S(2)}, u32[]{:S(2)}) collective-permute-start(bf16[256,512]{1,0:T(8,128)(2,1)S(1)} %get-tuple-element.457), channel_id=1, source_target_pairs={{0,6},{1,7},{2,4},{3,5},{4,2},{5,3},{6,0},{7,1},{8,22},{9,23},{10,... | collective-permute-start | bytes 786440 | tf_op jit(solution)/shard_map/ppermute | solution.py:30
  180.7 17.2 %collective-permute-start.30 = (bf16[256,512]{1,0:T(8,128)(2,1)S(1)}, bf16[256,512]{1,0:T(8,128)(2,1)S(1)}, u32[]{:S(2)}, u32[]{:S(2)}) collective-permute-start(bf16[256,512]{1,0:T(8,128)(2,1)S(1)} %get-tuple-element.450), channel_id=1, source_target_pairs={{0,2},{1,3},{2,0},{3,1},{4,6},{5,7},{6,4},{7,5},{8,18},{9,19},{10,... | collective-permute-start | bytes 786440 | tf_op jit(solution)/shard_map/ppermute | solution.py:30
  180.7 22.9 %collective-permute-start.28 = (bf16[256,512]{1,0:T(8,128)(2,1)S(1)}, bf16[256,512]{1,0:T(8,128)(2,1)S(1)}, u32[]{:S(2)}, u32[]{:S(2)}) collective-permute-start(bf16[256,512]{1,0:T(8,128)(2,1)S(1)} %get-tuple-element.431), channel_id=1, source_target_pairs={{0,4},{1,5},{2,6},{3,7},{4,0},{5,1},{6,2},{7,3},{8,20},{9,21},{10,... | collective-permute-start | bytes 786440 | tf_op jit(solution)/shard_map/ppermute | solution.py:30
  185.0 27.0 %collective-permute-start.27 = (bf16[256,512]{1,0:T(8,128)(2,1)S(1)}, bf16[256,512]{1,0:T(8,128)(2,1)S(1)}, u32[]{:S(2)}, u32[]{:S(2)}) collective-permute-start(bf16[256,512]{1,0:T(8,128)(2,1)S(1)} %get-tuple-element.429), channel_id=1, source_target_pairs={{0,0},{1,1},{2,2},{3,3},{4,4},{5,5},{6,6},{7,7},{8,16},{9,17},{10,... | collective-permute-start | bytes 786440 | tf_op jit(solution)/shard_map/ppermute | solution.py:30
  190.7 23.2 %collective-permute-start.36 = (bf16[256,512]{1,0:T(8,128)(2,1)S(1)}, bf16[256,512]{1,0:T(8,128)(2,1)S(1)}, u32[]{:S(2)}, u32[]{:S(2)}) collective-permute-start(bf16[256,512]{1,0:T(8,128)(2,1)S(1)} %get-tuple-element.467), channel_id=1, source_target_pairs={{0,4},{1,5},{2,6},{3,7},{4,0},{5,1},{6,2},{7,3},{8,20},{9,21},{10,... | collective-permute-start | bytes 786440 | tf_op jit(solution)/shard_map/ppermute | solution.py:30
  193.6 22.3 %collective-permute-start.35 = (bf16[256,512]{1,0:T(8,128)(2,1)S(1)}, bf16[256,512]{1,0:T(8,128)(2,1)S(1)}, u32[]{:S(2)}, u32[]{:S(2)}) collective-permute-start(bf16[256,512]{1,0:T(8,128)(2,1)S(1)} %get-tuple-element.466), channel_id=1, source_target_pairs={{0,0},{1,1},{2,2},{3,3},{4,4},{5,5},{6,6},{7,7},{8,16},{9,17},{10,... | collective-permute-start | bytes 786440 | tf_op jit(solution)/shard_map/ppermute | solution.py:30
  197.8 18.2 %collective-permute-start.33 = (bf16[256,512]{1,0:T(8,128)(2,1)S(1)}, bf16[256,512]{1,0:T(8,128)(2,1)S(1)}, u32[]{:S(2)}, u32[]{:S(2)}) collective-permute-start(bf16[256,512]{1,0:T(8,128)(2,1)S(1)} %get-tuple-element.465), channel_id=1, source_target_pairs={{0,6},{1,7},{2,4},{3,5},{4,2},{5,3},{6,0},{7,1},{8,22},{9,23},{10,... | collective-permute-start | bytes 786440 | tf_op jit(solution)/shard_map/ppermute | solution.py:30
  203.6 25.7 %collective-permute-start.32 = (bf16[256,512]{1,0:T(8,128)(2,1)S(1)}, bf16[256,512]{1,0:T(8,128)(2,1)S(1)}, u32[]{:S(2)}, u32[]{:S(2)}) collective-permute-start(bf16[256,512]{1,0:T(8,128)(2,1)S(1)} %get-tuple-element.462), channel_id=1, source_target_pairs={{0,2},{1,3},{2,0},{3,1},{4,6},{5,7},{6,4},{7,5},{8,18},{9,19},{10,... | collective-permute-start | bytes 786440 | tf_op jit(solution)/shard_map/ppermute | solution.py:30
  212.0 18.8 %copy-start.1 = (bf16[4,4,1,1,256,512]{5,4,3,2,1,0:T(8,128)(2,1)S(1)}, bf16[4,4,1,1,256,512]{5,4,3,2,1,0:T(8,128)(2,1)}, u32[]{:S(2)}) copy-start(bf16[4,4,1,1,256,512]{5,4,3,2,1,0:T(8,128)(2,1)} %param.7) | copy-start | bytes 12582916
  212.1 18.7 %collective-permute-start.37 = (bf16[2,256,512]{2,1,0:T(8,128)(2,1)S(1)}, bf16[2,256,512]{2,1,0:T(8,128)(2,1)S(1)}, u32[]{:S(2)}, u32[]{:S(2)}) collective-permute-start(bf16[2,256,512]{2,1,0:T(8,128)(2,1)S(1)} %pad_maximum_fusion.5.own), channel_id=1, source_target_pairs={{0,1},{1,0},{2,3},{3,2},{4,5},{5,4},{6,7},{7,6},{8,9},{9,8},{10,11... | collective-permute-start | bytes 1572872 | tf_op jit(solution)/shard_map/ppermute | solution.py:34
  213.9 23.7 %collective-permute-start.39 = (bf16[2,256,512]{2,1,0:T(8,128)(2,1)S(1)}, bf16[2,256,512]{2,1,0:T(8,128)(2,1)S(1)}, u32[]{:S(2)}, u32[]{:S(2)}) collective-permute-start(bf16[2,256,512]{2,1,0:T(8,128)(2,1)S(1)} %pad_maximum_fusion.4.own), channel_id=1, source_target_pairs={{0,1},{1,0},{2,3},{3,2},{4,5},{5,4},{6,7},{7,6},{8,9},{9,8},{10,11... | collective-permute-start | bytes 1572872 | tf_op jit(solution)/shard_map/ppermute | solution.py:34
  215.9 32.9 %collective-permute-start.38 = (bf16[2,256,512]{2,1,0:T(8,128)(2,1)S(1)}, bf16[2,256,512]{2,1,0:T(8,128)(2,1)S(1)}, u32[]{:S(2)}, u32[]{:S(2)}) collective-permute-start(bf16[2,256,512]{2,1,0:T(8,128)(2,1)S(1)} %pad_maximum_fusion.3.own), channel_id=1, source_target_pairs={{0,1},{1,0},{2,3},{3,2},{4,5},{5,4},{6,7},{7,6},{8,9},{9,8},{10,11... | collective-permute-start | bytes 1572872 | tf_op jit(solution)/shard_map/ppermute | solution.py:34
  229.3 30.3 %collective-permute-start.34 = (bf16[2,256,512]{2,1,0:T(8,128)(2,1)S(1)}, bf16[2,256,512]{2,1,0:T(8,128)(2,1)S(1)}, u32[]{:S(2)}, u32[]{:S(2)}) collective-permute-start(bf16[2,256,512]{2,1,0:T(8,128)(2,1)S(1)} %pad_maximum_fusion.2.own), channel_id=1, source_target_pairs={{0,1},{1,0},{2,3},{3,2},{4,5},{5,4},{6,7},{7,6},{8,9},{9,8},{10,11... | collective-permute-start | bytes 1572872 | tf_op jit(solution)/shard_map/ppermute | solution.py:34

commit v5 on v4

--- a/solution.py
+++ b/solution.py
@@ -260,10 +260,10 @@
     o.done("back", 1, 0)
     o.done("back", 3, 0)
     o.start("dsend", 1, 0)
+    o.done("dsend", 0, 0)
+    o.work("last", 0, 0)
     o.start("back", 1, 1)
     o.start("back", 3, 1)
-    o.done("dsend", 0, 0)
-    o.work("last", 0, 0)
     o.done("back", 2, 1)
     o.done("back", 0, 1)
     o.start("dsend", 0, 1)

time: 262 us -> 262 us (level)
  no operation moved by 1% of the time
where the time goes in v5:
time: 262 us; the launch traced here: 261 us
  waiting for transfers between devices  125 us (48%)
  starting transfers between devices  95.8 us (37%)
  Pallas kernels  36.1 us (14%)
  local copies, waits for them, and re-layouts  3.64 us (1%)
    ppermute x20, waiting for transfers between devices, exchange(): return lax.ppermute(value, axis, [(d, d ^ mask) for d in range(16)])  71.1 us
    ppermute x20, starting transfers between devices, swap(): return lax.ppermute(value, ('leaf', 'wide'), SWAPS[step])  64.2 us
    ppermute x20, waiting for transfers between devices, swap(): return lax.ppermute(value, ('leaf', 'wide'), SWAPS[step])  53.8 us
    ppermute x20, starting transfers between devices, exchange(): return lax.ppermute(value, axis, [(d, d ^ mask) for d in range(16)])  31.6 us
    pallas_call x20, Pallas kernels, level_call(): pl.pallas_call(functools.partial(level_body, split), grid_spec=pltpu.Pref...  29 us
  transfers between devices with their start and end apart: 40, of which 25 were waited for; matrix products, arithmetic and copies ran while one was open for 0% of the time, Pallas kernels for 13%

profile of v5, /device:TPU:1, one launch (start us, length us, event | category | flops | bytes accessed | tf_op | source)
XLA Modules:
  0.0 261.5 jit_solution(18368843746931729906)
XLA Ops:
  0.1 1.3 slice.6
  1.4 3.3 %collective-permute-start.9 = (bf16[4,256,512]{2,1,0:T(8,128)(2,1)S(1)}, bf16[4,256,512]{2,1,0:T(8,128)(2,1)S(1)}, u32[]{:S(2)}, u32[]{:S(2)}) collective-permute-start(bf16[4,256,512]{2,1,0:T(8,128)(2,1)S(1)} %slice.6), channel_id=1, source_target_pairs={{0,16},{16,0},{32,48},{48,32},{64,80},{80,64},{96,112},{112,96},{1... | collective-permute-start | bytes 3145736 | tf_op jit(solution)/shard_map/ppermute | solution.py:34
  4.7 2.2 copy-done
  6.9 2.3 shard_map.37
  9.8 2.4 collective-permute-done.8
  12.1 4.9 %collective-permute-start.12 = (bf16[3,256,512]{2,1,0:T(8,128)(2,1)}, bf16[3,256,512]{2,1,0:T(8,128)(2,1)S(1)}, u32[]{:S(2)}, u32[]{:S(2)}) collective-permute-start(bf16[3,256,512]{2,1,0:T(8,128)(2,1)} %get-tuple-element.328), channel_id=1, source_target_pairs={{0,2},{1,3},{2,0},{3,1},{4,6},{5,7},{6,4},{7,5},{8,18},{9,19},{10,... | collective-permute-start | bytes 2359304 | tf_op jit(solution)/shard_map/ppermute | solution.py:30
  17.0 3.3 %collective-permute-start.13 = (bf16[3,256,512]{2,1,0:T(8,128)(2,1)}, bf16[3,256,512]{2,1,0:T(8,128)(2,1)S(1)}, u32[]{:S(2)}, u32[]{:S(2)}) collective-permute-start(bf16[3,256,512]{2,1,0:T(8,128)(2,1)} %get-tuple-element.329), channel_id=1, source_target_pairs={{0,0},{1,1},{2,2},{3,3},{4,4},{5,5},{6,6},{7,7},{8,16},{9,17},{10,... | collective-permute-start | bytes 2359304 | tf_op jit(solution)/shard_map/ppermute | solution.py:30
  20.5 3.4 %collective-permute-start.11 = (bf16[3,256,512]{2,1,0:T(8,128)(2,1)}, bf16[3,256,512]{2,1,0:T(8,128)(2,1)S(1)}, u32[]{:S(2)}, u32[]{:S(2)}) collective-permute-start(bf16[3,256,512]{2,1,0:T(8,128)(2,1)} %copy-done.2), channel_id=1, source_target_pairs={{0,4},{1,5},{2,6},{3,7},{4,0},{5,1},{6,2},{7,3},{8,20},{9,21},{10,... | collective-permute-start | bytes 2359304 | tf_op jit(solution)/shard_map/ppermute | solution.py:30
  23.9 69.8 %conditional.1 = (bf16[256,512]{1,0:T(8,128)(2,1)S(1)}, bf16[256,512]{1,0:T(8,128)(2,1)S(1)}, bf16[256,512]{1,0:T(8,128)(2,1)S(1)}, bf16[256,512]{1,0:T(8,128)(2...) conditional(s32[]{:T(128)} %convert_element_type.3, () %tuple.134, ...), branch_computations={%region_0.0_spmd, %region_1.0_spmd} | conditional | flops 12 | bytes 50332180 | solution.py:284
  23.9 2.6 branch_1_fun.12.own
  26.5 3.0 %collective-permute-start = (bf16[2,256,512]{2,1,0:T(8,128)(2,1)S(1)}, bf16[2,256,512]{2,1,0:T(8,128)(2,1)S(1)}, u32[]{:S(2)}, u32[]{:S(2)}) collective-permute-start(bf16[2,256,512]{2,1,0:T(8,128)(2,1)S(1)} %branch_1_fun.12.own), channel_id=1, source_target_pairs={{0,32},{16,48},{32,0},{48,16},{64,96},{80,112},{96,64},{112,80},{1... | collective-permute-start | bytes 1572872 | tf_op jit(solution)/shard_map/cond/branch_1_fun/ppermute | solution.py:34
  33.7 8.3 %collective-permute-done.partner = bf16[2,256,512]{2,1,0:T(8,128)(2,1)S(1)} collective-permute-done((bf16[2,256,512]{2,1,0:T(8,128)(2,1)S(1)}, bf16[2,256,512]{2,1,0:T(8,128)(2,1)S(1)}, u32[]{:S(2)}, u32[]{:S(2)}) %collective-permute-start) | collective-permute-done | bytes 524320 | tf_op jit(solution)/shard_map/cond/branch_1_fun/ppermute | solution.py:34
  43.2 1.3 collective-permute-start.1
  44.5 2.9 %collective-permute-done.2.partner = bf16[2,256,512]{2,1,0:T(8,128)(2,1)S(1)} collective-permute-done((bf16[2,256,512]{2,1,0:T(8,128)(2,1)S(1)}, bf16[2,256,512]{2,1,0:T(8,128)(2,1)S(1)}, u32[]{:S(2)}, u32[]{:S(2)}) %collective-permute-start.2) | collective-permute-done | bytes 524320 | tf_op jit(solution)/shard_map/cond/branch_1_fun/ppermute | solution.py:34
  48.6 1.3 collective-permute-start.3
  49.9 6.5 %collective-permute-done.1.partner = bf16[2,256,512]{2,1,0:T(8,128)(2,1)S(1)} collective-permute-done((bf16[2,256,512]{2,1,0:T(8,128)(2,1)S(1)}, bf16[2,256,512]{2,1,0:T(8,128)(2,1)S(1)}, u32[]{:S(2)}, u32[]{:S(2)}) %collective-permute-start.1) | collective-permute-done | bytes 524320 | tf_op jit(solution)/shard_map/cond/branch_1_fun/ppermute | solution.py:34
  57.6 2.8 %collective-permute-start.4 = (bf16[2,256,512]{2,1,0:T(8,128)(2,1)S(1)}, bf16[2,256,512]{2,1,0:T(8,128)(2,1)S(1)}, u32[]{:S(2)}, u32[]{:S(2)}) collective-permute-start(bf16[2,256,512]{2,1,0:T(8,128)(2,1)S(1)} %branch_1_fun.18.own), channel_id=1, source_target_pairs={{0,128},{16,144},{32,160},{48,176},{64,192},{80,208},{96,224},{112... | collective-permute-start | bytes 1572872 | tf_op jit(solution)/shard_map/cond/branch_1_fun/ppermute | solution.py:34
  60.4 7.2 %collective-permute-done.3.partner = bf16[2,256,512]{2,1,0:T(8,128)(2,1)S(1)} collective-permute-done((bf16[2,256,512]{2,1,0:T(8,128)(2,1)S(1)}, bf16[2,256,512]{2,1,0:T(8,128)(2,1)S(1)}, u32[]{:S(2)}, u32[]{:S(2)}) %collective-permute-start.3) | collective-permute-done | bytes 524320 | tf_op jit(solution)/shard_map/cond/branch_1_fun/ppermute | solution.py:34
  68.8 3.1 %collective-permute-start.6 = (bf16[2,256,512]{2,1,0:T(8,128)(2,1)S(1)}, bf16[2,256,512]{2,1,0:T(8,128)(2,1)S(1)}, u32[]{:S(2)}, u32[]{:S(2)}) collective-permute-start(bf16[2,256,512]{2,1,0:T(8,128)(2,1)S(1)} %branch_1_fun.14.own), channel_id=1, source_target_pairs={{0,32},{16,48},{32,0},{48,16},{64,96},{80,112},{96,64},{112,80},{1... | collective-permute-start | bytes 1572872 | tf_op jit(solution)/shard_map/cond/branch_1_fun/ppermute | solution.py:34
  71.9 4.1 %collective-permute-done.4.partner = bf16[2,256,512]{2,1,0:T(8,128)(2,1)S(1)} collective-permute-done((bf16[2,256,512]{2,1,0:T(8,128)(2,1)S(1)}, bf16[2,256,512]{2,1,0:T(8,128)(2,1)S(1)}, u32[]{:S(2)}, u32[]{:S(2)}) %collective-permute-start.4) | collective-permute-done | bytes 524320 | tf_op jit(solution)/shard_map/cond/branch_1_fun/ppermute | solution.py:34
  77.2 1.6 collective-permute-done.6.partner
  78.8 2.4 collective-permute-start.5
  82.4 3.3 %collective-permute-start.7 = (bf16[2,256,512]{2,1,0:T(8,128)(2,1)S(1)}, bf16[2,256,512]{2,1,0:T(8,128)(2,1)S(1)}, u32[]{:S(2)}, u32[]{:S(2)}) collective-permute-start(bf16[2,256,512]{2,1,0:T(8,128)(2,1)S(1)} %branch_1_fun.15.own), channel_id=1, source_target_pairs={{0,32},{16,48},{32,0},{48,16},{64,96},{80,112},{96,64},{112,80},{1... | collective-permute-start | bytes 1572872 | tf_op jit(solution)/shard_map/cond/branch_1_fun/ppermute | solution.py:34
  85.8 3.1 %collective-permute-done.5.partner = bf16[2,256,512]{2,1,0:T(8,128)(2,1)S(1)} collective-permute-done((bf16[2,256,512]{2,1,0:T(8,128)(2,1)S(1)}, bf16[2,256,512]{2,1,0:T(8,128)(2,1)S(1)}, u32[]{:S(2)}, u32[]{:S(2)}) %collective-permute-start.5) | collective-permute-done | bytes 524320 | tf_op jit(solution)/shard_map/cond/branch_1_fun/ppermute | solution.py:34
  88.8 1.2 branch_1_fun.22
  90.1 2.4 collective-permute-done.7.partner
  93.7 3.5 %collective-permute-start.18 = (bf16[3,256,512]{2,1,0:T(8,128)(2,1)S(1)}, bf16[3,256,512]{2,1,0:T(8,128)(2,1)S(1)}, u32[]{:S(2)}, u32[]{:S(2)}) collective-permute-start(bf16[3,256,512]{2,1,0:T(8,128)(2,1)S(1)} %get-tuple-element.353), channel_id=1, source_target_pairs={{0,6},{1,7},{2,4},{3,5},{4,2},{5,3},{6,0},{7,1},{8,22},{9,23},{10,... | collective-permute-start | bytes 2359304 | tf_op jit(solution)/shard_map/ppermute | solution.py:30
  99.8 9.7 %collective-permute-done.10.partner = bf16[2,256,512]{2,1,0:T(8,128)(2,1)S(1)} collective-permute-done((bf16[2,256,512]{2,1,0:T(8,128)(2,1)S(1)}, bf16[2,256,512]{2,1,0:T(8,128)(2,1)S(1)}, u32[]{:S(2)}, u32[]{:S(2)}) %collective-permute-start.10) | collective-permute-done | bytes 524320 | tf_op jit(solution)/shard_map/ppermute | solution.py:34
  109.5 2.1 shard_map.38.own
  111.6 6.5 %collective-permute-done.18.refs_3_ = bf16[3,256,512]{2,1,0:T(8,128)(2,1)S(1)} collective-permute-done((bf16[3,256,512]{2,1,0:T(8,128)(2,1)S(1)}, bf16[3,256,512]{2,1,0:T(8,128)(2,1)S(1)}, u32[]{:S(2)}, u32[]{:S(2)}) %collective-permute-start.18) | collective-permute-done | bytes 786464 | tf_op jit(solution)/shard_map/ppermute | solution.py:30
  118.7 1.6 collective-permute-done.17
  121.4 2.7 %collective-permute-start.22 = (bf16[2,256,512]{2,1,0:T(8,128)(2,1)S(1)}, bf16[2,256,512]{2,1,0:T(8,128)(2,1)S(1)}, u32[]{:S(2)}, u32[]{:S(2)}) collective-permute-start(bf16[2,256,512]{2,1,0:T(8,128)(2,1)S(1)} %shard_map.39.own), channel_id=1, source_target_pairs={{0,128},{16,144},{32,160},{48,176},{64,192},{80,208},{96,224},{112... | collective-permute-start | bytes 1572872 | tf_op jit(solution)/shard_map/ppermute | solution.py:34
  124.2 5.0 %collective-permute-start.15 = (bf16[256,512]{1,0:T(8,128)(2,1)S(1)}, bf16[256,512]{1,0:T(8,128)(2,1)S(1)}, u32[]{:S(2)}, u32[]{:S(2)}) collective-permute-start(bf16[256,512]{1,0:T(8,128)(2,1)S(1)} %get-tuple-element.348), channel_id=1, source_target_pairs={{0,0},{1,1},{2,2},{3,3},{4,4},{5,5},{6,6},{7,7},{8,16},{9,17},{10,... | collective-permute-start | bytes 786440 | tf_op jit(solution)/shard_map/ppermute | solution.py:30
  130.3 3.1 %collective-permute-start.21 = (bf16[256,512]{1,0:T(8,128)(2,1)S(1)}, bf16[256,512]{1,0:T(8,128)(2,1)S(1)}, u32[]{:S(2)}, u32[]{:S(2)}) collective-permute-start(bf16[256,512]{1,0:T(8,128)(2,1)S(1)} %get-tuple-element.379), channel_id=1, source_target_pairs={{0,6},{1,7},{2,4},{3,5},{4,2},{5,3},{6,0},{7,1},{8,22},{9,23},{10,... | collective-permute-start | bytes 786440 | tf_op jit(solution)/shard_map/ppermute | solution.py:30
  133.4 5.3 %collective-permute-done.15 = bf16[256,512]{1,0:T(8,128)(2,1)S(1)} collective-permute-done((bf16[256,512]{1,0:T(8,128)(2,1)S(1)}, bf16[256,512]{1,0:T(8,128)(2,1)S(1)}, u32[]{:S(2)}, u32[]{:S(2)}) %collective-permute-start.15) | collective-permute-done | bytes 262176 | tf_op jit(solution)/shard_map/ppermute | solution.py:30
  138.7 1.2 shard_map.40
  140.0 4.5 %collective-permute-done.20 = bf16[256,512]{1,0:T(8,128)(2,1)S(1)} collective-permute-done((bf16[256,512]{1,0:T(8,128)(2,1)S(1)}, bf16[256,512]{1,0:T(8,128)(2,1)S(1)}, u32[]{:S(2)}, u32[]{:S(2)}) %collective-permute-start.20) | collective-permute-done | bytes 262176 | tf_op jit(solution)/shard_map/ppermute | solution.py:30
  145.7 2.2 collective-permute-done.21
  148.1 3.0 %collective-permute-start.24 = (bf16[256,512]{1,0:T(8,128)(2,1)S(1)}, bf16[256,512]{1,0:T(8,128)(2,1)S(1)}, u32[]{:S(2)}, u32[]{:S(2)}) collective-permute-start(bf16[256,512]{1,0:T(8,128)(2,1)S(1)} %get-tuple-element.413), channel_id=1, source_target_pairs={{0,4},{1,5},{2,6},{3,7},{4,0},{5,1},{6,2},{7,3},{8,20},{9,21},{10,... | collective-permute-start | bytes 786440 | tf_op jit(solution)/shard_map/ppermute | solution.py:30
  151.1 3.5 %collective-permute-start.19 = (bf16[256,512]{1,0:T(8,128)(2,1)S(1)}, bf16[256,512]{1,0:T(8,128)(2,1)S(1)}, u32[]{:S(2)}, u32[]{:S(2)}) collective-permute-start(bf16[256,512]{1,0:T(8,128)(2,1)S(1)} %get-tuple-element.373), channel_id=1, source_target_pairs={{0,0},{1,1},{2,2},{3,3},{4,4},{5,5},{6,6},{7,7},{8,16},{9,17},{10,... | collective-permute-start | bytes 786440 | tf_op jit(solution)/shard_map/ppermute | solution.py:30
  154.6 4.4 %collective-permute-start.25 = (bf16[256,512]{1,0:T(8,128)(2,1)S(1)}, bf16[256,512]{1,0:T(8,128)(2,1)S(1)}, u32[]{:S(2)}, u32[]{:S(2)}) collective-permute-start(bf16[256,512]{1,0:T(8,128)(2,1)S(1)} %get-tuple-element.420), channel_id=1, source_target_pairs={{0,2},{1,3},{2,0},{3,1},{4,6},{5,7},{6,4},{7,5},{8,18},{9,19},{10,... | collective-permute-start | bytes 786440 | tf_op jit(solution)/shard_map/ppermute | solution.py:30
  158.9 2.4 shard_map.42
  161.3 4.7 %collective-permute-done.19 = bf16[256,512]{1,0:T(8,128)(2,1)S(1)} collective-permute-done((bf16[256,512]{1,0:T(8,128)(2,1)S(1)}, bf16[256,512]{1,0:T(8,128)(2,1)S(1)}, u32[]{:S(2)}, u32[]{:S(2)}) %collective-permute-start.19) | collective-permute-done | bytes 262176 | tf_op jit(solution)/shard_map/ppermute | solution.py:30
  166.0 10.7 %collective-permute-done.25 = bf16[256,512]{1,0:T(8,128)(2,1)S(1)} collective-permute-done((bf16[256,512]{1,0:T(8,128)(2,1)S(1)}, bf16[256,512]{1,0:T(8,128)(2,1)S(1)}, u32[]{:S(2)}, u32[]{:S(2)}) %collective-permute-start.25) | collective-permute-done | bytes 262176 | tf_op jit(solution)/shard_map/ppermute | solution.py:30
  177.2 3.5 %collective-permute-start.32 = (bf16[256,512]{1,0:T(8,128)(2,1)S(1)}, bf16[256,512]{1,0:T(8,128)(2,1)S(1)}, u32[]{:S(2)}, u32[]{:S(2)}) collective-permute-start(bf16[256,512]{1,0:T(8,128)(2,1)S(1)} %get-tuple-element.458), channel_id=1, source_target_pairs={{0,6},{1,7},{2,4},{3,5},{4,2},{5,3},{6,0},{7,1},{8,22},{9,23},{10,... | collective-permute-start | bytes 786440 | tf_op jit(solution)/shard_map/ppermute | solution.py:30
  180.7 4.3 %collective-permute-start.28 = (bf16[256,512]{1,0:T(8,128)(2,1)S(1)}, bf16[256,512]{1,0:T(8,128)(2,1)S(1)}, u32[]{:S(2)}, u32[]{:S(2)}) collective-permute-start(bf16[256,512]{1,0:T(8,128)(2,1)S(1)} %get-tuple-element.431), channel_id=1, source_target_pairs={{0,4},{1,5},{2,6},{3,7},{4,0},{5,1},{6,2},{7,3},{8,20},{9,21},{10,... | collective-permute-start | bytes 786440 | tf_op jit(solution)/shard_map/ppermute | solution.py:30
  185.0 3.3 %collective-permute-start.27 = (bf16[256,512]{1,0:T(8,128)(2,1)S(1)}, bf16[256,512]{1,0:T(8,128)(2,1)S(1)}, u32[]{:S(2)}, u32[]{:S(2)}) collective-permute-start(bf16[256,512]{1,0:T(8,128)(2,1)S(1)} %get-tuple-element.429), channel_id=1, source_target_pairs={{0,0},{1,1},{2,2},{3,3},{4,4},{5,5},{6,6},{7,7},{8,16},{9,17},{10,... | collective-permute-start | bytes 786440 | tf_op jit(solution)/shard_map/ppermute | solution.py:30
  188.4 2.4 shard_map.43
  190.7 2.8 %collective-permute-start.37 = (bf16[256,512]{1,0:T(8,128)(2,1)S(1)}, bf16[256,512]{1,0:T(8,128)(2,1)S(1)}, u32[]{:S(2)}, u32[]{:S(2)}) collective-permute-start(bf16[256,512]{1,0:T(8,128)(2,1)S(1)} %get-tuple-element.473), channel_id=1, source_target_pairs={{0,4},{1,5},{2,6},{3,7},{4,0},{5,1},{6,2},{7,3},{8,20},{9,21},{10,... | collective-permute-start | bytes 786440 | tf_op jit(solution)/shard_map/ppermute | solution.py:30
  193.6 3.4 %collective-permute-start.36 = (bf16[256,512]{1,0:T(8,128)(2,1)S(1)}, bf16[256,512]{1,0:T(8,128)(2,1)S(1)}, u32[]{:S(2)}, u32[]{:S(2)}) collective-permute-start(bf16[256,512]{1,0:T(8,128)(2,1)S(1)} %get-tuple-element.472), channel_id=1, source_target_pairs={{0,0},{1,1},{2,2},{3,3},{4,4},{5,5},{6,6},{7,7},{8,16},{9,17},{10,... | collective-permute-start | bytes 786440 | tf_op jit(solution)/shard_map/ppermute | solution.py:30
  197.8 2.1 collective-permute-start.34
  199.9 3.6 %collective-permute-done.28 = bf16[256,512]{1,0:T(8,128)(2,1)S(1)} collective-permute-done((bf16[256,512]{1,0:T(8,128)(2,1)S(1)}, bf16[256,512]{1,0:T(8,128)(2,1)S(1)}, u32[]{:S(2)}, u32[]{:S(2)}) %collective-permute-start.28) | collective-permute-done | bytes 262176 | tf_op jit(solution)/shard_map/ppermute | solution.py:30
  203.6 8.5 %collective-permute-start.33 = (bf16[256,512]{1,0:T(8,128)(2,1)S(1)}, bf16[256,512]{1,0:T(8,128)(2,1)S(1)}, u32[]{:S(2)}, u32[]{:S(2)}) collective-permute-start(bf16[256,512]{1,0:T(8,128)(2,1)S(1)} %get-tuple-element.468), channel_id=1, source_target_pairs={{0,2},{1,3},{2,0},{3,1},{4,6},{5,7},{6,4},{7,5},{8,18},{9,19},{10,... | collective-permute-start | bytes 786440 | tf_op jit(solution)/shard_map/ppermute | solution.py:30
  212.1 1.5 collective-permute-start.30
  213.9 1.9 collective-permute-start.39
  216.0 13.2 %collective-permute-done.33 = bf16[256,512]{1,0:T(8,128)(2,1)S(1)} collective-permute-done((bf16[256,512]{1,0:T(8,128)(2,1)S(1)}, bf16[256,512]{1,0:T(8,128)(2,1)S(1)}, u32[]{:S(2)}, u32[]{:S(2)}) %collective-permute-start.33) | collective-permute-done | bytes 262176 | tf_op jit(solution)/shard_map/ppermute | solution.py:30
  229.3 1.6 collective-permute-start.35
  230.8 1.9 shard_map.44.outs_0_
  232.7 4.9 %collective-permute-done.39.partner = bf16[2,256,512]{2,1,0:T(8,128)(2,1)S(1)} collective-permute-done((bf16[2,256,512]{2,1,0:T(8,128)(2,1)S(1)}, bf16[2,256,512]{2,1,0:T(8,128)(2,1)S(1)}, u32[]{:S(2)}, u32[]{:S(2)}) %collective-permute-start.39) | collective-permute-done | bytes 524320 | tf_op jit(solution)/shard_map/ppermute | solution.py:34
  237.6 1.9 shard_map.45.outs_0_
  239.5 9.3 %collective-permute-done.38.partner = bf16[2,256,512]{2,1,0:T(8,128)(2,1)S(1)} collective-permute-done((bf16[2,256,512]{2,1,0:T(8,128)(2,1)S(1)}, bf16[2,256,512]{2,1,0:T(8,128)(2,1)S(1)}, u32[]{:S(2)}, u32[]{:S(2)}) %collective-permute-start.38) | collective-permute-done | bytes 524320 | tf_op jit(solution)/shard_map/ppermute | solution.py:34
  248.9 1.9 shard_map.46.outs_0_
  250.7 8.8 %collective-permute-done.35.partner = bf16[2,256,512]{2,1,0:T(8,128)(2,1)S(1)} collective-permute-done((bf16[2,256,512]{2,1,0:T(8,128)(2,1)S(1)}, bf16[2,256,512]{2,1,0:T(8,128)(2,1)S(1)}, u32[]{:S(2)}, u32[]{:S(2)}) %collective-permute-start.35) | collective-permute-done | bytes 524320 | tf_op jit(solution)/shard_map/ppermute | solution.py:34
  259.6 1.9 shard_map.47
  (80 shorter events, 22.3 us)
Async XLA Ops:
  1.4 7.9 %copy-start.5 = (bf16[4,256,512]{2,1,0:T(8,128)(2,1)}, bf16[4,256,512]{2,1,0:T(8,128)(2,1)S(1)}, u32[]{:S(2)}) copy-start(bf16[4,256,512]{2,1,0:T(8,128)(2,1)S(1)} %slice.6) | copy-start | bytes 3145732
  1.4 8.4 %collective-permute-start.9 = (bf16[4,256,512]{2,1,0:T(8,128)(2,1)S(1)}, bf16[4,256,512]{2,1,0:T(8,128)(2,1)S(1)}, u32[]{:S(2)}, u32[]{:S(2)}) collective-permute-start(bf16[4,256,512]{2,1,0:T(8,128)(2,1)S(1)} %slice.6), channel_id=1, source_target_pairs={{0,16},{16,0},{32,48},{48,32},{64,80},{80,64},{96,112},{112,96},{1... | collective-permute-start | bytes 3145736 | tf_op jit(solution)/shard_map/ppermute | solution.py:34
  4.7 2.2 copy-start
  6.9 2.3 copy-start.13
  9.2 11.2 %copy-start.2 = (bf16[3,256,512]{2,1,0:T(8,128)(2,1)}, bf16[3,256,512]{2,1,0:T(8,128)(2,1)S(1)}, u32[]{:S(2)}) copy-start(bf16[3,256,512]{2,1,0:T(8,128)(2,1)S(1)} %get-tuple-element.327) | copy-start | bytes 2359300
  9.4 2.8 %copy-start.7 = (bf16[4,256,512]{2,1,0:T(8,128)(2,1)}, bf16[4,256,512]{2,1,0:T(8,128)(2,1)S(1)}, u32[]{:S(2)}) copy-start(bf16[4,256,512]{2,1,0:T(8,128)(2,1)S(1)} %slice.7) | copy-start | bytes 3145732
  9.4 2.7 %collective-permute-start.8 = (bf16[4,256,512]{2,1,0:T(8,128)(2,1)S(1)}, bf16[4,256,512]{2,1,0:T(8,128)(2,1)S(1)}, u32[]{:S(2)}, u32[]{:S(2)}) collective-permute-start(bf16[4,256,512]{2,1,0:T(8,128)(2,1)S(1)} %slice.7), channel_id=1, source_target_pairs={{0,16},{16,0},{32,48},{48,32},{64,80},{80,64},{96,112},{112,96},{1... | collective-permute-start | bytes 3145736 | tf_op jit(solution)/shard_map/ppermute | solution.py:34
  9.8 7.3 %copy-start.9 = (bf16[4,256,512]{2,1,0:T(8,128)(2,1)}, bf16[4,256,512]{2,1,0:T(8,128)(2,1)S(1)}, u32[]{:S(2)}) copy-start(bf16[4,256,512]{2,1,0:T(8,128)(2,1)S(1)} %collective-permute-done.9) | copy-start | bytes 3145732
  12.1 4.9 %copy-start.11 = (bf16[4,256,512]{2,1,0:T(8,128)(2,1)}, bf16[4,256,512]{2,1,0:T(8,128)(2,1)S(1)}, u32[]{:S(2)}) copy-start(bf16[4,256,512]{2,1,0:T(8,128)(2,1)S(1)} %collective-permute-done.8) | copy-start | bytes 3145732
  12.1 85.7 %collective-permute-start.12 = (bf16[3,256,512]{2,1,0:T(8,128)(2,1)}, bf16[3,256,512]{2,1,0:T(8,128)(2,1)S(1)}, u32[]{:S(2)}, u32[]{:S(2)}) collective-permute-start(bf16[3,256,512]{2,1,0:T(8,128)(2,1)} %get-tuple-element.328), channel_id=1, source_target_pairs={{0,2},{1,3},{2,0},{3,1},{4,6},{5,7},{6,4},{7,5},{8,18},{9,19},{10,... | collective-permute-start | bytes 2359304 | tf_op jit(solution)/shard_map/ppermute | solution.py:30
  17.0 81.7 %collective-permute-start.13 = (bf16[3,256,512]{2,1,0:T(8,128)(2,1)}, bf16[3,256,512]{2,1,0:T(8,128)(2,1)S(1)}, u32[]{:S(2)}, u32[]{:S(2)}) collective-permute-start(bf16[3,256,512]{2,1,0:T(8,128)(2,1)} %get-tuple-element.329), channel_id=1, source_target_pairs={{0,0},{1,1},{2,2},{3,3},{4,4},{5,5},{6,6},{7,7},{8,16},{9,17},{10,... | collective-permute-start | bytes 2359304 | tf_op jit(solution)/shard_map/ppermute | solution.py:30
  20.5 79.3 %collective-permute-start.11 = (bf16[3,256,512]{2,1,0:T(8,128)(2,1)}, bf16[3,256,512]{2,1,0:T(8,128)(2,1)S(1)}, u32[]{:S(2)}, u32[]{:S(2)}) collective-permute-start(bf16[3,256,512]{2,1,0:T(8,128)(2,1)} %copy-done.2), channel_id=1, source_target_pairs={{0,4},{1,5},{2,6},{3,7},{4,0},{5,1},{6,2},{7,3},{8,20},{9,21},{10,... | collective-permute-start | bytes 2359304 | tf_op jit(solution)/shard_map/ppermute | solution.py:30
  23.9 5.6 %copy-start.4 = (bf16[4,4,256,512]{3,2,1,0:T(8,128)(2,1)S(1)}, bf16[4,4,256,512]{3,2,1,0:T(8,128)(2,1)}, u32[]{:S(2)}) copy-start(bf16[4,4,256,512]{3,2,1,0:T(8,128)(2,1)} %get-tuple-element.26.factor) | copy-start | bytes 12582916 | tf_op jit(solution)/shard_map/cond
  23.9 5.6 %copy-start.6 = (bf16[4,256,512]{2,1,0:T(8,128)(2,1)S(1)}, bf16[4,256,512]{2,1,0:T(8,128)(2,1)}, u32[]{:S(2)}) copy-start(bf16[4,256,512]{2,1,0:T(8,128)(2,1)} %get-tuple-element.39.own) | copy-start | bytes 3145732 | tf_op jit(solution)/shard_map/cond
  23.9 5.6 %copy-start.10 = (bf16[4,256,512]{2,1,0:T(8,128)(2,1)S(1)}, bf16[4,256,512]{2,1,0:T(8,128)(2,1)}, u32[]{:S(2)}) copy-start(bf16[4,256,512]{2,1,0:T(8,128)(2,1)} %get-tuple-element.33.partner) | copy-start | bytes 3145732 | tf_op jit(solution)/shard_map/cond
  26.5 4.9 %copy-start.8 = (bf16[4,256,512]{2,1,0:T(8,128)(2,1)S(1)}, bf16[4,256,512]{2,1,0:T(8,128)(2,1)}, u32[]{:S(2)}) copy-start(bf16[4,256,512]{2,1,0:T(8,128)(2,1)} %get-tuple-element.46.own) | copy-start | bytes 3145732 | tf_op jit(solution)/shard_map/cond
  26.5 4.9 %copy-start.12 = (bf16[4,256,512]{2,1,0:T(8,128)(2,1)S(1)}, bf16[4,256,512]{2,1,0:T(8,128)(2,1)}, u32[]{:S(2)}) copy-start(bf16[4,256,512]{2,1,0:T(8,128)(2,1)} %get-tuple-element.43.partner) | copy-start | bytes 3145732 | tf_op jit(solution)/shard_map/cond
  26.5 15.5 %collective-permute-start = (bf16[2,256,512]{2,1,0:T(8,128)(2,1)S(1)}, bf16[2,256,512]{2,1,0:T(8,128)(2,1)S(1)}, u32[]{:S(2)}, u32[]{:S(2)}) collective-permute-start(bf16[2,256,512]{2,1,0:T(8,128)(2,1)S(1)} %branch_1_fun.12.own), channel_id=1, source_target_pairs={{0,32},{16,48},{32,0},{48,16},{64,96},{80,112},{96,64},{112,80},{1... | collective-permute-start | bytes 1572872 | tf_op jit(solution)/shard_map/cond/branch_1_fun/ppermute | solution.py:34
  30.7 16.7 %collective-permute-start.2 = (bf16[2,256,512]{2,1,0:T(8,128)(2,1)S(1)}, bf16[2,256,512]{2,1,0:T(8,128)(2,1)S(1)}, u32[]{:S(2)}, u32[]{:S(2)}) collective-permute-start(bf16[2,256,512]{2,1,0:T(8,128)(2,1)S(1)} %branch_1_fun.13.own), channel_id=1, source_target_pairs={{0,32},{16,48},{32,0},{48,16},{64,96},{80,112},{96,64},{112,80},{1... | collective-permute-start | bytes 1572872 | tf_op jit(solution)/shard_map/cond/branch_1_fun/ppermute | solution.py:34
  43.2 13.2 %collective-permute-start.1 = (bf16[2,256,512]{2,1,0:T(8,128)(2,1)S(1)}, bf16[2,256,512]{2,1,0:T(8,128)(2,1)S(1)}, u32[]{:S(2)}, u32[]{:S(2)}) collective-permute-start(bf16[2,256,512]{2,1,0:T(8,128)(2,1)S(1)} %branch_1_fun.16.own), channel_id=1, source_target_pairs={{0,64},{16,80},{32,96},{48,112},{64,0},{80,16},{96,32},{112,48},{1... | collective-permute-start | bytes 1572872 | tf_op jit(solution)/shard_map/cond/branch_1_fun/ppermute | solution.py:34
  48.6 19.1 %collective-permute-start.3 = (bf16[2,256,512]{2,1,0:T(8,128)(2,1)S(1)}, bf16[2,256,512]{2,1,0:T(8,128)(2,1)S(1)}, u32[]{:S(2)}, u32[]{:S(2)}) collective-permute-start(bf16[2,256,512]{2,1,0:T(8,128)(2,1)S(1)} %branch_1_fun.17.own), channel_id=1, source_target_pairs={{0,64},{16,80},{32,96},{48,112},{64,0},{80,16},{96,32},{112,48},{1... | collective-permute-start | bytes 1572872 | tf_op jit(solution)/shard_map/cond/branch_1_fun/ppermute | solution.py:34
  57.6 18.4 %collective-permute-start.4 = (bf16[2,256,512]{2,1,0:T(8,128)(2,1)S(1)}, bf16[2,256,512]{2,1,0:T(8,128)(2,1)S(1)}, u32[]{:S(2)}, u32[]{:S(2)}) collective-permute-start(bf16[2,256,512]{2,1,0:T(8,128)(2,1)S(1)} %branch_1_fun.18.own), channel_id=1, source_target_pairs={{0,128},{16,144},{32,160},{48,176},{64,192},{80,208},{96,224},{112... | collective-permute-start | bytes 1572872 | tf_op jit(solution)/shard_map/cond/branch_1_fun/ppermute | solution.py:34
  68.8 10.0 %collective-permute-start.6 = (bf16[2,256,512]{2,1,0:T(8,128)(2,1)S(1)}, bf16[2,256,512]{2,1,0:T(8,128)(2,1)S(1)}, u32[]{:S(2)}, u32[]{:S(2)}) collective-permute-start(bf16[2,256,512]{2,1,0:T(8,128)(2,1)S(1)} %branch_1_fun.14.own), channel_id=1, source_target_pairs={{0,32},{16,48},{32,0},{48,16},{64,96},{80,112},{96,64},{112,80},{1... | collective-permute-start | bytes 1572872 | tf_op jit(solution)/shard_map/cond/branch_1_fun/ppermute | solution.py:34
  78.8 10.0 %collective-permute-start.5 = (bf16[2,256,512]{2,1,0:T(8,128)(2,1)S(1)}, bf16[2,256,512]{2,1,0:T(8,128)(2,1)S(1)}, u32[]{:S(2)}, u32[]{:S(2)}) collective-permute-start(bf16[2,256,512]{2,1,0:T(8,128)(2,1)S(1)} %branch_1_fun.19.own), channel_id=1, source_target_pairs={{0,128},{16,144},{32,160},{48,176},{64,192},{80,208},{96,224},{112... | collective-permute-start | bytes 1572872 | tf_op jit(solution)/shard_map/cond/branch_1_fun/ppermute | solution.py:34
  82.4 10.1 %collective-permute-start.7 = (bf16[2,256,512]{2,1,0:T(8,128)(2,1)S(1)}, bf16[2,256,512]{2,1,0:T(8,128)(2,1)S(1)}, u32[]{:S(2)}, u32[]{:S(2)}) collective-permute-start(bf16[2,256,512]{2,1,0:T(8,128)(2,1)S(1)} %branch_1_fun.15.own), channel_id=1, source_target_pairs={{0,32},{16,48},{32,0},{48,16},{64,96},{80,112},{96,64},{112,80},{1... | collective-permute-start | bytes 1572872 | tf_op jit(solution)/shard_map/cond/branch_1_fun/ppermute | solution.py:34
  93.7 24.4 %collective-permute-start.18 = (bf16[3,256,512]{2,1,0:T(8,128)(2,1)S(1)}, bf16[3,256,512]{2,1,0:T(8,128)(2,1)S(1)}, u32[]{:S(2)}, u32[]{:S(2)}) collective-permute-start(bf16[3,256,512]{2,1,0:T(8,128)(2,1)S(1)} %get-tuple-element.353), channel_id=1, source_target_pairs={{0,6},{1,7},{2,4},{3,5},{4,2},{5,3},{6,0},{7,1},{8,22},{9,23},{10,... | collective-permute-start | bytes 2359304 | tf_op jit(solution)/shard_map/ppermute | solution.py:30
  97.2 12.3 %collective-permute-start.10 = (bf16[2,256,512]{2,1,0:T(8,128)(2,1)S(1)}, bf16[2,256,512]{2,1,0:T(8,128)(2,1)S(1)}, u32[]{:S(2)}, u32[]{:S(2)}) collective-permute-start(bf16[2,256,512]{2,1,0:T(8,128)(2,1)S(1)} %get-tuple-element.343.own), channel_id=1, source_target_pairs={{0,64},{16,80},{32,96},{48,112},{64,0},{80,16},{96,32},{112,48},{1... | collective-permute-start | bytes 1572872 | tf_op jit(solution)/shard_map/ppermute | solution.py:34
  97.8 22.4 %collective-permute-start.16 = (bf16[2,256,512]{2,1,0:T(8,128)(2,1)S(1)}, bf16[2,256,512]{2,1,0:T(8,128)(2,1)S(1)}, u32[]{:S(2)}, u32[]{:S(2)}) collective-permute-start(bf16[2,256,512]{2,1,0:T(8,128)(2,1)S(1)} %get-tuple-element.360.own), channel_id=1, source_target_pairs={{0,64},{16,80},{32,96},{48,112},{64,0},{80,16},{96,32},{112,48},{1... | collective-permute-start | bytes 1572872 | tf_op jit(solution)/shard_map/ppermute | solution.py:34
  98.7 21.6 %copy-start.3 = (bf16[4,4,1,1,256,512]{5,4,3,2,1,0:T(8,128)(2,1)S(1)}, bf16[4,4,1,1,256,512]{5,4,3,2,1,0:T(8,128)(2,1)}, u32[]{:S(2)}) copy-start(bf16[4,4,1,1,256,512]{5,4,3,2,1,0:T(8,128)(2,1)} %param.6) | copy-start | bytes 12582916
  98.7 21.5 %collective-permute-start.17 = (bf16[256,512]{1,0:T(8,128)(2,1)S(1)}, bf16[256,512]{1,0:T(8,128)(2,1)S(1)}, u32[]{:S(2)}, u32[]{:S(2)}) collective-permute-start(bf16[256,512]{1,0:T(8,128)(2,1)S(1)} %get-tuple-element.351), channel_id=1, source_target_pairs={{0,4},{1,5},{2,6},{3,7},{4,0},{5,1},{6,2},{7,3},{8,20},{9,21},{10,... | collective-permute-start | bytes 786440 | tf_op jit(solution)/shard_map/ppermute | solution.py:30
  118.1 20.6 %collective-permute-start.14 = (bf16[2,256,512]{2,1,0:T(8,128)(2,1)S(1)}, bf16[2,256,512]{2,1,0:T(8,128)(2,1)S(1)}, u32[]{:S(2)}, u32[]{:S(2)}) collective-permute-start(bf16[2,256,512]{2,1,0:T(8,128)(2,1)S(1)} %shard_map.38.own), channel_id=1, source_target_pairs={{0,128},{16,144},{32,160},{48,176},{64,192},{80,208},{96,224},{112... | collective-permute-start | bytes 1572872 | tf_op jit(solution)/shard_map/ppermute | solution.py:34
  121.4 23.0 %collective-permute-start.22 = (bf16[2,256,512]{2,1,0:T(8,128)(2,1)S(1)}, bf16[2,256,512]{2,1,0:T(8,128)(2,1)S(1)}, u32[]{:S(2)}, u32[]{:S(2)}) collective-permute-start(bf16[2,256,512]{2,1,0:T(8,128)(2,1)S(1)} %shard_map.39.own), channel_id=1, source_target_pairs={{0,128},{16,144},{32,160},{48,176},{64,192},{80,208},{96,224},{112... | collective-permute-start | bytes 1572872 | tf_op jit(solution)/shard_map/ppermute | solution.py:34
  124.2 14.5 %collective-permute-start.15 = (bf16[256,512]{1,0:T(8,128)(2,1)S(1)}, bf16[256,512]{1,0:T(8,128)(2,1)S(1)}, u32[]{:S(2)}, u32[]{:S(2)}) collective-permute-start(bf16[256,512]{1,0:T(8,128)(2,1)S(1)} %get-tuple-element.348), channel_id=1, source_target_pairs={{0,0},{1,1},{2,2},{3,3},{4,4},{5,5},{6,6},{7,7},{8,16},{9,17},{10,... | collective-permute-start | bytes 786440 | tf_op jit(solution)/shard_map/ppermute | solution.py:30
  129.2 15.3 %collective-permute-start.20 = (bf16[256,512]{1,0:T(8,128)(2,1)S(1)}, bf16[256,512]{1,0:T(8,128)(2,1)S(1)}, u32[]{:S(2)}, u32[]{:S(2)}) collective-permute-start(bf16[256,512]{1,0:T(8,128)(2,1)S(1)} %get-tuple-element.375), channel_id=1, source_target_pairs={{0,2},{1,3},{2,0},{3,1},{4,6},{5,7},{6,4},{7,5},{8,18},{9,19},{10,... | collective-permute-start | bytes 786440 | tf_op jit(solution)/shard_map/ppermute | solution.py:30
  130.3 17.5 %collective-permute-start.21 = (bf16[256,512]{1,0:T(8,128)(2,1)S(1)}, bf16[256,512]{1,0:T(8,128)(2,1)S(1)}, u32[]{:S(2)}, u32[]{:S(2)}) collective-permute-start(bf16[256,512]{1,0:T(8,128)(2,1)S(1)} %get-tuple-element.379), channel_id=1, source_target_pairs={{0,6},{1,7},{2,4},{3,5},{4,2},{5,3},{6,0},{7,1},{8,22},{9,23},{10,... | collective-permute-start | bytes 786440 | tf_op jit(solution)/shard_map/ppermute | solution.py:30
  148.0 10.9 %collective-permute-start.23 = (bf16[4,256,512]{2,1,0:T(8,128)(2,1)S(1)}, bf16[4,256,512]{2,1,0:T(8,128)(2,1)S(1)}, u32[]{:S(2)}, u32[]{:S(2)}) collective-permute-start(bf16[4,256,512]{2,1,0:T(8,128)(2,1)S(1)} %pad_maximum_fusion.own), channel_id=1, source_target_pairs={{0,16},{16,0},{32,48},{48,32},{64,80},{80,64},{96,112},{112,96},{1... | collective-permute-start | bytes 3145736 | tf_op jit(solution)/shard_map/ppermute | solution.py:34
  148.1 13.2 %collective-permute-start.24 = (bf16[256,512]{1,0:T(8,128)(2,1)S(1)}, bf16[256,512]{1,0:T(8,128)(2,1)S(1)}, u32[]{:S(2)}, u32[]{:S(2)}) collective-permute-start(bf16[256,512]{1,0:T(8,128)(2,1)S(1)} %get-tuple-element.413), channel_id=1, source_target_pairs={{0,4},{1,5},{2,6},{3,7},{4,0},{5,1},{6,2},{7,3},{8,20},{9,21},{10,... | collective-permute-start | bytes 786440 | tf_op jit(solution)/shard_map/ppermute | solution.py:30
  151.1 14.9 %collective-permute-start.19 = (bf16[256,512]{1,0:T(8,128)(2,1)S(1)}, bf16[256,512]{1,0:T(8,128)(2,1)S(1)}, u32[]{:S(2)}, u32[]{:S(2)}) collective-permute-start(bf16[256,512]{1,0:T(8,128)(2,1)S(1)} %get-tuple-element.373), channel_id=1, source_target_pairs={{0,0},{1,1},{2,2},{3,3},{4,4},{5,5},{6,6},{7,7},{8,16},{9,17},{10,... | collective-permute-start | bytes 786440 | tf_op jit(solution)/shard_map/ppermute | solution.py:30
  154.6 22.1 %collective-permute-start.25 = (bf16[256,512]{1,0:T(8,128)(2,1)S(1)}, bf16[256,512]{1,0:T(8,128)(2,1)S(1)}, u32[]{:S(2)}, u32[]{:S(2)}) collective-permute-start(bf16[256,512]{1,0:T(8,128)(2,1)S(1)} %get-tuple-element.420), channel_id=1, source_target_pairs={{0,2},{1,3},{2,0},{3,1},{4,6},{5,7},{6,4},{7,5},{8,18},{9,19},{10,... | collective-permute-start | bytes 786440 | tf_op jit(solution)/shard_map/ppermute | solution.py:30
  158.9 18.1 %collective-permute-start.26 = (bf16[256,512]{1,0:T(8,128)(2,1)S(1)}, bf16[256,512]{1,0:T(8,128)(2,1)S(1)}, u32[]{:S(2)}, u32[]{:S(2)}) collective-permute-start(bf16[256,512]{1,0:T(8,128)(2,1)S(1)} %get-tuple-element.424), channel_id=1, source_target_pairs={{0,6},{1,7},{2,4},{3,5},{4,2},{5,3},{6,0},{7,1},{8,22},{9,23},{10,... | collective-permute-start | bytes 786440 | tf_op jit(solution)/shard_map/ppermute | solution.py:30
  177.1 11.2 %collective-permute-start.29 = (bf16[4,256,512]{2,1,0:T(8,128)(2,1)S(1)}, bf16[4,256,512]{2,1,0:T(8,128)(2,1)S(1)}, u32[]{:S(2)}, u32[]{:S(2)}) collective-permute-start(bf16[4,256,512]{2,1,0:T(8,128)(2,1)S(1)} %pad_maximum_fusion.1.own), channel_id=1, source_target_pairs={{0,16},{16,0},{32,48},{48,32},{64,80},{80,64},{96,112},{112,96},{1... | collective-permute-start | bytes 3145736 | tf_op jit(solution)/shard_map/ppermute | solution.py:34
  177.2 16.3 %collective-permute-start.32 = (bf16[256,512]{1,0:T(8,128)(2,1)S(1)}, bf16[256,512]{1,0:T(8,128)(2,1)S(1)}, u32[]{:S(2)}, u32[]{:S(2)}) collective-permute-start(bf16[256,512]{1,0:T(8,128)(2,1)S(1)} %get-tuple-element.458), channel_id=1, source_target_pairs={{0,6},{1,7},{2,4},{3,5},{4,2},{5,3},{6,0},{7,1},{8,22},{9,23},{10,... | collective-permute-start | bytes 786440 | tf_op jit(solution)/shard_map/ppermute | solution.py:30
  180.7 17.2 %collective-permute-start.31 = (bf16[256,512]{1,0:T(8,128)(2,1)S(1)}, bf16[256,512]{1,0:T(8,128)(2,1)S(1)}, u32[]{:S(2)}, u32[]{:S(2)}) collective-permute-start(bf16[256,512]{1,0:T(8,128)(2,1)S(1)} %get-tuple-element.451), channel_id=1, source_target_pairs={{0,2},{1,3},{2,0},{3,1},{4,6},{5,7},{6,4},{7,5},{8,18},{9,19},{10,... | collective-permute-start | bytes 786440 | tf_op jit(solution)/shard_map/ppermute | solution.py:30
  180.7 22.9 %collective-permute-start.28 = (bf16[256,512]{1,0:T(8,128)(2,1)S(1)}, bf16[256,512]{1,0:T(8,128)(2,1)S(1)}, u32[]{:S(2)}, u32[]{:S(2)}) collective-permute-start(bf16[256,512]{1,0:T(8,128)(2,1)S(1)} %get-tuple-element.431), channel_id=1, source_target_pairs={{0,4},{1,5},{2,6},{3,7},{4,0},{5,1},{6,2},{7,3},{8,20},{9,21},{10,... | collective-permute-start | bytes 786440 | tf_op jit(solution)/shard_map/ppermute | solution.py:30
  185.0 27.0 %collective-permute-start.27 = (bf16[256,512]{1,0:T(8,128)(2,1)S(1)}, bf16[256,512]{1,0:T(8,128)(2,1)S(1)}, u32[]{:S(2)}, u32[]{:S(2)}) collective-permute-start(bf16[256,512]{1,0:T(8,128)(2,1)S(1)} %get-tuple-element.429), channel_id=1, source_target_pairs={{0,0},{1,1},{2,2},{3,3},{4,4},{5,5},{6,6},{7,7},{8,16},{9,17},{10,... | collective-permute-start | bytes 786440 | tf_op jit(solution)/shard_map/ppermute | solution.py:30
  190.7 23.2 %collective-permute-start.37 = (bf16[256,512]{1,0:T(8,128)(2,1)S(1)}, bf16[256,512]{1,0:T(8,128)(2,1)S(1)}, u32[]{:S(2)}, u32[]{:S(2)}) collective-permute-start(bf16[256,512]{1,0:T(8,128)(2,1)S(1)} %get-tuple-element.473), channel_id=1, source_target_pairs={{0,4},{1,5},{2,6},{3,7},{4,0},{5,1},{6,2},{7,3},{8,20},{9,21},{10,... | collective-permute-start | bytes 786440 | tf_op jit(solution)/shard_map/ppermute | solution.py:30
  193.6 22.3 %collective-permute-start.36 = (bf16[256,512]{1,0:T(8,128)(2,1)S(1)}, bf16[256,512]{1,0:T(8,128)(2,1)S(1)}, u32[]{:S(2)}, u32[]{:S(2)}) collective-permute-start(bf16[256,512]{1,0:T(8,128)(2,1)S(1)} %get-tuple-element.472), channel_id=1, source_target_pairs={{0,0},{1,1},{2,2},{3,3},{4,4},{5,5},{6,6},{7,7},{8,16},{9,17},{10,... | collective-permute-start | bytes 786440 | tf_op jit(solution)/shard_map/ppermute | solution.py:30
  197.8 18.2 %collective-permute-start.34 = (bf16[256,512]{1,0:T(8,128)(2,1)S(1)}, bf16[256,512]{1,0:T(8,128)(2,1)S(1)}, u32[]{:S(2)}, u32[]{:S(2)}) collective-permute-start(bf16[256,512]{1,0:T(8,128)(2,1)S(1)} %get-tuple-element.471), channel_id=1, source_target_pairs={{0,6},{1,7},{2,4},{3,5},{4,2},{5,3},{6,0},{7,1},{8,22},{9,23},{10,... | collective-permute-start | bytes 786440 | tf_op jit(solution)/shard_map/ppermute | solution.py:30
  203.6 25.7 %collective-permute-start.33 = (bf16[256,512]{1,0:T(8,128)(2,1)S(1)}, bf16[256,512]{1,0:T(8,128)(2,1)S(1)}, u32[]{:S(2)}, u32[]{:S(2)}) collective-permute-start(bf16[256,512]{1,0:T(8,128)(2,1)S(1)} %get-tuple-element.468), channel_id=1, source_target_pairs={{0,2},{1,3},{2,0},{3,1},{4,6},{5,7},{6,4},{7,5},{8,18},{9,19},{10,... | collective-permute-start | bytes 786440 | tf_op jit(solution)/shard_map/ppermute | solution.py:30
  212.0 18.8 %copy-start.1 = (bf16[4,4,1,1,256,512]{5,4,3,2,1,0:T(8,128)(2,1)S(1)}, bf16[4,4,1,1,256,512]{5,4,3,2,1,0:T(8,128)(2,1)}, u32[]{:S(2)}) copy-start(bf16[4,4,1,1,256,512]{5,4,3,2,1,0:T(8,128)(2,1)} %param.7) | copy-start | bytes 12582916
  212.1 18.7 %collective-permute-start.30 = (bf16[2,256,512]{2,1,0:T(8,128)(2,1)S(1)}, bf16[2,256,512]{2,1,0:T(8,128)(2,1)S(1)}, u32[]{:S(2)}, u32[]{:S(2)}) collective-permute-start(bf16[2,256,512]{2,1,0:T(8,128)(2,1)S(1)} %pad_maximum_fusion.5.own), channel_id=1, source_target_pairs={{0,1},{1,0},{2,3},{3,2},{4,5},{5,4},{6,7},{7,6},{8,9},{9,8},{10,11... | collective-permute-start | bytes 1572872 | tf_op jit(solution)/shard_map/ppermute | solution.py:34
  213.9 23.7 %collective-permute-start.39 = (bf16[2,256,512]{2,1,0:T(8,128)(2,1)S(1)}, bf16[2,256,512]{2,1,0:T(8,128)(2,1)S(1)}, u32[]{:S(2)}, u32[]{:S(2)}) collective-permute-start(bf16[2,256,512]{2,1,0:T(8,128)(2,1)S(1)} %pad_maximum_fusion.4.own), channel_id=1, source_target_pairs={{0,1},{1,0},{2,3},{3,2},{4,5},{5,4},{6,7},{7,6},{8,9},{9,8},{10,11... | collective-permute-start | bytes 1572872 | tf_op jit(solution)/shard_map/ppermute | solution.py:34
  215.9 32.9 %collective-permute-start.38 = (bf16[2,256,512]{2,1,0:T(8,128)(2,1)S(1)}, bf16[2,256,512]{2,1,0:T(8,128)(2,1)S(1)}, u32[]{:S(2)}, u32[]{:S(2)}) collective-permute-start(bf16[2,256,512]{2,1,0:T(8,128)(2,1)S(1)} %pad_maximum_fusion.3.own), channel_id=1, source_target_pairs={{0,1},{1,0},{2,3},{3,2},{4,5},{5,4},{6,7},{7,6},{8,9},{9,8},{10,11... | collective-permute-start | bytes 1572872 | tf_op jit(solution)/shard_map/ppermute | solution.py:34
  229.3 30.3 %collective-permute-start.35 = (bf16[2,256,512]{2,1,0:T(8,128)(2,1)S(1)}, bf16[2,256,512]{2,1,0:T(8,128)(2,1)S(1)}, u32[]{:S(2)}, u32[]{:S(2)}) collective-permute-start(bf16[2,256,512]{2,1,0:T(8,128)(2,1)S(1)} %pad_maximum_fusion.2.own), channel_id=1, source_target_pairs={{0,1},{1,0},{2,3},{3,2},{4,5},{5,4},{6,7},{7,6},{8,9},{9,8},{10,11... | collective-permute-start | bytes 1572872 | tf_op jit(solution)/shard_map/ppermute | solution.py:34
